TPU v7x, 32 devices: a whole 2x2x4 slice. The times are simulated.
32 devices in a mesh: hop: 2 (over x), batch: 16 (over z, y, core).
Axes of the slice: x: 2, y: 2, z: 4, core: 2. Of those that a mesh axis runs over, the one named last changes fastest.
Arguments:
- section_rows: bfloat16 [2, 2048, 2048], P('hop', 'batch'), may hold values from -6 to 6
- weights: bfloat16 [2, 2048, 2048], P('hop'), may hold values from -0.125 to 0.125
- relation_table: bfloat16 [256, 2048], replicated, may hold values from -4 to 4
- relation_ids: int32 [2048], P('batch'), may hold values from 0 to 255
Outputs:
- weight_grad: float32 [2, 2048, 2048], P('hop', 'batch')
- relation_grad: float32 [256, 2048], P(('hop', 'batch'))
- query_grad: bfloat16 [2048, 2048], P('batch')
Inputs may be any that keep to these rules, and one draw needn't show every extreme that they name: `relation_ids`: relation index of each query.
All inputs are finite; a program needn't handle non-finite values.
Results may differ from a plain program's by a relative error of at most 0.0064.
Values may be sent and summed in bfloat16 or wider, within the bound.
No kernel may reach another device: no remote copies, remote signals or barrier semaphores. Data moves between devices by JAX's collectives and lax.ppermute only.
A program may use at most 128 MiB of HBM per device.

v0:
```python
import jax
import jax.numpy as jnp
from jax import lax
from jax.experimental import pallas as pl
from jax.experimental.pallas import tpu as pltpu
from jax.sharding import Mesh
from jax.sharding import PartitionSpec as P

F32 = jnp.float32
BF16 = jnp.bfloat16
TILE = 256


def dot(a, b, ca, cb):
    return lax.dot_general(a, b, (((ca,), (cb,)), ((), ())), preferred_element_type=F32)


def swap_core(block):
    return lax.ppermute(block, "core", [(0, 1), (1, 0)])


def mix(q_re, q_im, r_re, r_im):
    return (q_re * r_re - q_im * r_im).astype(BF16), (q_re * r_im + q_im * r_re).astype(BF16)


def trail_body(first, q_re, q_im, rows, weight, rel, onehot, right, query_grad, give, keep, mixed, hidden):
    width = weight.shape[0]
    half = width // 2
    is_first = first[0] == 1
    owned = give.shape[0]

    def at(step, base=0):
        return pl.ds(pl.multiple_of(base + step * TILE, TILE), TILE)

    def make_mixed(step, carry):
        z_re, z_im = mix(
            q_re[:, at(step)].astype(F32), q_im[:, at(step)].astype(F32),
            rel[:, at(step)].astype(F32), rel[:, at(step, half)].astype(F32),
        )
        mixed[:, at(step)] = z_re
        mixed[:, at(step, half)] = z_im
        return carry

    lax.fori_loop(0, half // TILE, make_mixed, 0)

    def make_hidden(step, carry):
        pre = dot(mixed[...], weight[:, at(step)], 1, 0)
        sig = jax.nn.sigmoid(pre)
        cot = rows[:, at(step)]
        grad = (cot.astype(F32) * (sig * (1.0 + pre * (1.0 - sig)))).astype(BF16)
        hidden[:, at(step)] = grad
        right[:, at(step)] = jnp.where(is_first, cot, grad)
        return carry

    lax.fori_loop(0, weight.shape[1] // TILE, make_hidden, 0)

    def make_query(step, carry):
        gz_re = dot(hidden[...], weight[at(step), :], 1, 1)
        gz_im = dot(hidden[...], weight[at(step, half), :], 1, 1)
        r_re, r_im = rel[:, at(step)].astype(F32), rel[:, at(step, half)].astype(F32)
        query_grad[:, at(step)] = (gz_re * r_re + gz_im * r_im).astype(BF16)
        query_grad[:, at(step, half)] = (gz_im * r_re - gz_re * r_im).astype(BF16)
        a, b = q_re[:, at(step)].astype(F32), q_im[:, at(step)].astype(F32)
        for base, grad in ((0, gz_re * a + gz_im * b), (half, gz_im * a - gz_re * b)):
            head = grad.astype(BF16)
            rest = (grad - head.astype(F32)).astype(BF16)
            total = dot(onehot[...], head, 1, 0) + dot(onehot[...], rest, 1, 0)
            give[:, at(step, base)] = total[:owned]
            keep[:, at(step, base)] = total[owned:]
        return carry

    lax.fori_loop(0, half // TILE, make_query, 0)


def trail(first, q_re, q_im, rows, weight, rel, onehot):
    rows_dev, hidden = rows.shape
    width = weight.shape[0]
    count_rel = onehot.shape[0]
    vmem = pl.BlockSpec(memory_space=pltpu.VMEM)
    flops = 4 * rows_dev * width * hidden + 4 * rows_dev * count_rel * width
    return pl.pallas_call(
        trail_body,
        out_shape=(
            jax.ShapeDtypeStruct((rows_dev, hidden), BF16),
            jax.ShapeDtypeStruct((rows_dev, width), BF16),
            jax.ShapeDtypeStruct((count_rel // 2, width), F32),
            jax.ShapeDtypeStruct((count_rel // 2, width), F32),
        ),
        in_specs=[pl.BlockSpec(memory_space=pltpu.SMEM)] + [vmem] * 6,
        out_specs=(vmem,) * 4,
        scratch_shapes=[pltpu.VMEM((rows_dev, width), BF16), pltpu.VMEM((rows_dev, hidden), BF16)],
        compiler_params=pltpu.CompilerParams(vmem_limit_bytes=40 * 1024 * 1024),
        cost_estimate=pl.CostEstimate(
            flops=flops, bytes_accessed=2 * width * hidden, transcendentals=rows_dev * hidden
        ),
    )(first, q_re, q_im, rows, weight, rel, onehot)


def local(section_rows, weights, relation_table, relation_ids):
    rows = section_rows[0]
    weight = weights[0]
    rows_dev, width = rows.shape
    half = width // 2
    count_rel = relation_table.shape[0]
    chips = lax.axis_size("chip")
    first = lax.axis_index("hop") == 0
    core = lax.axis_index("core")
    chip = lax.axis_index("chip")
    total_rows = rows_dev * chips * 2
    cols = width // chips
    owned = count_rel // (4 * chips)

    def columns(left):
        return left.reshape(left.shape[0], chips, cols).transpose(1, 0, 2)

    own_re = dot(rows, weight[:half], 1, 1).astype(BF16)
    q_re = lax.ppermute(own_re, "hop", [(0, 1)])
    own_im = dot(rows, weight[half:], 1, 1).astype(BF16)
    q_im = lax.ppermute(own_im, "hop", [(0, 1)])

    onehot = (relation_ids[:, None] == lax.iota(jnp.int32, count_rel)[None, :]).astype(BF16)
    rel = dot(onehot, relation_table, 1, 0).astype(BF16)
    number = lax.iota(jnp.int32, count_rel)
    side = number // (count_rel // 2)
    dest = number % (count_rel // 2) // (2 * owned)
    hop = number % (2 * owned) // owned
    which_core = jnp.where(side == 1, core, 1 - core)
    relation = ((hop * chips + dest) * 2 + which_core) * owned + number % owned
    onehot_t = (relation[:, None] == relation_ids[None, :]).astype(BF16)

    relf = rel.astype(F32)
    own_z = jnp.concatenate(
        mix(own_re.astype(F32), own_im.astype(F32), relf[:, :half], relf[:, half:]), axis=1
    )
    z_cols = lax.all_to_all(columns(own_z), "chip", 0, 0, tiled=True)

    right, grad_query, rel_give, rel_keep = trail(
        first.astype(jnp.int32).reshape(1), q_re, q_im, rows, weight, rel, onehot_t
    )
    query_back = lax.ppermute(grad_query, "hop", [(1, 0)])
    query_grad = jnp.where(first, query_back, grad_query)
    z_cols, _ = lax.optimization_barrier((z_cols, grad_query))
    z_cols = lax.ppermute(z_cols, "hop", [(0, 1)])
    rel_got = swap_core(rel_give)

    def chip_at(place):
        place = lax.rem(place, chips)
        return jnp.where(place < (chips + 1) // 2, 2 * place, 2 * (chips - place) - 1)

    ring = list(range(0, chips, 2)) + list(range(1, chips, 2))[::-1]
    place = jnp.where(lax.rem(chip, 2) == 0, chip // 2, chips - 1 - chip // 2)
    up = [(ring[i], ring[(i + 1) % chips]) for i in range(chips)]
    down = [(b, a) for a, b in up]
    blocks = [(right, 0)]
    fwd = bwd = right
    for s in range(1, chips // 2 + 1):
        fwd = lax.ppermute(fwd, "chip", up)
        blocks.append((fwd, chips - s))
        if s < chips - s:
            bwd = lax.ppermute(bwd, "chip", down)
            blocks.append((bwd, s))

    rel_sent = (rel_keep + rel_got).astype(BF16).reshape(chips, 2 * owned, chips, cols)
    rel_sent = rel_sent.transpose(0, 2, 1, 3).reshape(chips, 2 * owned * chips, cols)
    if rel_sent.shape[1] == rows_dev:
        shared = jnp.where(first, columns(query_back), rel_sent)
        shared, _ = lax.optimization_barrier((shared, (blocks[1][0], blocks[2][0])))
        query_cols = rel_rows = lax.all_to_all(shared, "chip", 0, 0, tiled=True)
    else:
        query_cols = lax.all_to_all(columns(query_back), "chip", 0, 0, tiled=True)
        rel_rows = lax.all_to_all(rel_sent, "chip", 0, 0, tiled=True)
    rel_sum = jnp.sum(rel_rows.astype(F32), axis=0) * jnp.sqrt(F32(count_rel) / F32(total_rows))
    rel_sum = rel_sum.reshape(chips, 2 * owned, cols).transpose(1, 0, 2).reshape(2, owned, width)
    relation_grad = jnp.where(first, lax.ppermute(rel_sum[0], "hop", [(1, 0)]), rel_sum[1])

    left_cols = jnp.where(first, query_cols, z_cols)
    partial = jnp.zeros((cols, width), F32)
    for block, step in blocks:
        left = lax.dynamic_index_in_dim(left_cols, chip_at(place + step), 0, keepdims=False)
        partial = partial + dot(left, block, 0, 0)
    partial = partial.reshape(2, cols // 2, width)
    keep = lax.dynamic_index_in_dim(partial, core, 0, keepdims=False)
    give = lax.dynamic_index_in_dim(partial, 1 - core, 0, keepdims=False)
    weight_grad = (keep + swap_core(give)) * (1.0 / jnp.sqrt(F32(total_rows)))
    return weight_grad[None], relation_grad, query_grad


def solution(mesh):
    hops, batch = mesh.devices.shape
    fine = Mesh(mesh.devices.reshape(hops, batch // 2, 2), ("hop", "chip", "core"))
    rows = ("chip", "core")
    return jax.shard_map(
        local,
        mesh=fine,
        in_specs=(P("hop", rows, None), P("hop", None, None), P(), P(rows)),
        out_specs=(P("hop", rows, None), P(("hop", "chip", "core"), None), P(rows, None)),
        check_vma=False,
    )
```

profile of v0, /device:TPU:9, one launch (start us, length us, event | category | flops | bytes accessed | tf_op | source)
XLA Modules:
  0.0 122.5 jit_solution(16090575851109935275)
XLA Ops:
  0.7 4.7 %fusion.12 = bf16[128,1024]{1,0:T(8,128)(2,1)} fusion(bf16[1,2048,2048]{2,1,0:T(8,128)(2,1)} %param.5, bf16[1,128,2048]{2,1,0:T(8,128)(2,1)} %param.4), kind=kOutput, calls=%fused_computation.15 | convolution fusion | flops 537001984 | bytes 4980736 | tf_op jit(solution)/shard_map/dot_general | solution.py:15
  5.4 3.1 %collective-permute-start.1 = (bf16[128,1024]{1,0:T(8,128)(2,1)}, bf16[128,1024]{1,0:T(8,128)(2,1)S(1)}, u32[]{:S(2)}, u32[]{:S(2)}) collective-permute-start(bf16[128,1024]{1,0:T(8,128)(2,1)} %fusion.12), channel_id=1, source_target_pairs={{0,16},{1,17},{2,18},{3,19},{4,20},{5,21},{6,22},{7,23},{8,24},{9,... | collective-permute-start | bytes 786440 | tf_op jit(solution)/shard_map/ppermute | solution.py:119
  8.5 0.3 fusion.58
  8.9 3.6 %fusion.18 = (bf16[128,1024]{1,0:T(8,128)(2,1)}, bf16[128,1024]{1,0:T(8,128)(2,1)}, bf16[128,1024]{1,0:T(8,128)(2,1)}) fusion(bf16[128,1024]{1,0:T(8,128)(2,1)} %fusion.12, f32[128,2048]{1,0:T(8,128)S(1)} %get-tuple-element.19, bf16[1,2048,2048]{2,1,0:T(8,128)(2,1)S(1)} %copy-done.1, bf16[1,128,2048]{2,1,0:T(8,128)(2,1)} %param.4), kind=kOutput, calls=%fused_computation.27 | convolution fusion | flops 538312704 | bytes 6815744 | tf_op jit(solution)/shard_map/dot_general | solution.py:15
  12.5 1.3 %collective-permute-start = (bf16[128,1024]{1,0:T(8,128)(2,1)}, bf16[128,1024]{1,0:T(8,128)(2,1)S(1)}, u32[]{:S(2)}, u32[]{:S(2)}) collective-permute-start(bf16[128,1024]{1,0:T(8,128)(2,1)} %get-tuple-element.21), channel_id=1, source_target_pairs={{0,16},{1,17},{2,18},{3,19},{4,20},{5,21},{6,22},{7,23},{8,24},{9,... | collective-permute-start | bytes 786440 | tf_op jit(solution)/shard_map/ppermute | solution.py:117
  13.9 0.1 compare_convert_fusion.onehot
  14.0 5.7 %collective-permute-done.q_re = bf16[128,1024]{1,0:T(8,128)(2,1)S(1)} collective-permute-done((bf16[128,1024]{1,0:T(8,128)(2,1)}, bf16[128,1024]{1,0:T(8,128)(2,1)S(1)}, u32[]{:S(2)}, u32[]{:S(2)}) %collective-permute-start) | collective-permute-done | bytes 262176 | tf_op jit(solution)/shard_map/ppermute | solution.py:117
  19.7 0.7 copy-done.6
  20.4 3.4 %copy-done.2 = bf16[1,2048,2048]{2,1,0:T(8,128)(2,1)S(1)} copy-done((bf16[1,2048,2048]{2,1,0:T(8,128)(2,1)S(1)}, bf16[1,2048,2048]{2,1,0:T(8,128)(2,1)}, u32[]{:S(2)}) %copy-start.2) | copy-done | bytes 8388632
  23.8 0.9 copy-done.7
  24.7 8.8 %shard_map.67 = (bf16[128,2048]{1,0:T(8,128)(2,1)}, bf16[128,2048]{1,0:T(8,128)(2,1)S(1)}, f32[128,2048]{1,0:T(8,128)}, f32[128,2048]{1,0:T(8,128)S(1)}) custom-call(s32[1]{0:T(128)} %bitcast.first, bf16[128,1024]{1,0:T(8,128)(2,1)S(1)} %copy-done.7, bf16[128,1024]{1,0:T(8,128)(2,1)S(1)} %collective-permute-done.1.q_im, bf16[128,2048]{1,0:T(8,128)(2,1)S(1)} %bitcast.96, ...), custom_call_target="tpu_custom_call" | custom-call | flops 2415919104 | bytes 8388608 | tf_op jit(solution)/shard_map/pallas_call | solution.py:81
  33.5 0.8 copy-done.4
  34.3 1.3 %collective-permute-start.3 = (f32[128,2048]{1,0:T(8,128)}, f32[128,2048]{1,0:T(8,128)}, u32[]{:S(2)}, u32[]{:S(2)}) collective-permute-start(f32[128,2048]{1,0:T(8,128)} %get-tuple-element.11), channel_id=1, source_target_pairs={{0,1},{1,0},{2,3},{3,2},{4,5},{5,4},{6,7},{7,6},{8,9},{9,8},{10,11... | collective-permute-start | bytes 3145736 | tf_op jit(solution)/shard_map/ppermute | solution.py:19
  35.6 1.3 %collective-permute-start.4 = (bf16[128,2048]{1,0:T(8,128)(2,1)}, bf16[128,2048]{1,0:T(8,128)(2,1)}, u32[]{:S(2)}, u32[]{:S(2)}) collective-permute-start(bf16[128,2048]{1,0:T(8,128)(2,1)} %get-tuple-element.12), channel_id=1, source_target_pairs={{0,4},{4,8},{8,12},{12,14},{14,10},{10,6},{6,2},{2,0},{1,5},{5,9},... | collective-permute-start | bytes 1572872 | tf_op jit(solution)/shard_map/ppermute | solution.py:157
  36.9 0.8 copy.16
  37.8 4.7 %all-to-all-start.1 = ((bf16[8,128,256]{2,1,0:T(8,128)(2,1)}), bf16[8,128,256]{2,1,0:T(8,128)(2,1)}, u32[]{:S(2)}, u32[]{:S(2)}) async-start(bf16[8,128,256]{2,1,0:T(8,128)(2,1)} %bitcast.93), calls=%async_computation.1 | async-start | bytes 1048576 | tf_op jit(solution)/shard_map/all_to_all | solution.py:135
  42.5 1.3 %collective-permute-start.2 = (bf16[128,2048]{1,0:T(8,128)(2,1)S(1)}, bf16[128,2048]{1,0:T(8,128)(2,1)S(1)}, u32[]{:S(2)}, u32[]{:S(2)}) collective-permute-start(bf16[128,2048]{1,0:T(8,128)(2,1)S(1)} %copy-done.5), channel_id=1, source_target_pairs={{16,0},{17,1},{18,2},{19,3},{20,4},{21,5},{22,6},{23,7},{24,8},{25... | collective-permute-start | bytes 1572872 | tf_op jit(solution)/shard_map/ppermute | solution.py:140
  43.8 5.6 %collective-permute-done.4 = bf16[128,2048]{1,0:T(8,128)(2,1)} collective-permute-done((bf16[128,2048]{1,0:T(8,128)(2,1)}, bf16[128,2048]{1,0:T(8,128)(2,1)}, u32[]{:S(2)}, u32[]{:S(2)}) %collective-permute-start.4) | collective-permute-done | bytes 524320 | tf_op jit(solution)/shard_map/ppermute | solution.py:157
  49.4 1.4 %collective-permute-start.7 = (bf16[128,2048]{1,0:T(8,128)(2,1)}, bf16[128,2048]{1,0:T(8,128)(2,1)}, u32[]{:S(2)}, u32[]{:S(2)}) collective-permute-start(bf16[128,2048]{1,0:T(8,128)(2,1)} %collective-permute-done.4), channel_id=1, source_target_pairs={{0,4},{4,8},{8,12},{12,14},{14,10},{10,6},{6,2},{2,0},{1,5},{5,9},... | collective-permute-start | bytes 1572872 | tf_op jit(solution)/shard_map/ppermute | solution.py:157
  50.9 1.3 %add_convert_fusion = bf16[128,2048]{1,0:T(8,128)(2,1)S(1)} fusion(f32[128,2048]{1,0:T(8,128)S(1)} %get-tuple-element.10, f32[128,2048]{1,0:T(8,128)} %collective-permute-done.3), kind=kLoop, calls=%fused_computation.21 | loop fusion | flops 524288 | bytes 2621440 | tf_op jit(solution)/shard_map/convert_element_type | solution.py:163
  52.2 0.1 copy.13
  52.3 0.1 copy.9
  52.5 4.7 %collective-permute-done.2 = bf16[128,2048]{1,0:T(8,128)(2,1)S(1)} collective-permute-done((bf16[128,2048]{1,0:T(8,128)(2,1)S(1)}, bf16[128,2048]{1,0:T(8,128)(2,1)S(1)}, u32[]{:S(2)}, u32[]{:S(2)}) %collective-permute-start.2) | collective-permute-done | bytes 524320 | tf_op jit(solution)/shard_map/ppermute | solution.py:140
  57.1 0.9 fusion.21
  58.0 8.7 %collective-permute-done.5 = bf16[128,2048]{1,0:T(8,128)(2,1)} collective-permute-done((bf16[128,2048]{1,0:T(8,128)(2,1)}, bf16[128,2048]{1,0:T(8,128)(2,1)}, u32[]{:S(2)}, u32[]{:S(2)}) %collective-permute-start.5) | collective-permute-done | bytes 524320 | tf_op jit(solution)/shard_map/ppermute | solution.py:160
  66.7 4.6 %all-to-all-start = ((bf16[8,128,256]{2,1,0:T(8,128)(2,1)}), bf16[8,128,256]{2,1,0:T(8,128)(2,1)S(1)}, u32[]{:S(2)}, u32[]{:S(2)}) async-start(bf16[8,128,256]{2,1,0:T(8,128)(2,1)} %fusion.21), calls=%async_computation | async-start | bytes 1048576 | tf_op jit(solution)/shard_map/all_to_all | solution.py:168
  71.3 2.0 %collective-permute-start.9 = (bf16[128,2048]{1,0:T(8,128)(2,1)}, bf16[128,2048]{1,0:T(8,128)(2,1)}, u32[]{:S(2)}, u32[]{:S(2)}) collective-permute-start(bf16[128,2048]{1,0:T(8,128)(2,1)} %collective-permute-done.7), channel_id=1, source_target_pairs={{0,4},{4,8},{8,12},{12,14},{14,10},{10,6},{6,2},{2,0},{1,5},{5,9},... | collective-permute-start | bytes 1572872 | tf_op jit(solution)/shard_map/ppermute | solution.py:157
  73.3 4.8 %collective-permute-start.6 = (bf16[8,128,256]{2,1,0:T(8,128)(2,1)}, bf16[8,128,256]{2,1,0:T(8,128)(2,1)}, u32[]{:S(2)}, u32[]{:S(2)}) collective-permute-start(bf16[8,128,256]{2,1,0:T(8,128)(2,1)} %all-to-all-done.1), channel_id=1, source_target_pairs={{0,16},{1,17},{2,18},{3,19},{4,20},{5,21},{6,22},{7,23},{8,24},{9,... | collective-permute-start | bytes 1572872 | tf_op jit(solution)/shard_map/ppermute | solution.py:143
  78.1 17.2 %collective-permute-done.8 = bf16[128,2048]{1,0:T(8,128)(2,1)} collective-permute-done((bf16[128,2048]{1,0:T(8,128)(2,1)}, bf16[128,2048]{1,0:T(8,128)(2,1)}, u32[]{:S(2)}, u32[]{:S(2)}) %collective-permute-start.8) | collective-permute-done | bytes 524320 | tf_op jit(solution)/shard_map/ppermute | solution.py:160
  95.2 1.5 %collective-permute-start.11 = (bf16[128,2048]{1,0:T(8,128)(2,1)}, bf16[128,2048]{1,0:T(8,128)(2,1)S(1)}, u32[]{:S(2)}, u32[]{:S(2)}) collective-permute-start(bf16[128,2048]{1,0:T(8,128)(2,1)} %collective-permute-done.9), channel_id=1, source_target_pairs={{0,4},{4,8},{8,12},{12,14},{14,10},{10,6},{6,2},{2,0},{1,5},{5,9},... | collective-permute-start | bytes 1572872 | tf_op jit(solution)/shard_map/ppermute | solution.py:157
  96.7 0.1 broadcast_select_fusion.1
  96.8 1.5 %fusion.31 = f32[256,2048]{1,0:T(8,128)S(1)} fusion(bf16[128,2048]{1,0:T(8,128)(2,1)} %collective-permute-done.4, bf16[8,128,256]{2,1,0:T(8,128)(2,1)S(1)} %broadcast_select_fusion.1, s32[]{:T(128)S(6)} %select_n.165), kind=kOutput, calls=%fused_computation.48 | convolution fusion | flops 134217728 | bytes 2686980 | tf_op jit(solution)/shard_map/dot_general | solution.py:15
  98.3 1.5 %fusion.29 = f32[256,2048]{1,0:T(8,128)S(1)} fusion(bf16[128,2048]{1,0:T(8,128)(2,1)} %collective-permute-done.5, bf16[8,128,256]{2,1,0:T(8,128)(2,1)S(1)} %broadcast_select_fusion.1, s32[]{:T(128)S(6)} %select_n.167), kind=kOutput, calls=%fused_computation.46 | convolution fusion | flops 134217728 | bytes 2686980 | tf_op jit(solution)/shard_map/dot_general | solution.py:15
  99.8 1.5 %fusion.26 = f32[256,2048]{1,0:T(8,128)S(1)} fusion(bf16[128,2048]{1,0:T(8,128)(2,1)} %collective-permute-done.8, bf16[8,128,256]{2,1,0:T(8,128)(2,1)S(1)} %broadcast_select_fusion.1, s32[]{:T(128)S(6)} %select_n.171), kind=kOutput, calls=%fused_computation.43 | convolution fusion | flops 134217728 | bytes 2686980 | tf_op jit(solution)/shard_map/dot_general | solution.py:15
  101.3 0.1 convert_reduce_fusion
  101.4 1.5 %fusion.8 = f32[256,2048]{1,0:T(8,128)S(1)} fusion(f32[256,2048]{1,0:T(8,128)S(1)} %fusion.29, f32[256,2048]{1,0:T(8,128)S(1)} %fusion.31, bf16[128,2048]{1,0:T(8,128)(2,1)} %get-tuple-element.12, bf16[8,128,256]{2,1,0:T(8,128)(2,1)S(1)} %broadcast_select_fusion.1, s32[]{:T(128)S(6)} %select_n.163), kind=kOutput, calls=%fused_computation.12 | convolution fusion | flops 135266304 | bytes 6881284 | tf_op jit(solution)/shard_map/dot_general | solution.py:15
  102.9 4.4 %collective-permute-done.10 = bf16[128,2048]{1,0:T(8,128)(2,1)} collective-permute-done((bf16[128,2048]{1,0:T(8,128)(2,1)}, bf16[128,2048]{1,0:T(8,128)(2,1)}, u32[]{:S(2)}, u32[]{:S(2)}) %collective-permute-start.10) | collective-permute-done | bytes 524320 | tf_op jit(solution)/shard_map/ppermute | solution.py:160
  107.3 1.5 %fusion.23 = f32[256,2048]{1,0:T(8,128)S(1)} fusion(bf16[128,2048]{1,0:T(8,128)(2,1)} %collective-permute-done.10, bf16[8,128,256]{2,1,0:T(8,128)(2,1)S(1)} %broadcast_select_fusion.1, s32[]{:T(128)S(6)} %select_n.175), kind=kOutput, calls=%fused_computation.40 | convolution fusion | flops 134217728 | bytes 2686980 | tf_op jit(solution)/shard_map/dot_general | solution.py:15
  108.8 1.5 %fusion.7 = f32[256,2048]{1,0:T(8,128)S(1)} fusion(f32[256,2048]{1,0:T(8,128)S(1)} %fusion.26, f32[256,2048]{1,0:T(8,128)S(1)} %fusion.8, bf16[128,2048]{1,0:T(8,128)(2,1)} %collective-permute-done.7, bf16[8,128,256]{2,1,0:T(8,128)(2,1)S(1)} %broadcast_select_fusion.1, s32[]{:T(128)S(6)} %select_n.169), kind=kOutput, calls=%fused_computation.10 | convolution fusion | flops 135266304 | bytes 6881284 | tf_op jit(solution)/shard_map/dot_general | solution.py:15
  110.3 1.5 %fusion.6 = f32[256,2048]{1,0:T(8,128)S(1)} fusion(f32[256,2048]{1,0:T(8,128)S(1)} %fusion.23, f32[256,2048]{1,0:T(8,128)S(1)} %fusion.7, bf16[128,2048]{1,0:T(8,128)(2,1)} %collective-permute-done.9, bf16[8,128,256]{2,1,0:T(8,128)(2,1)S(1)} %broadcast_select_fusion.1, s32[]{:T(128)S(6)} %select_n.173), kind=kOutput, calls=%fused_computation.8 | convolution fusion | flops 135266304 | bytes 6881284 | tf_op jit(solution)/shard_map/dot_general | solution.py:15
  111.9 0.5 convolution_add_fusion
  112.3 0.1 dynamic-slice_bitcast_fusion
  112.4 2.7 %collective-permute-start.12 = (f32[128,2048]{1,0:T(8,128)S(1)}, f32[128,2048]{1,0:T(8,128)S(1)}, u32[]{:S(2)}, u32[]{:S(2)}) collective-permute-start(f32[128,2048]{1,0:T(8,128)S(1)} %dynamic-slice_bitcast_fusion), channel_id=1, source_target_pairs={{0,1},{1,0},{2,3},{3,2},{4,5},{5,4},{6,7},{7,6},{8,9},{9,8},{10,11... | collective-permute-start | bytes 3145736 | tf_op jit(solution)/shard_map/ppermute | solution.py:19
  115.1 1.3 %collective-permute-start.13 = (f32[8,2048]{1,0:T(8,128)S(1)}, f32[8,2048]{1,0:T(8,128)S(1)}, u32[]{:S(2)}, u32[]{:S(2)}) collective-permute-start(f32[8,2048]{1,0:T(8,128)S(1)} %bitcast.105), channel_id=1, source_target_pairs={{16,0},{17,1},{18,2},{19,3},{20,4},{21,5},{22,6},{23,7},{24,8},{25... | collective-permute-start | bytes 196616 | tf_op jit(solution)/shard_map/ppermute | solution.py:174
  116.4 0.9 broadcast_select_fusion
  117.3 3.5 %collective-permute-done.13 = f32[8,2048]{1,0:T(8,128)S(1)} collective-permute-done((f32[8,2048]{1,0:T(8,128)S(1)}, f32[8,2048]{1,0:T(8,128)S(1)}, u32[]{:S(2)}, u32[]{:S(2)}) %collective-permute-start.13) | collective-permute-done | bytes 65568 | tf_op jit(solution)/shard_map/ppermute | solution.py:174
  120.7 0.6 broadcast_select_fusion.2
  121.4 1.1 fusion.16
  (35 shorter events, 0.2 us)
Async XLA Ops:
  0.6 7.9 %copy-start = (bf16[256,2048]{1,0:T(8,128)(2,1)S(1)}, bf16[256,2048]{1,0:T(8,128)(2,1)}, u32[]{:S(2)}) copy-start(bf16[256,2048]{1,0:T(8,128)(2,1)} %param.6) | copy-start | bytes 3145732
  0.6 7.9 %copy-start.10 = (s32[128]{0:T(128)S(1)}, s32[128]{0:T(128)}, u32[]{:S(2)}) copy-start(s32[128]{0:T(128)} %param.7) | copy-start | bytes 1540
  0.7 8.2 %copy-start.1 = (bf16[1,2048,2048]{2,1,0:T(8,128)(2,1)S(1)}, bf16[1,2048,2048]{2,1,0:T(8,128)(2,1)}, u32[]{:S(2)}) copy-start(bf16[1,2048,2048]{2,1,0:T(8,128)(2,1)} %param.5) | copy-start | bytes 25165828
  5.4 15.0 %collective-permute-start.1 = (bf16[128,1024]{1,0:T(8,128)(2,1)}, bf16[128,1024]{1,0:T(8,128)(2,1)S(1)}, u32[]{:S(2)}, u32[]{:S(2)}) collective-permute-start(bf16[128,1024]{1,0:T(8,128)(2,1)} %fusion.12), channel_id=1, source_target_pairs={{0,16},{1,17},{2,18},{3,19},{4,20},{5,21},{6,22},{7,23},{8,24},{9,... | collective-permute-start | bytes 786440 | tf_op jit(solution)/shard_map/ppermute | solution.py:119
  8.9 11.5 %copy-start.3 = (bf16[1,128,2048]{2,1,0:T(8,128)(2,1)S(1)}, bf16[1,128,2048]{2,1,0:T(8,128)(2,1)}, u32[]{:S(2)}) copy-start(bf16[1,128,2048]{2,1,0:T(8,128)(2,1)} %param.4) | copy-start | bytes 1572868
  12.5 7.1 %collective-permute-start = (bf16[128,1024]{1,0:T(8,128)(2,1)}, bf16[128,1024]{1,0:T(8,128)(2,1)S(1)}, u32[]{:S(2)}, u32[]{:S(2)}) collective-permute-start(bf16[128,1024]{1,0:T(8,128)(2,1)} %get-tuple-element.21), channel_id=1, source_target_pairs={{0,16},{1,17},{2,18},{3,19},{4,20},{5,21},{6,22},{7,23},{8,24},{9,... | collective-permute-start | bytes 786440 | tf_op jit(solution)/shard_map/ppermute | solution.py:117
  19.7 0.7 copy-start.6
  20.4 3.4 %copy-start.2 = (bf16[1,2048,2048]{2,1,0:T(8,128)(2,1)S(1)}, bf16[1,2048,2048]{2,1,0:T(8,128)(2,1)}, u32[]{:S(2)}) copy-start(bf16[1,2048,2048]{2,1,0:T(8,128)(2,1)} %param.5) | copy-start | bytes 25165828
  23.8 0.9 copy-start.7
  24.7 12.2 %copy-start.8 = (bf16[128,1024]{1,0:T(8,128)(2,1)S(1)}, bf16[128,1024]{1,0:T(8,128)(2,1)}, u32[]{:S(2)}) copy-start(bf16[128,1024]{1,0:T(8,128)(2,1)} %get-tuple-element.15) | copy-start | bytes 786436
  24.7 12.2 %copy-start.9 = (bf16[128,1024]{1,0:T(8,128)(2,1)S(1)}, bf16[128,1024]{1,0:T(8,128)(2,1)}, u32[]{:S(2)}) copy-start(bf16[128,1024]{1,0:T(8,128)(2,1)} %get-tuple-element.16) | copy-start | bytes 786436
  33.5 0.8 copy-start.4
  34.3 8.2 %copy-start.5 = (bf16[128,2048]{1,0:T(8,128)(2,1)S(1)}, bf16[128,2048]{1,0:T(8,128)(2,1)}, u32[]{:S(2)}) copy-start(bf16[128,2048]{1,0:T(8,128)(2,1)} %copy-done.4) | copy-start | bytes 1572868
  34.3 16.5 %collective-permute-start.3 = (f32[128,2048]{1,0:T(8,128)}, f32[128,2048]{1,0:T(8,128)}, u32[]{:S(2)}, u32[]{:S(2)}) collective-permute-start(f32[128,2048]{1,0:T(8,128)} %get-tuple-element.11), channel_id=1, source_target_pairs={{0,1},{1,0},{2,3},{3,2},{4,5},{5,4},{6,7},{7,6},{8,9},{9,8},{10,11... | collective-permute-start | bytes 3145736 | tf_op jit(solution)/shard_map/ppermute | solution.py:19
  35.6 13.9 %collective-permute-start.4 = (bf16[128,2048]{1,0:T(8,128)(2,1)}, bf16[128,2048]{1,0:T(8,128)(2,1)}, u32[]{:S(2)}, u32[]{:S(2)}) collective-permute-start(bf16[128,2048]{1,0:T(8,128)(2,1)} %get-tuple-element.12), channel_id=1, source_target_pairs={{0,4},{4,8},{8,12},{12,14},{14,10},{10,6},{6,2},{2,0},{1,5},{5,9},... | collective-permute-start | bytes 1572872 | tf_op jit(solution)/shard_map/ppermute | solution.py:157
  37.8 28.9 %all-to-all-start.1 = ((bf16[8,128,256]{2,1,0:T(8,128)(2,1)}), bf16[8,128,256]{2,1,0:T(8,128)(2,1)}, u32[]{:S(2)}, u32[]{:S(2)}) async-start(bf16[8,128,256]{2,1,0:T(8,128)(2,1)} %bitcast.93), calls=%async_computation.1 | async-start | bytes 1048576 | tf_op jit(solution)/shard_map/all_to_all | solution.py:135
  42.5 24.2 %collective-permute-start.5 = (bf16[128,2048]{1,0:T(8,128)(2,1)}, bf16[128,2048]{1,0:T(8,128)(2,1)}, u32[]{:S(2)}, u32[]{:S(2)}) collective-permute-start(bf16[128,2048]{1,0:T(8,128)(2,1)} %get-tuple-element.12), channel_id=1, source_target_pairs={{4,0},{8,4},{12,8},{14,12},{10,14},{6,10},{2,6},{0,2},{5,1},{9,5},... | collective-permute-start | bytes 1572872 | tf_op jit(solution)/shard_map/ppermute | solution.py:160
  42.5 14.6 %collective-permute-start.2 = (bf16[128,2048]{1,0:T(8,128)(2,1)S(1)}, bf16[128,2048]{1,0:T(8,128)(2,1)S(1)}, u32[]{:S(2)}, u32[]{:S(2)}) collective-permute-start(bf16[128,2048]{1,0:T(8,128)(2,1)S(1)} %copy-done.5), channel_id=1, source_target_pairs={{16,0},{17,1},{18,2},{19,3},{20,4},{21,5},{22,6},{23,7},{24,8},{25... | collective-permute-start | bytes 1572872 | tf_op jit(solution)/shard_map/ppermute | solution.py:140
  49.4 21.9 %collective-permute-start.7 = (bf16[128,2048]{1,0:T(8,128)(2,1)}, bf16[128,2048]{1,0:T(8,128)(2,1)}, u32[]{:S(2)}, u32[]{:S(2)}) collective-permute-start(bf16[128,2048]{1,0:T(8,128)(2,1)} %collective-permute-done.4), channel_id=1, source_target_pairs={{0,4},{4,8},{8,12},{12,14},{14,10},{10,6},{6,2},{2,0},{1,5},{5,9},... | collective-permute-start | bytes 1572872 | tf_op jit(solution)/shard_map/ppermute | solution.py:157
  66.7 30.0 %all-to-all-start = ((bf16[8,128,256]{2,1,0:T(8,128)(2,1)}), bf16[8,128,256]{2,1,0:T(8,128)(2,1)S(1)}, u32[]{:S(2)}, u32[]{:S(2)}) async-start(bf16[8,128,256]{2,1,0:T(8,128)(2,1)} %fusion.21), calls=%async_computation | async-start | bytes 1048576 | tf_op jit(solution)/shard_map/all_to_all | solution.py:168
  71.3 23.9 %collective-permute-start.8 = (bf16[128,2048]{1,0:T(8,128)(2,1)}, bf16[128,2048]{1,0:T(8,128)(2,1)}, u32[]{:S(2)}, u32[]{:S(2)}) collective-permute-start(bf16[128,2048]{1,0:T(8,128)(2,1)} %collective-permute-done.5), channel_id=1, source_target_pairs={{4,0},{8,4},{12,8},{14,12},{10,14},{6,10},{2,6},{0,2},{5,1},{9,5},... | collective-permute-start | bytes 1572872 | tf_op jit(solution)/shard_map/ppermute | solution.py:160
  71.3 23.9 %collective-permute-start.9 = (bf16[128,2048]{1,0:T(8,128)(2,1)}, bf16[128,2048]{1,0:T(8,128)(2,1)}, u32[]{:S(2)}, u32[]{:S(2)}) collective-permute-start(bf16[128,2048]{1,0:T(8,128)(2,1)} %collective-permute-done.7), channel_id=1, source_target_pairs={{0,4},{4,8},{8,12},{12,14},{14,10},{10,6},{6,2},{2,0},{1,5},{5,9},... | collective-permute-start | bytes 1572872 | tf_op jit(solution)/shard_map/ppermute | solution.py:157
  73.3 23.4 %collective-permute-start.6 = (bf16[8,128,256]{2,1,0:T(8,128)(2,1)}, bf16[8,128,256]{2,1,0:T(8,128)(2,1)}, u32[]{:S(2)}, u32[]{:S(2)}) collective-permute-start(bf16[8,128,256]{2,1,0:T(8,128)(2,1)} %all-to-all-done.1), channel_id=1, source_target_pairs={{0,16},{1,17},{2,18},{3,19},{4,20},{5,21},{6,22},{7,23},{8,24},{9,... | collective-permute-start | bytes 1572872 | tf_op jit(solution)/shard_map/ppermute | solution.py:143
  95.2 12.1 %collective-permute-start.10 = (bf16[128,2048]{1,0:T(8,128)(2,1)}, bf16[128,2048]{1,0:T(8,128)(2,1)}, u32[]{:S(2)}, u32[]{:S(2)}) collective-permute-start(bf16[128,2048]{1,0:T(8,128)(2,1)} %collective-permute-done.8), channel_id=1, source_target_pairs={{4,0},{8,4},{12,8},{14,12},{10,14},{6,10},{2,6},{0,2},{5,1},{9,5},... | collective-permute-start | bytes 1572872 | tf_op jit(solution)/shard_map/ppermute | solution.py:160
  95.2 16.6 %collective-permute-start.11 = (bf16[128,2048]{1,0:T(8,128)(2,1)}, bf16[128,2048]{1,0:T(8,128)(2,1)S(1)}, u32[]{:S(2)}, u32[]{:S(2)}) collective-permute-start(bf16[128,2048]{1,0:T(8,128)(2,1)} %collective-permute-done.9), channel_id=1, source_target_pairs={{0,4},{4,8},{8,12},{12,14},{14,10},{10,6},{6,2},{2,0},{1,5},{5,9},... | collective-permute-start | bytes 1572872 | tf_op jit(solution)/shard_map/ppermute | solution.py:157
  112.4 8.9 %collective-permute-start.12 = (f32[128,2048]{1,0:T(8,128)S(1)}, f32[128,2048]{1,0:T(8,128)S(1)}, u32[]{:S(2)}, u32[]{:S(2)}) collective-permute-start(f32[128,2048]{1,0:T(8,128)S(1)} %dynamic-slice_bitcast_fusion), channel_id=1, source_target_pairs={{0,1},{1,0},{2,3},{3,2},{4,5},{5,4},{6,7},{7,6},{8,9},{9,8},{10,11... | collective-permute-start | bytes 3145736 | tf_op jit(solution)/shard_map/ppermute | solution.py:19
  115.1 5.6 %collective-permute-start.13 = (f32[8,2048]{1,0:T(8,128)S(1)}, f32[8,2048]{1,0:T(8,128)S(1)}, u32[]{:S(2)}, u32[]{:S(2)}) collective-permute-start(f32[8,2048]{1,0:T(8,128)S(1)} %bitcast.105), channel_id=1, source_target_pairs={{16,0},{17,1},{18,2},{19,3},{20,4},{21,5},{22,6},{23,7},{24,8},{25... | collective-permute-start | bytes 196616 | tf_op jit(solution)/shard_map/ppermute | solution.py:174
where the time goes:
time: 125 us; the launch traced here: 122 us
  waiting for transfers between devices  49.7 us (40%)
  starting transfers between devices  31.2 us (25%)
  matrix products  19.7 us (16%)
  Pallas kernels  8.79 us (7%)
  local copies, waits for them, and re-layouts  7.07 us (6%)
  other arithmetic  5.09 us (4%)
    ppermute x3, waiting for transfers between devices, local(): bwd = lax.ppermute(bwd, 'chip', down)  30.2 us
    dot_general x11, matrix products, dot(): lax.dot_general(a, b, (((ca,), (cb,)), ((), ())), preferred_element_type=...  19.7 us
    pallas_call x1, Pallas kernels, trail(): pl.pallas_call(trail_body, out_shape=(jax.ShapeDtypeStruct((rows_dev, hid...  8.79 us
    ppermute x4, starting transfers between devices, local(): fwd = lax.ppermute(fwd, 'chip', up)  6.12 us
    unnamed x23, local copies, waits for them, and re-layouts  5.98 us
    ppermute x1, waiting for transfers between devices, local(): q_re = lax.ppermute(own_re, 'hop', [(0, 1)])  5.68 us
    ppermute x4, waiting for transfers between devices, local(): fwd = lax.ppermute(fwd, 'chip', up)  5.66 us
    ppermute x1, starting transfers between devices, local(): z_cols = lax.ppermute(z_cols, 'hop', [(0, 1)])  4.8 us
  transfers between devices with their start and end apart: 16, of which 7 were waited for; matrix products, arithmetic and copies ran while one was open for 16% of the time, Pallas kernels for 0%

commit v1 on v0

--- a/solution.py
+++ b/solution.py
@@ -23,28 +23,91 @@
     return (q_re * r_re - q_im * r_im).astype(BF16), (q_re * r_im + q_im * r_re).astype(BF16)
 
 
-def trail_body(first, q_re, q_im, rows, weight, rel, onehot, right, query_grad, give, keep, mixed, hidden):
+def at(step, base=0):
+    return pl.ds(pl.multiple_of(base + step * TILE, TILE), TILE)
+
+
+def lead_body(rows, weight, onehot, table, query, mixed, rel, held, sems):
+    half = weight.shape[0] // 2
+    steps = half // TILE
+
+    def load(step, side):
+        piece = at(step, side * half)
+        return pltpu.make_async_copy(weight.at[piece], held.at[piece], sems.at[2 * step + side])
+
+    for step in range(steps):
+        for side in range(2):
+            load(step, side).start()
+    for step in range(steps):
+        span = pl.ds(step * TILE, TILE)
+        r_re = dot(onehot[...], table[:, at(step)], 1, 0)
+        r_im = dot(onehot[...], table[:, at(step, half)], 1, 0)
+        load(step, 0).wait()
+        q_re = dot(rows[...], held[at(step)], 1, 1).astype(BF16)
+        load(step, 1).wait()
+        q_im = dot(rows[...], held[at(step, half)], 1, 1).astype(BF16)
+        query[0, :, span], query[1, :, span] = q_re, q_im
+        rel[0, :, span], rel[1, :, span] = r_re.astype(BF16), r_im.astype(BF16)
+        z_re, z_im = mix(q_re.astype(F32), q_im.astype(F32), r_re, r_im)
+        if mixed.shape[2] == TILE:
+            mixed[step], mixed[steps + step] = z_re, z_im
+        else:
+            mixed[0, :, span], mixed[1, :, span] = z_re, z_im
+
+
+def lead(rows, weight, onehot, table, chips):
+    rows_dev, hidden = rows.shape
+    width = weight.shape[0]
+    half = width // 2
+    cols = width // chips
+    count_rel = table.shape[0]
+    vmem = pl.BlockSpec(memory_space=pltpu.VMEM)
+    pair = jax.ShapeDtypeStruct((2, rows_dev, half), BF16)
+    apart = jax.ShapeDtypeStruct((chips, rows_dev, cols), BF16) if cols == TILE else pair
+    query, mixed, rel = pl.pallas_call(
+        lead_body,
+        out_shape=(pair, apart, pair),
+        in_specs=[vmem, pl.BlockSpec(memory_space=pltpu.HBM), vmem, vmem],
+        out_specs=(vmem,) * 3,
+        scratch_shapes=[
+            pltpu.VMEM((width, hidden), BF16),
+            pltpu.SemaphoreType.DMA((width // TILE,)),
+        ],
+        compiler_params=pltpu.CompilerParams(vmem_limit_bytes=56 * 1024 * 1024),
+        cost_estimate=pl.CostEstimate(
+            flops=2 * rows_dev * width * (hidden + count_rel), bytes_accessed=2 * width * hidden, transcendentals=0
+        ),
+    )(rows, weight, onehot, table)
+    if cols != TILE:
+        mixed = mixed.reshape(2, rows_dev, chips // 2, cols).transpose(0, 2, 1, 3).reshape(chips, rows_dev, cols)
+    return query, mixed, rel
+
+
+def trail_body(first, query, rows, weight, rel, onehot, right, query_grad, give, keep, mixed, hidden, held, sems):
     width = weight.shape[0]
     half = width // 2
     is_first = first[0] == 1
     owned = give.shape[0]
-
-    def at(step, base=0):
-        return pl.ds(pl.multiple_of(base + step * TILE, TILE), TILE)
+    tiles = weight.shape[1] // TILE
+
+    def load(step):
+        return pltpu.make_async_copy(weight.at[:, at(step)], held.at[:, at(step)], sems.at[step])
+
+    for step in range(tiles):
+        load(step).start()
 
     def make_mixed(step, carry):
-        z_re, z_im = mix(
-            q_re[:, at(step)].astype(F32), q_im[:, at(step)].astype(F32),
-            rel[:, at(step)].astype(F32), rel[:, at(step, half)].astype(F32),
+        mixed[:, at(step)], mixed[:, at(step, half)] = mix(
+            query[0, :, at(step)].astype(F32), query[1, :, at(step)].astype(F32),
+            rel[0, :, at(step)].astype(F32), rel[1, :, at(step)].astype(F32),
         )
-        mixed[:, at(step)] = z_re
-        mixed[:, at(step, half)] = z_im
         return carry
 
     lax.fori_loop(0, half // TILE, make_mixed, 0)
 
     def make_hidden(step, carry):
-        pre = dot(mixed[...], weight[:, at(step)], 1, 0)
+        load(step).wait()
+        pre = dot(mixed[...], held[:, at(step)], 1, 0)
         sig = jax.nn.sigmoid(pre)
         cot = rows[:, at(step)]
         grad = (cot.astype(F32) * (sig * (1.0 + pre * (1.0 - sig)))).astype(BF16)
@@ -52,15 +115,15 @@
         right[:, at(step)] = jnp.where(is_first, cot, grad)
         return carry
 
-    lax.fori_loop(0, weight.shape[1] // TILE, make_hidden, 0)
+    lax.fori_loop(0, tiles, make_hidden, 0)
 
     def make_query(step, carry):
-        gz_re = dot(hidden[...], weight[at(step), :], 1, 1)
-        gz_im = dot(hidden[...], weight[at(step, half), :], 1, 1)
-        r_re, r_im = rel[:, at(step)].astype(F32), rel[:, at(step, half)].astype(F32)
+        gz_re = dot(hidden[...], held[at(step), :], 1, 1)
+        gz_im = dot(hidden[...], held[at(step, half), :], 1, 1)
+        r_re, r_im = rel[0, :, at(step)].astype(F32), rel[1, :, at(step)].astype(F32)
         query_grad[:, at(step)] = (gz_re * r_re + gz_im * r_im).astype(BF16)
         query_grad[:, at(step, half)] = (gz_im * r_re - gz_re * r_im).astype(BF16)
-        a, b = q_re[:, at(step)].astype(F32), q_im[:, at(step)].astype(F32)
+        a, b = query[0, :, at(step)].astype(F32), query[1, :, at(step)].astype(F32)
         for base, grad in ((0, gz_re * a + gz_im * b), (half, gz_im * a - gz_re * b)):
             head = grad.astype(BF16)
             rest = (grad - head.astype(F32)).astype(BF16)
@@ -72,7 +135,7 @@
     lax.fori_loop(0, half // TILE, make_query, 0)
 
 
-def trail(first, q_re, q_im, rows, weight, rel, onehot):
+def trail(first, query, rows, weight, rel, onehot):
     rows_dev, hidden = rows.shape
     width = weight.shape[0]
     count_rel = onehot.shape[0]
@@ -86,14 +149,19 @@
             jax.ShapeDtypeStruct((count_rel // 2, width), F32),
             jax.ShapeDtypeStruct((count_rel // 2, width), F32),
         ),
-        in_specs=[pl.BlockSpec(memory_space=pltpu.SMEM)] + [vmem] * 6,
+        in_specs=[pl.BlockSpec(memory_space=pltpu.SMEM), vmem, vmem, pl.BlockSpec(memory_space=pltpu.HBM), vmem, vmem],
         out_specs=(vmem,) * 4,
-        scratch_shapes=[pltpu.VMEM((rows_dev, width), BF16), pltpu.VMEM((rows_dev, hidden), BF16)],
-        compiler_params=pltpu.CompilerParams(vmem_limit_bytes=40 * 1024 * 1024),
+        scratch_shapes=[
+            pltpu.VMEM((rows_dev, width), BF16),
+            pltpu.VMEM((rows_dev, hidden), BF16),
+            pltpu.VMEM((width, hidden), BF16),
+            pltpu.SemaphoreType.DMA((hidden // TILE,)),
+        ],
+        compiler_params=pltpu.CompilerParams(vmem_limit_bytes=56 * 1024 * 1024),
         cost_estimate=pl.CostEstimate(
             flops=flops, bytes_accessed=2 * width * hidden, transcendentals=rows_dev * hidden
         ),
-    )(first, q_re, q_im, rows, weight, rel, onehot)
+    )(first, query, rows, weight, rel, onehot)
 
 
 def local(section_rows, weights, relation_table, relation_ids):
@@ -113,13 +181,7 @@
     def columns(left):
         return left.reshape(left.shape[0], chips, cols).transpose(1, 0, 2)
 
-    own_re = dot(rows, weight[:half], 1, 1).astype(BF16)
-    q_re = lax.ppermute(own_re, "hop", [(0, 1)])
-    own_im = dot(rows, weight[half:], 1, 1).astype(BF16)
-    q_im = lax.ppermute(own_im, "hop", [(0, 1)])
-
     onehot = (relation_ids[:, None] == lax.iota(jnp.int32, count_rel)[None, :]).astype(BF16)
-    rel = dot(onehot, relation_table, 1, 0).astype(BF16)
     number = lax.iota(jnp.int32, count_rel)
     side = number // (count_rel // 2)
     dest = number % (count_rel // 2) // (2 * owned)
@@ -128,14 +190,13 @@
     relation = ((hop * chips + dest) * 2 + which_core) * owned + number % owned
     onehot_t = (relation[:, None] == relation_ids[None, :]).astype(BF16)
 
-    relf = rel.astype(F32)
-    own_z = jnp.concatenate(
-        mix(own_re.astype(F32), own_im.astype(F32), relf[:, :half], relf[:, half:]), axis=1
-    )
-    z_cols = lax.all_to_all(columns(own_z), "chip", 0, 0, tiled=True)
+    own_query, own_mixed, rel = lead(rows, weight, onehot, relation_table, chips)
+    query = lax.ppermute(own_query, "hop", [(0, 1)])
+    z_cols = lax.all_to_all(own_mixed, "chip", 0, 0, tiled=True)
+    query, z_cols = lax.optimization_barrier((query, z_cols))
 
     right, grad_query, rel_give, rel_keep = trail(
-        first.astype(jnp.int32).reshape(1), q_re, q_im, rows, weight, rel, onehot_t
+        first.astype(jnp.int32).reshape(1), query, rows, weight, rel, onehot_t
     )
     query_back = lax.ppermute(grad_query, "hop", [(1, 0)])
     query_grad = jnp.where(first, query_back, grad_query)
@@ -151,14 +212,16 @@
     place = jnp.where(lax.rem(chip, 2) == 0, chip // 2, chips - 1 - chip // 2)
     up = [(ring[i], ring[(i + 1) % chips]) for i in range(chips)]
     down = [(b, a) for a, b in up]
-    blocks = [(right, 0)]
+    blocks = [(right, 0, 0)]
     fwd = bwd = right
-    for s in range(1, chips // 2 + 1):
+    for s in range(1, (chips + 1) // 2):
         fwd = lax.ppermute(fwd, "chip", up)
-        blocks.append((fwd, chips - s))
-        if s < chips - s:
-            bwd = lax.ppermute(bwd, "chip", down)
-            blocks.append((bwd, s))
+        bwd = lax.ppermute(bwd, "chip", down)
+        blocks += [(fwd, chips - s, 0), (bwd, s, 0)]
+    if chips % 2 == 0:
+        mid = rows_dev // 2
+        blocks.append((lax.ppermute(fwd[:mid], "chip", up), chips // 2, 0))
+        blocks.append((lax.ppermute(bwd[mid:], "chip", down), chips // 2, mid))
 
     rel_sent = (rel_keep + rel_got).astype(BF16).reshape(chips, 2 * owned, chips, cols)
     rel_sent = rel_sent.transpose(0, 2, 1, 3).reshape(chips, 2 * owned * chips, cols)
@@ -175,9 +238,11 @@
 
     left_cols = jnp.where(first, query_cols, z_cols)
     partial = jnp.zeros((cols, width), F32)
-    for block, step in blocks:
+    for block, step, base in blocks:
         left = lax.dynamic_index_in_dim(left_cols, chip_at(place + step), 0, keepdims=False)
-        partial = partial + dot(left, block, 0, 0)
+        if step == chips // 2:
+            left, relation_grad = lax.optimization_barrier((left, relation_grad))
+        partial = partial + dot(left[base:base + block.shape[0]], block, 0, 0)
     partial = partial.reshape(2, cols // 2, width)
     keep = lax.dynamic_index_in_dim(partial, core, 0, keepdims=False)
     give = lax.dynamic_index_in_dim(partial, 1 - core, 0, keepdims=False)

time: 125 us -> 118 us (0.944)
  the two profiles are of different devices: /device:TPU:9 before, /device:TPU:15 now
where the time goes in v1:
time: 118 us
  waiting for transfers between devices  48.7 us (41%)
  starting transfers between devices  27.4 us (23%)
  Pallas kernels  21.3 us (18%)
  other arithmetic  9.34 us (8%)
  matrix products  6.36 us (5%)
  local copies, waits for them, and re-layouts  3.68 us (3%)
    ppermute x3, waiting for transfers between devices, local(): fwd = lax.ppermute(fwd, 'chip', up)  23.8 us
    ppermute x1, waiting for transfers between devices, local(): query = lax.ppermute(own_query, 'hop', [(0, 1)])  12.2 us
    pallas_call x1, Pallas kernels, trail(): pl.pallas_call(trail_body, out_shape=(jax.ShapeDtypeStruct((rows_dev, hid...  11.6 us
    ppermute x3, waiting for transfers between devices, local(): bwd = lax.ppermute(bwd, 'chip', down)  10.9 us
    pallas_call x1, Pallas kernels, lead(): pl.pallas_call(lead_body, out_shape=(pair, apart, pair), in_specs=[vmem,...  9.7 us
    dot_general x9, matrix products, dot(): lax.dot_general(a, b, (((ca,), (cb,)), ((), ())), preferred_element_type=...  6.36 us
    all_to_all x1, starting transfers between devices, local(): z_cols = lax.all_to_all(own_mixed, 'chip', 0, 0, tiled=True)  5.67 us
    all_to_all x1, starting transfers between devices, local(): query_cols = rel_rows = lax.all_to_all(shared, 'chip', 0, 0, tiled=True)  5.44 us
  transfers between devices with their start and end apart: 16, of which 5 were waited for; matrix products, arithmetic and copies ran while one was open for 11% of the time, Pallas kernels for 0%

profile of v1, /device:TPU:15, one launch (start us, length us, event | category | flops | bytes accessed | tf_op | source)
XLA Modules:
  0.0 117.6 jit_solution(15756850076396219196)
XLA Ops:
  0.6 1.4 %fusion.8.onehot = bf16[128,256]{1,0:T(8,128)(2,1)} fusion(s32[128]{0:T(128)} %param.7), kind=kLoop, calls=%fused_computation.20 | loop fusion | flops 65536 | bytes 66048 | tf_op jit(solution)/shard_map/convert_element_type | solution.py:184
  2.0 9.7 %shard_map.67 = (bf16[2,128,1024]{2,1,0:T(8,128)(2,1)}, bf16[8,128,256]{2,1,0:T(8,128)(2,1)}, bf16[2,128,1024]{2,1,0:T(8,128)(2,1)}) custom-call(bf16[128,2048]{1,0:T(8,128)(2,1)} %bitcast.73, bf16[2048,2048]{1,0:T(8,128)(2,1)} %bitcast.69, bf16[128,256]{1,0:T(8,128)(2,1)} %fusion.8.onehot, bf16[256,2048]{1,0:T(8,128)(2,1)} %table.1), custom_call_target="tpu_custom_call" | custom-call | flops 1207959552 | bytes 8388608 | tf_op jit(solution)/shard_map/pallas_call | solution.py:67
  11.7 5.7 %all-to-all-start = ((bf16[8,128,256]{2,1,0:T(8,128)(2,1)}), bf16[8,128,256]{2,1,0:T(8,128)(2,1)S(1)}, u32[]{:S(2)}, u32[]{:S(2)}) async-start(bf16[8,128,256]{2,1,0:T(8,128)(2,1)} %get-tuple-element.19), calls=%async_computation | async-start | bytes 1048576 | tf_op jit(solution)/shard_map/all_to_all | solution.py:195
  17.4 1.3 %collective-permute-start = (bf16[2,128,1024]{2,1,0:T(8,128)(2,1)}, bf16[2,128,1024]{2,1,0:T(8,128)(2,1)S(1)}, u32[]{:S(2)}, u32[]{:S(2)}) collective-permute-start(bf16[2,128,1024]{2,1,0:T(8,128)(2,1)} %get-tuple-element.18), channel_id=1, source_target_pairs={{0,16},{1,17},{2,18},{3,19},{4,20},{5,21},{6,22},{7,23},{8,24},{9,... | collective-permute-start | bytes 1572872 | tf_op jit(solution)/shard_map/ppermute | solution.py:194
  18.7 0.7 compare_convert_fusion.onehot
  19.4 12.2 %collective-permute-done.query = bf16[2,128,1024]{2,1,0:T(8,128)(2,1)S(1)} collective-permute-done((bf16[2,128,1024]{2,1,0:T(8,128)(2,1)}, bf16[2,128,1024]{2,1,0:T(8,128)(2,1)S(1)}, u32[]{:S(2)}, u32[]{:S(2)}) %collective-permute-start) | collective-permute-done | bytes 524320 | tf_op jit(solution)/shard_map/ppermute | solution.py:194
  31.7 0.8 copy-done
  32.4 11.6 %shard_map.68 = (bf16[128,2048]{1,0:T(8,128)(2,1)}, bf16[128,2048]{1,0:T(8,128)(2,1)}, f32[128,2048]{1,0:T(8,128)}, f32[128,2048]{1,0:T(8,128)}) custom-call(s32[1]{0:T(128)} %bitcast.first, bf16[2,128,1024]{2,1,0:T(8,128)(2,1)} %copy-done, bf16[128,2048]{1,0:T(8,128)(2,1)} %bitcast.74, bf16[2048,2048]{1,0:T(8,128)(2,1)} %bitcast.70, ...), custom_call_target="tpu_custom_call" | custom-call | flops 2415919104 | bytes 8388608 | tf_op jit(solution)/shard_map/pallas_call | solution.py:144
  44.0 2.2 %collective-permute-start.2 = (f32[128,2048]{1,0:T(8,128)}, f32[128,2048]{1,0:T(8,128)S(1)}, u32[]{:S(2)}, u32[]{:S(2)}) collective-permute-start(f32[128,2048]{1,0:T(8,128)} %get-tuple-element.24), channel_id=1, source_target_pairs={{0,1},{1,0},{2,3},{3,2},{4,5},{5,4},{6,7},{7,6},{8,9},{9,8},{10,11... | collective-permute-start | bytes 3145736 | tf_op jit(solution)/shard_map/ppermute | solution.py:19
  46.3 1.2 %collective-permute-start.4 = (bf16[128,2048]{1,0:T(8,128)(2,1)}, bf16[128,2048]{1,0:T(8,128)(2,1)S(1)}, u32[]{:S(2)}, u32[]{:S(2)}) collective-permute-start(bf16[128,2048]{1,0:T(8,128)(2,1)} %get-tuple-element.25), channel_id=1, source_target_pairs={{4,0},{8,4},{12,8},{14,12},{10,14},{6,10},{2,6},{0,2},{5,1},{9,5},... | collective-permute-start | bytes 1572872 | tf_op jit(solution)/shard_map/ppermute | solution.py:219
  47.4 0.3 collective-permute-start.3
  47.7 1.3 %collective-permute-start.1 = (bf16[128,2048]{1,0:T(8,128)(2,1)}, bf16[128,2048]{1,0:T(8,128)(2,1)S(1)}, u32[]{:S(2)}, u32[]{:S(2)}) collective-permute-start(bf16[128,2048]{1,0:T(8,128)(2,1)} %get-tuple-element.22), channel_id=1, source_target_pairs={{16,0},{17,1},{18,2},{19,3},{20,4},{21,5},{22,6},{23,7},{24,8},{25... | collective-permute-start | bytes 1572872 | tf_op jit(solution)/shard_map/ppermute | solution.py:201
  49.1 10.9 %collective-permute-done.4 = bf16[128,2048]{1,0:T(8,128)(2,1)S(1)} collective-permute-done((bf16[128,2048]{1,0:T(8,128)(2,1)}, bf16[128,2048]{1,0:T(8,128)(2,1)S(1)}, u32[]{:S(2)}, u32[]{:S(2)}) %collective-permute-start.4) | collective-permute-done | bytes 524320 | tf_op jit(solution)/shard_map/ppermute | solution.py:219
  60.0 1.2 %collective-permute-start.7 = (bf16[128,2048]{1,0:T(8,128)(2,1)S(1)}, bf16[128,2048]{1,0:T(8,128)(2,1)}, u32[]{:S(2)}, u32[]{:S(2)}) collective-permute-start(bf16[128,2048]{1,0:T(8,128)(2,1)S(1)} %collective-permute-done.4), channel_id=1, source_target_pairs={{4,0},{8,4},{12,8},{14,12},{10,14},{6,10},{2,6},{0,2},{5,1},{9,5},... | collective-permute-start | bytes 1572872 | tf_op jit(solution)/shard_map/ppermute | solution.py:219
  61.2 0.0 collective-permute-done.3
  61.2 0.3 collective-permute-start.6
  61.4 1.3 %add_convert_fusion = bf16[128,2048]{1,0:T(8,128)(2,1)S(1)} fusion(f32[128,2048]{1,0:T(8,128)} %get-tuple-element.23, f32[128,2048]{1,0:T(8,128)S(1)} %collective-permute-done.2), kind=kLoop, calls=%fused_computation.13 | loop fusion | flops 524288 | bytes 2621440 | tf_op jit(solution)/shard_map/convert_element_type | solution.py:226
  62.8 0.1 copy.10
  63.0 0.1 copy.8
  63.1 0.9 fusion.7
  64.0 5.4 %all-to-all-start.1 = ((bf16[8,128,256]{2,1,0:T(8,128)(2,1)}), bf16[8,128,256]{2,1,0:T(8,128)(2,1)S(1)}, u32[]{:S(2)}, u32[]{:S(2)}) async-start(bf16[8,128,256]{2,1,0:T(8,128)(2,1)} %fusion.7), calls=%async_computation.1 | async-start | bytes 1048576 | tf_op jit(solution)/shard_map/all_to_all | solution.py:231
  69.4 4.1 %collective-permute-done.6 = bf16[128,2048]{1,0:T(8,128)(2,1)} collective-permute-done((bf16[128,2048]{1,0:T(8,128)(2,1)S(1)}, bf16[128,2048]{1,0:T(8,128)(2,1)}, u32[]{:S(2)}, u32[]{:S(2)}) %collective-permute-start.6) | collective-permute-done | bytes 524320 | tf_op jit(solution)/shard_map/ppermute | solution.py:218
  73.5 0.3 collective-permute-start.8
  73.8 1.2 %collective-permute-start.9 = (bf16[128,2048]{1,0:T(8,128)(2,1)}, bf16[128,2048]{1,0:T(8,128)(2,1)S(1)}, u32[]{:S(2)}, u32[]{:S(2)}) collective-permute-start(bf16[128,2048]{1,0:T(8,128)(2,1)} %collective-permute-done.7), channel_id=1, source_target_pairs={{4,0},{8,4},{12,8},{14,12},{10,14},{6,10},{2,6},{0,2},{5,1},{9,5},... | collective-permute-start | bytes 1572872 | tf_op jit(solution)/shard_map/ppermute | solution.py:219
  75.0 1.3 %collective-permute-start.5 = (bf16[8,128,256]{2,1,0:T(8,128)(2,1)S(1)}, bf16[8,128,256]{2,1,0:T(8,128)(2,1)}, u32[]{:S(2)}, u32[]{:S(2)}) collective-permute-start(bf16[8,128,256]{2,1,0:T(8,128)(2,1)S(1)} %all-to-all-done), channel_id=1, source_target_pairs={{0,16},{1,17},{2,18},{3,19},{4,20},{5,21},{6,22},{7,23},{8,24},{9,... | collective-permute-start | bytes 1572872 | tf_op jit(solution)/shard_map/ppermute | solution.py:204
  76.3 19.6 %collective-permute-done.8 = bf16[128,2048]{1,0:T(8,128)(2,1)S(1)} collective-permute-done((bf16[128,2048]{1,0:T(8,128)(2,1)}, bf16[128,2048]{1,0:T(8,128)(2,1)S(1)}, u32[]{:S(2)}, u32[]{:S(2)}) %collective-permute-start.8) | collective-permute-done | bytes 524320 | tf_op jit(solution)/shard_map/ppermute | solution.py:218
  95.9 0.7 slice.28
  96.6 0.7 slice.29
  97.4 1.5 %collective-permute-start.12 = (bf16[64,2048]{1,0:T(8,128)(2,1)}, bf16[64,2048]{1,0:T(8,128)(2,1)S(1)}, u32[]{:S(2)}, u32[]{:S(2)}) collective-permute-start(bf16[64,2048]{1,0:T(8,128)(2,1)} %slice.29), channel_id=1, source_target_pairs={{4,0},{8,4},{12,8},{14,12},{10,14},{6,10},{2,6},{0,2},{5,1},{9,5},... | collective-permute-start | bytes 786440 | tf_op jit(solution)/shard_map/ppermute | solution.py:224
  98.8 0.1 convert_reduce_fusion
  98.9 1.4 %collective-permute-start.10 = (f32[8,2048]{1,0:T(8,128)S(1)}, f32[8,2048]{1,0:T(8,128)S(1)}, u32[]{:S(2)}, u32[]{:S(2)}) collective-permute-start(f32[8,2048]{1,0:T(8,128)S(1)} %bitcast.80), channel_id=1, source_target_pairs={{16,0},{17,1},{18,2},{19,3},{20,4},{21,5},{22,6},{23,7},{24,8},{25... | collective-permute-start | bytes 196616 | tf_op jit(solution)/shard_map/ppermute | solution.py:237
  100.4 1.1 broadcast_select_fusion.1
  101.5 0.5 fusion.17
  102.0 0.5 fusion.15
  102.5 0.1 copy-done.6
  102.6 0.5 fusion.4
  103.1 1.5 %fusion.12 = f32[256,2048]{1,0:T(8,128)S(1)} fusion(bf16[128,2048]{1,0:T(8,128)(2,1)} %collective-permute-done.7, bf16[8,128,256]{2,1,0:T(8,128)(2,1)S(1)} %broadcast_select_fusion.1, s32[]{:T(128)S(6)} %select_n.173), kind=kOutput, calls=%fused_computation.25 | convolution fusion | flops 134217728 | bytes 2686980 | tf_op jit(solution)/shard_map/dot_general | solution.py:15
  104.6 0.5 fusion.9
  105.0 1.5 %fusion.3 = f32[256,2048]{1,0:T(8,128)S(1)} fusion(f32[256,2048]{1,0:T(8,128)S(1)} %fusion.12, f32[256,2048]{1,0:T(8,128)S(1)} %fusion.4, bf16[128,2048]{1,0:T(8,128)(2,1)} %collective-permute-done.6, bf16[8,128,256]{2,1,0:T(8,128)(2,1)S(1)} %broadcast_select_fusion.1, s32[]{:T(128)S(6)} %select_n.171), kind=kOutput, calls=%fused_computation.5 | convolution fusion | flops 135266304 | bytes 6881284 | tf_op jit(solution)/shard_map/dot_general | solution.py:15
  106.6 0.6 broadcast_select_fusion.2
  107.2 0.5 fusion.29
  107.7 0.5 fusion.27
  108.1 0.6 fusion.2
  108.7 1.1 dynamic-slice_bitcast_fusion
  109.8 2.9 %collective-permute-start.13 = (f32[128,2048]{1,0:T(8,128)}, f32[128,2048]{1,0:T(8,128)}, u32[]{:S(2)}, u32[]{:S(2)}) collective-permute-start(f32[128,2048]{1,0:T(8,128)} %dynamic-slice_bitcast_fusion), channel_id=1, source_target_pairs={{0,1},{1,0},{2,3},{3,2},{4,5},{5,4},{6,7},{7,6},{8,9},{9,8},{10,11... | collective-permute-start | bytes 3145736 | tf_op jit(solution)/shard_map/ppermute | solution.py:19
  112.7 0.8 broadcast_select_fusion
  113.5 1.8 %collective-permute-done.13 = f32[128,2048]{1,0:T(8,128)} collective-permute-done((f32[128,2048]{1,0:T(8,128)}, f32[128,2048]{1,0:T(8,128)}, u32[]{:S(2)}, u32[]{:S(2)}) %collective-permute-start.13) | collective-permute-done | bytes 1048608 | tf_op jit(solution)/shard_map/ppermute | solution.py:19
  115.3 2.3 %fusion.6 = f32[1,128,2048]{2,1,0:T(8,128)} fusion(f32[128,2048]{1,0:T(8,128)} %collective-permute-done.13, f32[2,128,2048]{2,1,0:T(8,128)S(1)} %bitcast.72, s32[]{:T(128)S(6)} %select_n.182), kind=kLoop, calls=%fused_computation.10 | loop fusion | flops 524288 | bytes 3145732 | tf_op jit(solution)/shard_map/broadcast_in_dim | solution.py:250
  (30 shorter events, 0.1 us)
Async XLA Ops:
  2.0 16.7 %copy-start.7 = (s32[128]{0:T(128)S(1)}, s32[128]{0:T(128)}, u32[]{:S(2)}) copy-start(s32[128]{0:T(128)} %param.7) | copy-start | bytes 1540
  11.7 19.9 %all-to-all-start = ((bf16[8,128,256]{2,1,0:T(8,128)(2,1)}), bf16[8,128,256]{2,1,0:T(8,128)(2,1)S(1)}, u32[]{:S(2)}, u32[]{:S(2)}) async-start(bf16[8,128,256]{2,1,0:T(8,128)(2,1)} %get-tuple-element.19), calls=%async_computation | async-start | bytes 1048576 | tf_op jit(solution)/shard_map/all_to_all | solution.py:195
  17.4 14.3 %collective-permute-start = (bf16[2,128,1024]{2,1,0:T(8,128)(2,1)}, bf16[2,128,1024]{2,1,0:T(8,128)(2,1)S(1)}, u32[]{:S(2)}, u32[]{:S(2)}) collective-permute-start(bf16[2,128,1024]{2,1,0:T(8,128)(2,1)} %get-tuple-element.18), channel_id=1, source_target_pairs={{0,16},{1,17},{2,18},{3,19},{4,20},{5,21},{6,22},{7,23},{8,24},{9,... | collective-permute-start | bytes 1572872 | tf_op jit(solution)/shard_map/ppermute | solution.py:194
  31.7 0.8 copy-start
  44.0 17.4 %collective-permute-start.2 = (f32[128,2048]{1,0:T(8,128)}, f32[128,2048]{1,0:T(8,128)S(1)}, u32[]{:S(2)}, u32[]{:S(2)}) collective-permute-start(f32[128,2048]{1,0:T(8,128)} %get-tuple-element.24), channel_id=1, source_target_pairs={{0,1},{1,0},{2,3},{3,2},{4,5},{5,4},{6,7},{7,6},{8,9},{9,8},{10,11... | collective-permute-start | bytes 3145736 | tf_op jit(solution)/shard_map/ppermute | solution.py:19
  46.3 13.7 %collective-permute-start.4 = (bf16[128,2048]{1,0:T(8,128)(2,1)}, bf16[128,2048]{1,0:T(8,128)(2,1)S(1)}, u32[]{:S(2)}, u32[]{:S(2)}) collective-permute-start(bf16[128,2048]{1,0:T(8,128)(2,1)} %get-tuple-element.25), channel_id=1, source_target_pairs={{4,0},{8,4},{12,8},{14,12},{10,14},{6,10},{2,6},{0,2},{5,1},{9,5},... | collective-permute-start | bytes 1572872 | tf_op jit(solution)/shard_map/ppermute | solution.py:219
  47.4 13.7 %collective-permute-start.3 = (bf16[128,2048]{1,0:T(8,128)(2,1)}, bf16[128,2048]{1,0:T(8,128)(2,1)S(1)}, u32[]{:S(2)}, u32[]{:S(2)}) collective-permute-start(bf16[128,2048]{1,0:T(8,128)(2,1)} %get-tuple-element.25), channel_id=1, source_target_pairs={{0,4},{4,8},{8,12},{12,14},{14,10},{10,6},{6,2},{2,0},{1,5},{5,9},... | collective-permute-start | bytes 1572872 | tf_op jit(solution)/shard_map/ppermute | solution.py:218
  47.7 15.3 %collective-permute-start.1 = (bf16[128,2048]{1,0:T(8,128)(2,1)}, bf16[128,2048]{1,0:T(8,128)(2,1)S(1)}, u32[]{:S(2)}, u32[]{:S(2)}) collective-permute-start(bf16[128,2048]{1,0:T(8,128)(2,1)} %get-tuple-element.22), channel_id=1, source_target_pairs={{16,0},{17,1},{18,2},{19,3},{20,4},{21,5},{22,6},{23,7},{24,8},{25... | collective-permute-start | bytes 1572872 | tf_op jit(solution)/shard_map/ppermute | solution.py:201
  60.0 3.0 %copy-start.2 = (bf16[128,2048]{1,0:T(8,128)(2,1)}, bf16[128,2048]{1,0:T(8,128)(2,1)S(1)}, u32[]{:S(2)}) copy-start(bf16[128,2048]{1,0:T(8,128)(2,1)S(1)} %collective-permute-done.4) | copy-start | bytes 1572868
  60.0 13.9 %collective-permute-start.7 = (bf16[128,2048]{1,0:T(8,128)(2,1)S(1)}, bf16[128,2048]{1,0:T(8,128)(2,1)}, u32[]{:S(2)}, u32[]{:S(2)}) collective-permute-start(bf16[128,2048]{1,0:T(8,128)(2,1)S(1)} %collective-permute-done.4), channel_id=1, source_target_pairs={{4,0},{8,4},{12,8},{14,12},{10,14},{6,10},{2,6},{0,2},{5,1},{9,5},... | collective-permute-start | bytes 1572872 | tf_op jit(solution)/shard_map/ppermute | solution.py:219
  61.2 8.2 %copy-start.4 = (bf16[128,2048]{1,0:T(8,128)(2,1)}, bf16[128,2048]{1,0:T(8,128)(2,1)S(1)}, u32[]{:S(2)}) copy-start(bf16[128,2048]{1,0:T(8,128)(2,1)S(1)} %collective-permute-done.3) | copy-start | bytes 1572868
  61.2 12.4 %collective-permute-start.6 = (bf16[128,2048]{1,0:T(8,128)(2,1)S(1)}, bf16[128,2048]{1,0:T(8,128)(2,1)}, u32[]{:S(2)}, u32[]{:S(2)}) collective-permute-start(bf16[128,2048]{1,0:T(8,128)(2,1)S(1)} %collective-permute-done.3), channel_id=1, source_target_pairs={{0,4},{4,8},{8,12},{12,14},{14,10},{10,6},{6,2},{2,0},{1,5},{5,9},... | collective-permute-start | bytes 1572872 | tf_op jit(solution)/shard_map/ppermute | solution.py:218
  64.0 34.9 %all-to-all-start.1 = ((bf16[8,128,256]{2,1,0:T(8,128)(2,1)}), bf16[8,128,256]{2,1,0:T(8,128)(2,1)S(1)}, u32[]{:S(2)}, u32[]{:S(2)}) async-start(bf16[8,128,256]{2,1,0:T(8,128)(2,1)} %fusion.7), calls=%async_computation.1 | async-start | bytes 1048576 | tf_op jit(solution)/shard_map/all_to_all | solution.py:231
  73.5 22.4 %collective-permute-start.8 = (bf16[128,2048]{1,0:T(8,128)(2,1)}, bf16[128,2048]{1,0:T(8,128)(2,1)S(1)}, u32[]{:S(2)}, u32[]{:S(2)}) collective-permute-start(bf16[128,2048]{1,0:T(8,128)(2,1)} %collective-permute-done.6), channel_id=1, source_target_pairs={{0,4},{4,8},{8,12},{12,14},{14,10},{10,6},{6,2},{2,0},{1,5},{5,9},... | collective-permute-start | bytes 1572872 | tf_op jit(solution)/shard_map/ppermute | solution.py:218
  73.8 22.8 %collective-permute-start.9 = (bf16[128,2048]{1,0:T(8,128)(2,1)}, bf16[128,2048]{1,0:T(8,128)(2,1)S(1)}, u32[]{:S(2)}, u32[]{:S(2)}) collective-permute-start(bf16[128,2048]{1,0:T(8,128)(2,1)} %collective-permute-done.7), channel_id=1, source_target_pairs={{4,0},{8,4},{12,8},{14,12},{10,14},{6,10},{2,6},{0,2},{5,1},{9,5},... | collective-permute-start | bytes 1572872 | tf_op jit(solution)/shard_map/ppermute | solution.py:219
  75.0 25.4 %collective-permute-start.5 = (bf16[8,128,256]{2,1,0:T(8,128)(2,1)S(1)}, bf16[8,128,256]{2,1,0:T(8,128)(2,1)}, u32[]{:S(2)}, u32[]{:S(2)}) collective-permute-start(bf16[8,128,256]{2,1,0:T(8,128)(2,1)S(1)} %all-to-all-done), channel_id=1, source_target_pairs={{0,16},{1,17},{2,18},{3,19},{4,20},{5,21},{6,22},{7,23},{8,24},{9,... | collective-permute-start | bytes 1572872 | tf_op jit(solution)/shard_map/ppermute | solution.py:204
  96.6 10.6 %collective-permute-start.11 = (bf16[64,2048]{1,0:T(8,128)(2,1)}, bf16[64,2048]{1,0:T(8,128)(2,1)S(1)}, u32[]{:S(2)}, u32[]{:S(2)}) collective-permute-start(bf16[64,2048]{1,0:T(8,128)(2,1)} %slice.28), channel_id=1, source_target_pairs={{0,4},{4,8},{8,12},{12,14},{14,10},{10,6},{6,2},{2,0},{1,5},{5,9},... | collective-permute-start | bytes 786440 | tf_op jit(solution)/shard_map/ppermute | solution.py:223
  97.4 10.3 %collective-permute-start.12 = (bf16[64,2048]{1,0:T(8,128)(2,1)}, bf16[64,2048]{1,0:T(8,128)(2,1)S(1)}, u32[]{:S(2)}, u32[]{:S(2)}) collective-permute-start(bf16[64,2048]{1,0:T(8,128)(2,1)} %slice.29), channel_id=1, source_target_pairs={{4,0},{8,4},{12,8},{14,12},{10,14},{6,10},{2,6},{0,2},{5,1},{9,5},... | collective-permute-start | bytes 786440 | tf_op jit(solution)/shard_map/ppermute | solution.py:224
  98.8 2.7 %copy-start.5 = (bf16[128,2048]{1,0:T(8,128)(2,1)S(1)}, bf16[128,2048]{1,0:T(8,128)(2,1)}, u32[]{:S(2)}) copy-start(bf16[128,2048]{1,0:T(8,128)(2,1)} %copy-done.4) | copy-start | bytes 1572868
  98.9 3.1 %copy-start.3 = (bf16[128,2048]{1,0:T(8,128)(2,1)S(1)}, bf16[128,2048]{1,0:T(8,128)(2,1)}, u32[]{:S(2)}) copy-start(bf16[128,2048]{1,0:T(8,128)(2,1)} %copy-done.2) | copy-start | bytes 1572868
  98.9 7.6 %collective-permute-start.10 = (f32[8,2048]{1,0:T(8,128)S(1)}, f32[8,2048]{1,0:T(8,128)S(1)}, u32[]{:S(2)}, u32[]{:S(2)}) collective-permute-start(f32[8,2048]{1,0:T(8,128)S(1)} %bitcast.80), channel_id=1, source_target_pairs={{16,0},{17,1},{18,2},{19,3},{20,4},{21,5},{22,6},{23,7},{24,8},{25... | collective-permute-start | bytes 196616 | tf_op jit(solution)/shard_map/ppermute | solution.py:237
  101.5 1.0 copy-start.6
  108.7 4.0 %copy-start.1 = (bf16[128,2048]{1,0:T(8,128)(2,1)S(1)}, bf16[128,2048]{1,0:T(8,128)(2,1)}, u32[]{:S(2)}) copy-start(bf16[128,2048]{1,0:T(8,128)(2,1)} %get-tuple-element.22) | copy-start | bytes 1572868
  109.8 5.5 %collective-permute-start.13 = (f32[128,2048]{1,0:T(8,128)}, f32[128,2048]{1,0:T(8,128)}, u32[]{:S(2)}, u32[]{:S(2)}) collective-permute-start(f32[128,2048]{1,0:T(8,128)} %dynamic-slice_bitcast_fusion), channel_id=1, source_target_pairs={{0,1},{1,0},{2,3},{3,2},{4,5},{5,4},{6,7},{7,6},{8,9},{9,8},{10,11... | collective-permute-start | bytes 3145736 | tf_op jit(solution)/shard_map/ppermute | solution.py:19

commit v2 on v1

--- a/solution.py
+++ b/solution.py
@@ -9,6 +9,7 @@
 F32 = jnp.float32
 BF16 = jnp.bfloat16
 TILE = 256
+GRANT = 16 * 1024 * 1024
 
 
 def dot(a, b, ca, cb):
@@ -27,25 +28,15 @@
     return pl.ds(pl.multiple_of(base + step * TILE, TILE), TILE)
 
 
-def lead_body(rows, weight, onehot, table, query, mixed, rel, held, sems):
+def lead_body(rows, weight, onehot, table, query, mixed, rel):
     half = weight.shape[0] // 2
     steps = half // TILE
-
-    def load(step, side):
-        piece = at(step, side * half)
-        return pltpu.make_async_copy(weight.at[piece], held.at[piece], sems.at[2 * step + side])
-
-    for step in range(steps):
-        for side in range(2):
-            load(step, side).start()
     for step in range(steps):
         span = pl.ds(step * TILE, TILE)
         r_re = dot(onehot[...], table[:, at(step)], 1, 0)
         r_im = dot(onehot[...], table[:, at(step, half)], 1, 0)
-        load(step, 0).wait()
-        q_re = dot(rows[...], held[at(step)], 1, 1).astype(BF16)
-        load(step, 1).wait()
-        q_im = dot(rows[...], held[at(step, half)], 1, 1).astype(BF16)
+        q_re = dot(rows[...], weight[at(step)], 1, 1).astype(BF16)
+        q_im = dot(rows[...], weight[at(step, half)], 1, 1).astype(BF16)
         query[0, :, span], query[1, :, span] = q_re, q_im
         rel[0, :, span], rel[1, :, span] = r_re.astype(BF16), r_im.astype(BF16)
         z_re, z_im = mix(q_re.astype(F32), q_im.astype(F32), r_re, r_im)
@@ -67,13 +58,9 @@
     query, mixed, rel = pl.pallas_call(
         lead_body,
         out_shape=(pair, apart, pair),
-        in_specs=[vmem, pl.BlockSpec(memory_space=pltpu.HBM), vmem, vmem],
+        in_specs=[vmem] * 4,
         out_specs=(vmem,) * 3,
-        scratch_shapes=[
-            pltpu.VMEM((width, hidden), BF16),
-            pltpu.SemaphoreType.DMA((width // TILE,)),
-        ],
-        compiler_params=pltpu.CompilerParams(vmem_limit_bytes=56 * 1024 * 1024),
+        compiler_params=pltpu.CompilerParams(vmem_limit_bytes=GRANT),
         cost_estimate=pl.CostEstimate(
             flops=2 * rows_dev * width * (hidden + count_rel), bytes_accessed=2 * width * hidden, transcendentals=0
         ),
@@ -83,18 +70,11 @@
     return query, mixed, rel
 
 
-def trail_body(first, query, rows, weight, rel, onehot, right, query_grad, give, keep, mixed, hidden, held, sems):
+def trail_body(first, query, rows, weight, rel, onehot, right, query_grad, give, keep, mixed, hidden):
     width = weight.shape[0]
     half = width // 2
     is_first = first[0] == 1
     owned = give.shape[0]
-    tiles = weight.shape[1] // TILE
-
-    def load(step):
-        return pltpu.make_async_copy(weight.at[:, at(step)], held.at[:, at(step)], sems.at[step])
-
-    for step in range(tiles):
-        load(step).start()
 
     def make_mixed(step, carry):
         mixed[:, at(step)], mixed[:, at(step, half)] = mix(
@@ -106,8 +86,7 @@
     lax.fori_loop(0, half // TILE, make_mixed, 0)
 
     def make_hidden(step, carry):
-        load(step).wait()
-        pre = dot(mixed[...], held[:, at(step)], 1, 0)
+        pre = dot(mixed[...], weight[:, at(step)], 1, 0)
         sig = jax.nn.sigmoid(pre)
         cot = rows[:, at(step)]
         grad = (cot.astype(F32) * (sig * (1.0 + pre * (1.0 - sig)))).astype(BF16)
@@ -115,11 +94,11 @@
         right[:, at(step)] = jnp.where(is_first, cot, grad)
         return carry
 
-    lax.fori_loop(0, tiles, make_hidden, 0)
+    lax.fori_loop(0, weight.shape[1] // TILE, make_hidden, 0)
 
     def make_query(step, carry):
-        gz_re = dot(hidden[...], held[at(step), :], 1, 1)
-        gz_im = dot(hidden[...], held[at(step, half), :], 1, 1)
+        gz_re = dot(hidden[...], weight[at(step), :], 1, 1)
+        gz_im = dot(hidden[...], weight[at(step, half), :], 1, 1)
         r_re, r_im = rel[0, :, at(step)].astype(F32), rel[1, :, at(step)].astype(F32)
         query_grad[:, at(step)] = (gz_re * r_re + gz_im * r_im).astype(BF16)
         query_grad[:, at(step, half)] = (gz_im * r_re - gz_re * r_im).astype(BF16)
@@ -149,17 +128,12 @@
             jax.ShapeDtypeStruct((count_rel // 2, width), F32),
             jax.ShapeDtypeStruct((count_rel // 2, width), F32),
         ),
-        in_specs=[pl.BlockSpec(memory_space=pltpu.SMEM), vmem, vmem, pl.BlockSpec(memory_space=pltpu.HBM), vmem, vmem],
+        in_specs=[pl.BlockSpec(memory_space=pltpu.SMEM)] + [vmem] * 5,
         out_specs=(vmem,) * 4,
-        scratch_shapes=[
-            pltpu.VMEM((rows_dev, width), BF16),
-            pltpu.VMEM((rows_dev, hidden), BF16),
-            pltpu.VMEM((width, hidden), BF16),
-            pltpu.SemaphoreType.DMA((hidden // TILE,)),
-        ],
-        compiler_params=pltpu.CompilerParams(vmem_limit_bytes=56 * 1024 * 1024),
+        scratch_shapes=[pltpu.VMEM((rows_dev, width), BF16), pltpu.VMEM((rows_dev, hidden), BF16)],
+        compiler_params=pltpu.CompilerParams(vmem_limit_bytes=GRANT),
         cost_estimate=pl.CostEstimate(
-            flops=flops, bytes_accessed=2 * width * hidden, transcendentals=rows_dev * hidden
+            flops=flops, bytes_accessed=4 * width * hidden, transcendentals=rows_dev * hidden
         ),
     )(first, query, rows, weight, rel, onehot)
 
@@ -193,14 +167,13 @@
     own_query, own_mixed, rel = lead(rows, weight, onehot, relation_table, chips)
     query = lax.ppermute(own_query, "hop", [(0, 1)])
     z_cols = lax.all_to_all(own_mixed, "chip", 0, 0, tiled=True)
-    query, z_cols = lax.optimization_barrier((query, z_cols))
 
     right, grad_query, rel_give, rel_keep = trail(
         first.astype(jnp.int32).reshape(1), query, rows, weight, rel, onehot_t
     )
     query_back = lax.ppermute(grad_query, "hop", [(1, 0)])
     query_grad = jnp.where(first, query_back, grad_query)
-    z_cols, _ = lax.optimization_barrier((z_cols, grad_query))
+    z_cols, right = lax.optimization_barrier((z_cols, right))
     z_cols = lax.ppermute(z_cols, "hop", [(0, 1)])
     rel_got = swap_core(rel_give)
 
@@ -213,21 +186,22 @@
     up = [(ring[i], ring[(i + 1) % chips]) for i in range(chips)]
     down = [(b, a) for a, b in up]
     blocks = [(right, 0, 0)]
-    fwd = bwd = right
+    mid = rows_dev // 2
+    fwd = bwd = [right[:mid], right[mid:]]
     for s in range(1, (chips + 1) // 2):
-        fwd = lax.ppermute(fwd, "chip", up)
-        bwd = lax.ppermute(bwd, "chip", down)
-        blocks += [(fwd, chips - s, 0), (bwd, s, 0)]
+        fwd = [lax.ppermute(part, "chip", up) for part in fwd]
+        bwd = [lax.ppermute(part, "chip", down) for part in bwd]
+        for base, ahead, behind in zip((0, mid), fwd, bwd):
+            blocks += [(ahead, chips - s, base), (behind, s, base)]
     if chips % 2 == 0:
-        mid = rows_dev // 2
-        blocks.append((lax.ppermute(fwd[:mid], "chip", up), chips // 2, 0))
-        blocks.append((lax.ppermute(bwd[mid:], "chip", down), chips // 2, mid))
+        blocks.append((lax.ppermute(fwd[0], "chip", up), chips // 2, 0))
+        blocks.append((lax.ppermute(bwd[1], "chip", down), chips // 2, mid))
 
     rel_sent = (rel_keep + rel_got).astype(BF16).reshape(chips, 2 * owned, chips, cols)
     rel_sent = rel_sent.transpose(0, 2, 1, 3).reshape(chips, 2 * owned * chips, cols)
     if rel_sent.shape[1] == rows_dev:
         shared = jnp.where(first, columns(query_back), rel_sent)
-        shared, _ = lax.optimization_barrier((shared, (blocks[1][0], blocks[2][0])))
+        shared, _ = lax.optimization_barrier((shared, tuple(block for block, _, _ in blocks[1:5])))
         query_cols = rel_rows = lax.all_to_all(shared, "chip", 0, 0, tiled=True)
     else:
         query_cols = lax.all_to_all(columns(query_back), "chip", 0, 0, tiled=True)

time: 118 us -> 122 us (1.034)
  the two profiles are of different devices: /device:TPU:15 before, /device:TPU:9 now
where the time goes in v2:
time: 122 us; the launch traced here: 120 us
  waiting for transfers between devices  37.6 us (31%)
  starting transfers between devices  35.1 us (29%)
  matrix products  15.8 us (13%)
  Pallas kernels  12.6 us (10%)
  local copies, waits for them, and re-layouts  10.4 us (9%)
  other arithmetic  7.02 us (6%)
    ppermute x6, waiting for transfers between devices, local(): bwd = [lax.ppermute(part, 'chip', down) for part in bwd]  21.2 us
    dot_general x15, matrix products, dot(): lax.dot_general(a, b, (((ca,), (cb,)), ((), ())), preferred_element_type=...  15.8 us
    ppermute x1, waiting for transfers between devices, local(): query_back = lax.ppermute(grad_query, 'hop', [(1, 0)])  9.86 us
    unnamed x17, local copies, waits for them, and re-layouts  9.16 us
    pallas_call x1, Pallas kernels, trail(): pl.pallas_call(trail_body, out_shape=(jax.ShapeDtypeStruct((rows_dev, hid...  8.75 us
    ppermute x6, starting transfers between devices, local(): fwd = [lax.ppermute(part, 'chip', up) for part in fwd]  8.48 us
    all_to_all x1, starting transfers between devices, local(): z_cols = lax.all_to_all(own_mixed, 'chip', 0, 0, tiled=True)  5.73 us
    all_to_all x1, starting transfers between devices, local(): query_cols = rel_rows = lax.all_to_all(shared, 'chip', 0, 0, tiled=True)  5.73 us
  transfers between devices with their start and end apart: 22, of which 6 were waited for; matrix products, arithmetic and copies ran while one was open for 16% of the time, Pallas kernels for 7%

profile of v2, /device:TPU:9, one launch (start us, length us, event | category | flops | bytes accessed | tf_op | source)
XLA Modules:
  0.0 119.5 jit_solution(17173359592355430788)
XLA Ops:
  0.6 0.7 fusion.13.onehot
  1.4 3.4 %copy-done = bf16[1,2048,2048]{2,1,0:T(8,128)(2,1)S(1)} copy-done((bf16[1,2048,2048]{2,1,0:T(8,128)(2,1)S(1)}, bf16[1,2048,2048]{2,1,0:T(8,128)(2,1)}, u32[]{:S(2)}) %copy-start) | copy-done | bytes 8388632
  4.8 1.0 copy-done.2
  5.8 1.2 %copy-done.4 = bf16[256,2048]{1,0:T(8,128)(2,1)S(1)} copy-done((bf16[256,2048]{1,0:T(8,128)(2,1)S(1)}, bf16[256,2048]{1,0:T(8,128)(2,1)}, u32[]{:S(2)}) %copy-start.4) | copy-done | bytes 1048600
  7.0 3.9 %shard_map.67 = (bf16[2,128,1024]{2,1,0:T(8,128)(2,1)S(1)}, bf16[8,128,256]{2,1,0:T(8,128)(2,1)}, bf16[2,128,1024]{2,1,0:T(8,128)(2,1)S(1)}) custom-call(bf16[128,2048]{1,0:T(8,128)(2,1)S(1)} %bitcast.95, bf16[2048,2048]{1,0:T(8,128)(2,1)S(1)} %bitcast.93, bf16[128,256]{1,0:T(8,128)(2,1)S(1)} %fusion.13.onehot, bf16[256,2048]{1,0:T(8,128)(2,1)S(1)} %copy-done.4), custom_call_target="tpu_custom_call" | custom-call | flops 1207959552 | bytes 8388608 | tf_op jit(solution)/shard_map/pallas_call | solution.py:58
  10.9 3.1 %collective-permute-start = (bf16[2,128,1024]{2,1,0:T(8,128)(2,1)S(1)}, bf16[2,128,1024]{2,1,0:T(8,128)(2,1)S(1)}, u32[]{:S(2)}, u32[]{:S(2)}) collective-permute-start(bf16[2,128,1024]{2,1,0:T(8,128)(2,1)S(1)} %get-tuple-element.17), channel_id=1, source_target_pairs={{0,16},{1,17},{2,18},{3,19},{4,20},{5,21},{6,22},{7,23},{8,24},{9,... | collective-permute-start | bytes 1572872 | tf_op jit(solution)/shard_map/ppermute | solution.py:168
  14.1 5.7 %all-to-all-start = ((bf16[8,128,256]{2,1,0:T(8,128)(2,1)}), bf16[8,128,256]{2,1,0:T(8,128)(2,1)}, u32[]{:S(2)}, u32[]{:S(2)}) async-start(bf16[8,128,256]{2,1,0:T(8,128)(2,1)} %get-tuple-element.22), calls=%async_computation | async-start | bytes 1048576 | tf_op jit(solution)/shard_map/all_to_all | solution.py:169
  19.9 4.7 %collective-permute-done.query = bf16[2,128,1024]{2,1,0:T(8,128)(2,1)S(1)} collective-permute-done((bf16[2,128,1024]{2,1,0:T(8,128)(2,1)S(1)}, bf16[2,128,1024]{2,1,0:T(8,128)(2,1)S(1)}, u32[]{:S(2)}, u32[]{:S(2)}) %collective-permute-start) | collective-permute-done | bytes 524320 | tf_op jit(solution)/shard_map/ppermute | solution.py:168
  24.6 3.4 %copy-done.1 = bf16[1,2048,2048]{2,1,0:T(8,128)(2,1)S(1)} copy-done((bf16[1,2048,2048]{2,1,0:T(8,128)(2,1)S(1)}, bf16[1,2048,2048]{2,1,0:T(8,128)(2,1)}, u32[]{:S(2)}) %copy-start.1) | copy-done | bytes 8388632
  28.0 8.8 %shard_map.68 = (bf16[128,2048]{1,0:T(8,128)(2,1)S(1)}, bf16[128,2048]{1,0:T(8,128)(2,1)}, f32[128,2048]{1,0:T(8,128)}, f32[128,2048]{1,0:T(8,128)S(1)}) custom-call(s32[1]{0:T(128)} %bitcast.first, bf16[2,128,1024]{2,1,0:T(8,128)(2,1)S(1)} %collective-permute-done.query, bf16[128,2048]{1,0:T(8,128)(2,1)S(1)} %bitcast.96, bf16[2048,2048]{1,0:T(8,128)(2,1)S(1)} %bitcast.94, ...), custom_call_target="tpu_custom_call" | custom-call | flops 2415919104 | bytes 16777216 | tf_op jit(solution)/shard_map/pallas_call | solution.py:123
  36.7 1.5 %collective-permute-start.2 = (f32[128,2048]{1,0:T(8,128)}, f32[128,2048]{1,0:T(8,128)}, u32[]{:S(2)}, u32[]{:S(2)}) collective-permute-start(f32[128,2048]{1,0:T(8,128)} %get-tuple-element.21), channel_id=1, source_target_pairs={{0,1},{1,0},{2,3},{3,2},{4,5},{5,4},{6,7},{7,6},{8,9},{9,8},{10,11... | collective-permute-start | bytes 3145736 | tf_op jit(solution)/shard_map/ppermute | solution.py:20
  38.3 1.3 %collective-permute-start.1 = (bf16[128,2048]{1,0:T(8,128)(2,1)}, bf16[128,2048]{1,0:T(8,128)(2,1)S(1)}, u32[]{:S(2)}, u32[]{:S(2)}) collective-permute-start(bf16[128,2048]{1,0:T(8,128)(2,1)} %get-tuple-element.19), channel_id=1, source_target_pairs={{16,0},{17,1},{18,2},{19,3},{20,4},{21,5},{22,6},{23,7},{24,8},{25... | collective-permute-start | bytes 1572872 | tf_op jit(solution)/shard_map/ppermute | solution.py:174
  39.6 1.4 %collective-permute-start.3 = (bf16[64,2048]{1,0:T(8,128)(2,1)S(1)}, bf16[64,2048]{1,0:T(8,128)(2,1)S(1)}, u32[]{:S(2)}, u32[]{:S(2)}) collective-permute-start(bf16[64,2048]{1,0:T(8,128)(2,1)S(1)} %get-tuple-element.31), channel_id=1, source_target_pairs={{0,4},{4,8},{8,12},{12,14},{14,10},{10,6},{6,2},{2,0},{1,5},{5,9},... | collective-permute-start | bytes 786440 | tf_op jit(solution)/shard_map/ppermute | solution.py:192
  41.2 1.3 %collective-permute-start.5 = (bf16[64,2048]{1,0:T(8,128)(2,1)S(1)}, bf16[64,2048]{1,0:T(8,128)(2,1)S(1)}, u32[]{:S(2)}, u32[]{:S(2)}) collective-permute-start(bf16[64,2048]{1,0:T(8,128)(2,1)S(1)} %get-tuple-element.32), channel_id=1, source_target_pairs={{0,4},{4,8},{8,12},{12,14},{14,10},{10,6},{6,2},{2,0},{1,5},{5,9},... | collective-permute-start | bytes 786440 | tf_op jit(solution)/shard_map/ppermute | solution.py:192
  42.6 1.3 %add_convert_fusion = bf16[128,2048]{1,0:T(8,128)(2,1)S(1)} fusion(f32[128,2048]{1,0:T(8,128)S(1)} %get-tuple-element.20, f32[128,2048]{1,0:T(8,128)} %collective-permute-done.2), kind=kLoop, calls=%fused_computation.19 | loop fusion | flops 524288 | bytes 2621440 | tf_op jit(solution)/shard_map/convert_element_type | solution.py:200
  44.2 9.9 %collective-permute-done.1 = bf16[128,2048]{1,0:T(8,128)(2,1)S(1)} collective-permute-done((bf16[128,2048]{1,0:T(8,128)(2,1)}, bf16[128,2048]{1,0:T(8,128)(2,1)S(1)}, u32[]{:S(2)}, u32[]{:S(2)}) %collective-permute-start.1) | collective-permute-done | bytes 524320 | tf_op jit(solution)/shard_map/ppermute | solution.py:174
  54.1 0.9 fusion.12
  55.0 5.7 %all-to-all-start.1 = ((bf16[8,128,256]{2,1,0:T(8,128)(2,1)}), bf16[8,128,256]{2,1,0:T(8,128)(2,1)S(1)}, u32[]{:S(2)}, u32[]{:S(2)}) async-start(bf16[8,128,256]{2,1,0:T(8,128)(2,1)} %fusion.12), calls=%async_computation.1 | async-start | bytes 1048576 | tf_op jit(solution)/shard_map/all_to_all | solution.py:205
  60.8 1.4 %collective-permute-start.8 = (bf16[64,2048]{1,0:T(8,128)(2,1)S(1)}, bf16[64,2048]{1,0:T(8,128)(2,1)}, u32[]{:S(2)}, u32[]{:S(2)}) collective-permute-start(bf16[64,2048]{1,0:T(8,128)(2,1)S(1)} %collective-permute-done.3), channel_id=1, source_target_pairs={{0,4},{4,8},{8,12},{12,14},{14,10},{10,6},{6,2},{2,0},{1,5},{5,9},... | collective-permute-start | bytes 786440 | tf_op jit(solution)/shard_map/ppermute | solution.py:192
  62.2 1.5 %collective-permute-start.10 = (bf16[64,2048]{1,0:T(8,128)(2,1)S(1)}, bf16[64,2048]{1,0:T(8,128)(2,1)}, u32[]{:S(2)}, u32[]{:S(2)}) collective-permute-start(bf16[64,2048]{1,0:T(8,128)(2,1)S(1)} %collective-permute-done.5), channel_id=1, source_target_pairs={{0,4},{4,8},{8,12},{12,14},{14,10},{10,6},{6,2},{2,0},{1,5},{5,9},... | collective-permute-start | bytes 786440 | tf_op jit(solution)/shard_map/ppermute | solution.py:192
  63.7 15.1 %collective-permute-done.11 = bf16[64,2048]{1,0:T(8,128)(2,1)} collective-permute-done((bf16[64,2048]{1,0:T(8,128)(2,1)S(1)}, bf16[64,2048]{1,0:T(8,128)(2,1)}, u32[]{:S(2)}, u32[]{:S(2)}) %collective-permute-start.11) | collective-permute-done | bytes 262176 | tf_op jit(solution)/shard_map/ppermute | solution.py:193
  78.8 1.5 %collective-permute-start.12 = (bf16[64,2048]{1,0:T(8,128)(2,1)}, bf16[64,2048]{1,0:T(8,128)(2,1)S(1)}, u32[]{:S(2)}, u32[]{:S(2)}) collective-permute-start(bf16[64,2048]{1,0:T(8,128)(2,1)} %collective-permute-done.8), channel_id=1, source_target_pairs={{0,4},{4,8},{8,12},{12,14},{14,10},{10,6},{6,2},{2,0},{1,5},{5,9},... | collective-permute-start | bytes 786440 | tf_op jit(solution)/shard_map/ppermute | solution.py:192
  80.3 2.0 %collective-permute-start.7 = (bf16[8,128,256]{2,1,0:T(8,128)(2,1)}, bf16[8,128,256]{2,1,0:T(8,128)(2,1)S(1)}, u32[]{:S(2)}, u32[]{:S(2)}) collective-permute-start(bf16[8,128,256]{2,1,0:T(8,128)(2,1)} %all-to-all-done), channel_id=1, source_target_pairs={{0,16},{1,17},{2,18},{3,19},{4,20},{5,21},{6,22},{7,23},{8,24},{9,... | collective-permute-start | bytes 1572872 | tf_op jit(solution)/shard_map/ppermute | solution.py:177
  82.3 2.1 %collective-permute-done.9 = bf16[64,2048]{1,0:T(8,128)(2,1)} collective-permute-done((bf16[64,2048]{1,0:T(8,128)(2,1)}, bf16[64,2048]{1,0:T(8,128)(2,1)}, u32[]{:S(2)}, u32[]{:S(2)}) %collective-permute-start.9) | collective-permute-done | bytes 262176 | tf_op jit(solution)/shard_map/ppermute | solution.py:193
  84.4 1.5 %collective-permute-start.14 = (bf16[64,2048]{1,0:T(8,128)(2,1)}, bf16[64,2048]{1,0:T(8,128)(2,1)}, u32[]{:S(2)}, u32[]{:S(2)}) collective-permute-start(bf16[64,2048]{1,0:T(8,128)(2,1)} %collective-permute-done.10), channel_id=1, source_target_pairs={{0,4},{4,8},{8,12},{12,14},{14,10},{10,6},{6,2},{2,0},{1,5},{5,9},... | collective-permute-start | bytes 786440 | tf_op jit(solution)/shard_map/ppermute | solution.py:192
  85.9 4.0 %collective-permute-done.15 = bf16[64,2048]{1,0:T(8,128)(2,1)S(1)} collective-permute-done((bf16[64,2048]{1,0:T(8,128)(2,1)}, bf16[64,2048]{1,0:T(8,128)(2,1)S(1)}, u32[]{:S(2)}, u32[]{:S(2)}) %collective-permute-start.15) | collective-permute-done | bytes 262176 | tf_op jit(solution)/shard_map/ppermute | solution.py:193
  89.9 1.5 %collective-permute-start.17 = (bf16[64,2048]{1,0:T(8,128)(2,1)S(1)}, bf16[64,2048]{1,0:T(8,128)(2,1)}, u32[]{:S(2)}, u32[]{:S(2)}) collective-permute-start(bf16[64,2048]{1,0:T(8,128)(2,1)S(1)} %collective-permute-done.12), channel_id=1, source_target_pairs={{0,4},{4,8},{8,12},{12,14},{14,10},{10,6},{6,2},{2,0},{1,5},{5,9},... | collective-permute-start | bytes 786440 | tf_op jit(solution)/shard_map/ppermute | solution.py:197
  91.5 1.3 %collective-permute-start.16 = (f32[8,2048]{1,0:T(8,128)S(1)}, f32[8,2048]{1,0:T(8,128)S(1)}, u32[]{:S(2)}, u32[]{:S(2)}) collective-permute-start(f32[8,2048]{1,0:T(8,128)S(1)} %bitcast.104), channel_id=1, source_target_pairs={{16,0},{17,1},{18,2},{19,3},{20,4},{21,5},{22,6},{23,7},{24,8},{25... | collective-permute-start | bytes 196616 | tf_op jit(solution)/shard_map/ppermute | solution.py:211
  92.9 1.4 %fusion.24 = f32[256,2048]{1,0:T(8,128)S(1)} fusion(bf16[64,2048]{1,0:T(8,128)(2,1)} %collective-permute-done.4, bf16[8,128,256]{2,1,0:T(8,128)(2,1)S(1)} %broadcast_select_fusion.1, s32[]{:T(128)S(6)} %select_n.181), kind=kOutput, calls=%fused_computation.51 | convolution fusion | flops 67108864 | bytes 2392068 | tf_op jit(solution)/shard_map/dot_general | solution.py:16
  94.3 0.5 fusion.22
  94.8 0.5 fusion.23
  95.7 0.6 fusion.9
  96.3 1.4 %fusion.21 = f32[256,2048]{1,0:T(8,128)S(1)} fusion(bf16[64,2048]{1,0:T(8,128)(2,1)} %collective-permute-done.9, bf16[8,128,256]{2,1,0:T(8,128)(2,1)S(1)} %broadcast_select_fusion.1, s32[]{:T(128)S(6)} %select_n.185), kind=kOutput, calls=%fused_computation.44 | convolution fusion | flops 67108864 | bytes 2392068 | tf_op jit(solution)/shard_map/dot_general | solution.py:16
  97.7 1.4 %fusion.19 = f32[256,2048]{1,0:T(8,128)S(1)} fusion(bf16[64,2048]{1,0:T(8,128)(2,1)} %collective-permute-done.11, bf16[8,128,256]{2,1,0:T(8,128)(2,1)S(1)} %broadcast_select_fusion.1, s32[]{:T(128)S(6)} %select_n.185, s32[]{:T(128)S(6)} %add.226), kind=kOutput, calls=%fused_computation.40 | convolution fusion | flops 67108864 | bytes 2392072 | tf_op jit(solution)/shard_map/dot_general | solution.py:16
  99.1 1.4 %fusion.20 = f32[256,2048]{1,0:T(8,128)S(1)} fusion(bf16[64,2048]{1,0:T(8,128)(2,1)} %collective-permute-done.10, bf16[8,128,256]{2,1,0:T(8,128)(2,1)S(1)} %broadcast_select_fusion.1, s32[]{:T(128)S(6)} %select_n.183, s32[]{:T(128)S(6)} %add.226), kind=kOutput, calls=%fused_computation.42 | convolution fusion | flops 67108864 | bytes 2392072 | tf_op jit(solution)/shard_map/dot_general | solution.py:16
  100.5 0.5 fusion.16
  101.0 1.4 %fusion.18 = f32[256,2048]{1,0:T(8,128)S(1)} fusion(bf16[64,2048]{1,0:T(8,128)(2,1)} %collective-permute-done.13, bf16[8,128,256]{2,1,0:T(8,128)(2,1)S(1)} %broadcast_select_fusion.1, s32[]{:T(128)S(6)} %select_n.189), kind=kOutput, calls=%fused_computation.37 | convolution fusion | flops 67108864 | bytes 2392068 | tf_op jit(solution)/shard_map/dot_general | solution.py:16
  102.4 1.4 %fusion.17 = f32[256,2048]{1,0:T(8,128)S(1)} fusion(bf16[64,2048]{1,0:T(8,128)(2,1)} %collective-permute-done.14, bf16[8,128,256]{2,1,0:T(8,128)(2,1)S(1)} %broadcast_select_fusion.1, s32[]{:T(128)S(6)} %select_n.187, s32[]{:T(128)S(6)} %add.226), kind=kOutput, calls=%fused_computation.35 | convolution fusion | flops 67108864 | bytes 2392072 | tf_op jit(solution)/shard_map/dot_general | solution.py:16
  103.8 1.5 %fusion.4 = f32[256,2048]{1,0:T(8,128)S(1)} fusion(f32[256,2048]{1,0:T(8,128)S(1)} %fusion.19, f32[256,2048]{1,0:T(8,128)S(1)} %fusion.20, f32[256,2048]{1,0:T(8,128)S(1)} %fusion.21, f32[256,2048]{1,0:T(8,128)S(1)} %fusion.9, bf16[64,2048]{1,0:T(8,128)(2,1)} %collective-permute-done.8, bf16[8,128,256]{2,1,0:T(8,128)(2,1)S(1)} %broadcast_select_fusion.1, ...), kind=kOutput, calls=%fused_computation.7 | convolution fusion | flops 69206016 | bytes 10780676 | tf_op jit(solution)/shard_map/dot_general | solution.py:16
  105.4 0.6 fusion.6
  106.0 0.6 broadcast_select_fusion.2
  106.6 1.4 %fusion.26 = f32[256,2048]{1,0:T(8,128)S(1)} fusion(bf16[64,2048]{1,0:T(8,128)(2,1)} %collective-permute-done.18, bf16[128,256]{1,0:T(8,128)(2,1)S(1)} %dynamic-slice_bitcast_fusion.1), kind=kOutput, calls=%fused_computation.54 | convolution fusion | flops 67108864 | bytes 2392064 | tf_op jit(solution)/shard_map/dot_general | solution.py:16
  108.1 1.4 %fusion = f32[256,2048]{1,0:T(8,128)S(1)} fusion(f32[256,2048]{1,0:T(8,128)S(1)} %fusion.26, f32[256,2048]{1,0:T(8,128)S(1)} %fusion.6, bf16[64,2048]{1,0:T(8,128)(2,1)} %collective-permute-done.17, bf16[128,256]{1,0:T(8,128)(2,1)S(1)} %dynamic-slice_bitcast_fusion.1), kind=kOutput, calls=%fused_computation.1 | convolution fusion | flops 68157440 | bytes 6586368 | tf_op jit(solution)/shard_map/dot_general | solution.py:16
  109.5 1.1 dynamic-slice_bitcast_fusion
  110.6 4.0 %collective-permute-start.19 = (f32[128,2048]{1,0:T(8,128)}, f32[128,2048]{1,0:T(8,128)}, u32[]{:S(2)}, u32[]{:S(2)}) collective-permute-start(f32[128,2048]{1,0:T(8,128)} %dynamic-slice_bitcast_fusion), channel_id=1, source_target_pairs={{0,1},{1,0},{2,3},{3,2},{4,5},{5,4},{6,7},{7,6},{8,9},{9,8},{10,11... | collective-permute-start | bytes 3145736 | tf_op jit(solution)/shard_map/ppermute | solution.py:20
  114.6 0.9 broadcast_select_fusion
  115.5 1.8 %collective-permute-done.19 = f32[128,2048]{1,0:T(8,128)} collective-permute-done((f32[128,2048]{1,0:T(8,128)}, f32[128,2048]{1,0:T(8,128)}, u32[]{:S(2)}, u32[]{:S(2)}) %collective-permute-start.19) | collective-permute-done | bytes 1048608 | tf_op jit(solution)/shard_map/ppermute | solution.py:20
  117.2 2.3 %fusion.11 = f32[1,128,2048]{2,1,0:T(8,128)} fusion(f32[128,2048]{1,0:T(8,128)} %collective-permute-done.19, f32[2,128,2048]{2,1,0:T(8,128)S(1)} %bitcast.98, s32[]{:T(128)S(6)} %select_n.194), kind=kLoop, calls=%fused_computation.16 | loop fusion | flops 524288 | bytes 3145732 | tf_op jit(solution)/shard_map/broadcast_in_dim | solution.py:224
  (47 shorter events, 1.5 us)
Async XLA Ops:
  1.4 3.4 %copy-start = (bf16[1,2048,2048]{2,1,0:T(8,128)(2,1)S(1)}, bf16[1,2048,2048]{2,1,0:T(8,128)(2,1)}, u32[]{:S(2)}) copy-start(bf16[1,2048,2048]{2,1,0:T(8,128)(2,1)} %param.5) | copy-start | bytes 25165828
  4.8 1.0 copy-start.2
  5.8 1.2 %copy-start.4 = (bf16[256,2048]{1,0:T(8,128)(2,1)S(1)}, bf16[256,2048]{1,0:T(8,128)(2,1)}, u32[]{:S(2)}) copy-start(bf16[256,2048]{1,0:T(8,128)(2,1)} %table.1) | copy-start | bytes 3145732
  7.0 12.8 %copy-start.7 = (s32[128]{0:T(128)S(1)}, s32[128]{0:T(128)}, u32[]{:S(2)}) copy-start(s32[128]{0:T(128)} %param.7) | copy-start | bytes 1540
  7.0 17.6 %copy-start.3 = (bf16[1,128,2048]{2,1,0:T(8,128)(2,1)S(1)}, bf16[1,128,2048]{2,1,0:T(8,128)(2,1)}, u32[]{:S(2)}) copy-start(bf16[1,128,2048]{2,1,0:T(8,128)(2,1)} %param.4) | copy-start | bytes 1572868
  10.9 13.7 %collective-permute-start = (bf16[2,128,1024]{2,1,0:T(8,128)(2,1)S(1)}, bf16[2,128,1024]{2,1,0:T(8,128)(2,1)S(1)}, u32[]{:S(2)}, u32[]{:S(2)}) collective-permute-start(bf16[2,128,1024]{2,1,0:T(8,128)(2,1)S(1)} %get-tuple-element.17), channel_id=1, source_target_pairs={{0,16},{1,17},{2,18},{3,19},{4,20},{5,21},{6,22},{7,23},{8,24},{9,... | collective-permute-start | bytes 1572872 | tf_op jit(solution)/shard_map/ppermute | solution.py:168
  14.1 25.5 %all-to-all-start = ((bf16[8,128,256]{2,1,0:T(8,128)(2,1)}), bf16[8,128,256]{2,1,0:T(8,128)(2,1)}, u32[]{:S(2)}, u32[]{:S(2)}) async-start(bf16[8,128,256]{2,1,0:T(8,128)(2,1)} %get-tuple-element.22), calls=%async_computation | async-start | bytes 1048576 | tf_op jit(solution)/shard_map/all_to_all | solution.py:169
  24.6 3.4 %copy-start.1 = (bf16[1,2048,2048]{2,1,0:T(8,128)(2,1)S(1)}, bf16[1,2048,2048]{2,1,0:T(8,128)(2,1)}, u32[]{:S(2)}) copy-start(bf16[1,2048,2048]{2,1,0:T(8,128)(2,1)} %param.5) | copy-start | bytes 25165828
  36.7 5.7 %collective-permute-start.2 = (f32[128,2048]{1,0:T(8,128)}, f32[128,2048]{1,0:T(8,128)}, u32[]{:S(2)}, u32[]{:S(2)}) collective-permute-start(f32[128,2048]{1,0:T(8,128)} %get-tuple-element.21), channel_id=1, source_target_pairs={{0,1},{1,0},{2,3},{3,2},{4,5},{5,4},{6,7},{7,6},{8,9},{9,8},{10,11... | collective-permute-start | bytes 3145736 | tf_op jit(solution)/shard_map/ppermute | solution.py:20
  38.3 15.8 %collective-permute-start.1 = (bf16[128,2048]{1,0:T(8,128)(2,1)}, bf16[128,2048]{1,0:T(8,128)(2,1)S(1)}, u32[]{:S(2)}, u32[]{:S(2)}) collective-permute-start(bf16[128,2048]{1,0:T(8,128)(2,1)} %get-tuple-element.19), channel_id=1, source_target_pairs={{16,0},{17,1},{18,2},{19,3},{20,4},{21,5},{22,6},{23,7},{24,8},{25... | collective-permute-start | bytes 1572872 | tf_op jit(solution)/shard_map/ppermute | solution.py:174
  39.6 15.4 %collective-permute-start.3 = (bf16[64,2048]{1,0:T(8,128)(2,1)S(1)}, bf16[64,2048]{1,0:T(8,128)(2,1)S(1)}, u32[]{:S(2)}, u32[]{:S(2)}) collective-permute-start(bf16[64,2048]{1,0:T(8,128)(2,1)S(1)} %get-tuple-element.31), channel_id=1, source_target_pairs={{0,4},{4,8},{8,12},{12,14},{14,10},{10,6},{6,2},{2,0},{1,5},{5,9},... | collective-permute-start | bytes 786440 | tf_op jit(solution)/shard_map/ppermute | solution.py:192
  41.0 14.0 %collective-permute-start.4 = (bf16[64,2048]{1,0:T(8,128)(2,1)S(1)}, bf16[64,2048]{1,0:T(8,128)(2,1)}, u32[]{:S(2)}, u32[]{:S(2)}) collective-permute-start(bf16[64,2048]{1,0:T(8,128)(2,1)S(1)} %get-tuple-element.31), channel_id=1, source_target_pairs={{4,0},{8,4},{12,8},{14,12},{10,14},{6,10},{2,6},{0,2},{5,1},{9,5},... | collective-permute-start | bytes 786440 | tf_op jit(solution)/shard_map/ppermute | solution.py:193
  41.2 13.8 %collective-permute-start.5 = (bf16[64,2048]{1,0:T(8,128)(2,1)S(1)}, bf16[64,2048]{1,0:T(8,128)(2,1)S(1)}, u32[]{:S(2)}, u32[]{:S(2)}) collective-permute-start(bf16[64,2048]{1,0:T(8,128)(2,1)S(1)} %get-tuple-element.32), channel_id=1, source_target_pairs={{0,4},{4,8},{8,12},{12,14},{14,10},{10,6},{6,2},{2,0},{1,5},{5,9},... | collective-permute-start | bytes 786440 | tf_op jit(solution)/shard_map/ppermute | solution.py:192
  42.5 12.6 %collective-permute-start.6 = (bf16[64,2048]{1,0:T(8,128)(2,1)S(1)}, bf16[64,2048]{1,0:T(8,128)(2,1)S(1)}, u32[]{:S(2)}, u32[]{:S(2)}) collective-permute-start(bf16[64,2048]{1,0:T(8,128)(2,1)S(1)} %get-tuple-element.32), channel_id=1, source_target_pairs={{4,0},{8,4},{12,8},{14,12},{10,14},{6,10},{2,6},{0,2},{5,1},{9,5},... | collective-permute-start | bytes 786440 | tf_op jit(solution)/shard_map/ppermute | solution.py:193
  55.0 23.8 %copy-start.5 = (bf16[64,2048]{1,0:T(8,128)(2,1)}, bf16[64,2048]{1,0:T(8,128)(2,1)S(1)}, u32[]{:S(2)}) copy-start(bf16[64,2048]{1,0:T(8,128)(2,1)S(1)} %collective-permute-done.3) | copy-start | bytes 786436
  55.0 36.4 %all-to-all-start.1 = ((bf16[8,128,256]{2,1,0:T(8,128)(2,1)}), bf16[8,128,256]{2,1,0:T(8,128)(2,1)S(1)}, u32[]{:S(2)}, u32[]{:S(2)}) async-start(bf16[8,128,256]{2,1,0:T(8,128)(2,1)} %fusion.12), calls=%async_computation.1 | async-start | bytes 1048576 | tf_op jit(solution)/shard_map/all_to_all | solution.py:205
  60.8 18.0 %collective-permute-start.11 = (bf16[64,2048]{1,0:T(8,128)(2,1)S(1)}, bf16[64,2048]{1,0:T(8,128)(2,1)}, u32[]{:S(2)}, u32[]{:S(2)}) collective-permute-start(bf16[64,2048]{1,0:T(8,128)(2,1)S(1)} %collective-permute-done.6), channel_id=1, source_target_pairs={{4,0},{8,4},{12,8},{14,12},{10,14},{6,10},{2,6},{0,2},{5,1},{9,5},... | collective-permute-start | bytes 786440 | tf_op jit(solution)/shard_map/ppermute | solution.py:193
  60.8 18.0 %collective-permute-start.8 = (bf16[64,2048]{1,0:T(8,128)(2,1)S(1)}, bf16[64,2048]{1,0:T(8,128)(2,1)}, u32[]{:S(2)}, u32[]{:S(2)}) collective-permute-start(bf16[64,2048]{1,0:T(8,128)(2,1)S(1)} %collective-permute-done.3), channel_id=1, source_target_pairs={{0,4},{4,8},{8,12},{12,14},{14,10},{10,6},{6,2},{2,0},{1,5},{5,9},... | collective-permute-start | bytes 786440 | tf_op jit(solution)/shard_map/ppermute | solution.py:192
  62.2 22.2 %collective-permute-start.9 = (bf16[64,2048]{1,0:T(8,128)(2,1)}, bf16[64,2048]{1,0:T(8,128)(2,1)}, u32[]{:S(2)}, u32[]{:S(2)}) collective-permute-start(bf16[64,2048]{1,0:T(8,128)(2,1)} %collective-permute-done.4), channel_id=1, source_target_pairs={{4,0},{8,4},{12,8},{14,12},{10,14},{6,10},{2,6},{0,2},{5,1},{9,5},... | collective-permute-start | bytes 786440 | tf_op jit(solution)/shard_map/ppermute | solution.py:193
  62.2 22.2 %collective-permute-start.10 = (bf16[64,2048]{1,0:T(8,128)(2,1)S(1)}, bf16[64,2048]{1,0:T(8,128)(2,1)}, u32[]{:S(2)}, u32[]{:S(2)}) collective-permute-start(bf16[64,2048]{1,0:T(8,128)(2,1)S(1)} %collective-permute-done.5), channel_id=1, source_target_pairs={{0,4},{4,8},{8,12},{12,14},{14,10},{10,6},{6,2},{2,0},{1,5},{5,9},... | collective-permute-start | bytes 786440 | tf_op jit(solution)/shard_map/ppermute | solution.py:192
  78.8 11.1 %collective-permute-start.15 = (bf16[64,2048]{1,0:T(8,128)(2,1)}, bf16[64,2048]{1,0:T(8,128)(2,1)S(1)}, u32[]{:S(2)}, u32[]{:S(2)}) collective-permute-start(bf16[64,2048]{1,0:T(8,128)(2,1)} %collective-permute-done.11), channel_id=1, source_target_pairs={{4,0},{8,4},{12,8},{14,12},{10,14},{6,10},{2,6},{0,2},{5,1},{9,5},... | collective-permute-start | bytes 786440 | tf_op jit(solution)/shard_map/ppermute | solution.py:193
  78.8 11.1 %collective-permute-start.12 = (bf16[64,2048]{1,0:T(8,128)(2,1)}, bf16[64,2048]{1,0:T(8,128)(2,1)S(1)}, u32[]{:S(2)}, u32[]{:S(2)}) collective-permute-start(bf16[64,2048]{1,0:T(8,128)(2,1)} %collective-permute-done.8), channel_id=1, source_target_pairs={{0,4},{4,8},{8,12},{12,14},{14,10},{10,6},{6,2},{2,0},{1,5},{5,9},... | collective-permute-start | bytes 786440 | tf_op jit(solution)/shard_map/ppermute | solution.py:192
  80.3 11.2 %collective-permute-start.7 = (bf16[8,128,256]{2,1,0:T(8,128)(2,1)}, bf16[8,128,256]{2,1,0:T(8,128)(2,1)S(1)}, u32[]{:S(2)}, u32[]{:S(2)}) collective-permute-start(bf16[8,128,256]{2,1,0:T(8,128)(2,1)} %all-to-all-done), channel_id=1, source_target_pairs={{0,16},{1,17},{2,18},{3,19},{4,20},{5,21},{6,22},{7,23},{8,24},{9,... | collective-permute-start | bytes 1572872 | tf_op jit(solution)/shard_map/ppermute | solution.py:177
  84.4 16.6 %collective-permute-start.13 = (bf16[64,2048]{1,0:T(8,128)(2,1)}, bf16[64,2048]{1,0:T(8,128)(2,1)}, u32[]{:S(2)}, u32[]{:S(2)}) collective-permute-start(bf16[64,2048]{1,0:T(8,128)(2,1)} %collective-permute-done.9), channel_id=1, source_target_pairs={{4,0},{8,4},{12,8},{14,12},{10,14},{6,10},{2,6},{0,2},{5,1},{9,5},... | collective-permute-start | bytes 786440 | tf_op jit(solution)/shard_map/ppermute | solution.py:193
  84.4 18.0 %collective-permute-start.14 = (bf16[64,2048]{1,0:T(8,128)(2,1)}, bf16[64,2048]{1,0:T(8,128)(2,1)}, u32[]{:S(2)}, u32[]{:S(2)}) collective-permute-start(bf16[64,2048]{1,0:T(8,128)(2,1)} %collective-permute-done.10), channel_id=1, source_target_pairs={{0,4},{4,8},{8,12},{12,14},{14,10},{10,6},{6,2},{2,0},{1,5},{5,9},... | collective-permute-start | bytes 786440 | tf_op jit(solution)/shard_map/ppermute | solution.py:192
  89.9 16.7 %collective-permute-start.18 = (bf16[64,2048]{1,0:T(8,128)(2,1)S(1)}, bf16[64,2048]{1,0:T(8,128)(2,1)}, u32[]{:S(2)}, u32[]{:S(2)}) collective-permute-start(bf16[64,2048]{1,0:T(8,128)(2,1)S(1)} %collective-permute-done.15), channel_id=1, source_target_pairs={{4,0},{8,4},{12,8},{14,12},{10,14},{6,10},{2,6},{0,2},{5,1},{9,5},... | collective-permute-start | bytes 786440 | tf_op jit(solution)/shard_map/ppermute | solution.py:198
  89.9 18.1 %collective-permute-start.17 = (bf16[64,2048]{1,0:T(8,128)(2,1)S(1)}, bf16[64,2048]{1,0:T(8,128)(2,1)}, u32[]{:S(2)}, u32[]{:S(2)}) collective-permute-start(bf16[64,2048]{1,0:T(8,128)(2,1)S(1)} %collective-permute-done.12), channel_id=1, source_target_pairs={{0,4},{4,8},{8,12},{12,14},{14,10},{10,6},{6,2},{2,0},{1,5},{5,9},... | collective-permute-start | bytes 786440 | tf_op jit(solution)/shard_map/ppermute | solution.py:197
  91.5 14.5 %collective-permute-start.16 = (f32[8,2048]{1,0:T(8,128)S(1)}, f32[8,2048]{1,0:T(8,128)S(1)}, u32[]{:S(2)}, u32[]{:S(2)}) collective-permute-start(f32[8,2048]{1,0:T(8,128)S(1)} %bitcast.104), channel_id=1, source_target_pairs={{16,0},{17,1},{18,2},{19,3},{20,4},{21,5},{22,6},{23,7},{24,8},{25... | collective-permute-start | bytes 196616 | tf_op jit(solution)/shard_map/ppermute | solution.py:211
  94.3 1.0 copy-start.6
  110.6 6.7 %collective-permute-start.19 = (f32[128,2048]{1,0:T(8,128)}, f32[128,2048]{1,0:T(8,128)}, u32[]{:S(2)}, u32[]{:S(2)}) collective-permute-start(f32[128,2048]{1,0:T(8,128)} %dynamic-slice_bitcast_fusion), channel_id=1, source_target_pairs={{0,1},{1,0},{2,3},{3,2},{4,5},{5,4},{6,7},{7,6},{8,9},{9,8},{10,11... | collective-permute-start | bytes 3145736 | tf_op jit(solution)/shard_map/ppermute | solution.py:20

commit v3 on v2

--- a/solution.py
+++ b/solution.py
@@ -9,7 +9,6 @@
 F32 = jnp.float32
 BF16 = jnp.bfloat16
 TILE = 256
-GRANT = 16 * 1024 * 1024
 
 
 def dot(a, b, ca, cb):
@@ -28,22 +27,61 @@
     return pl.ds(pl.multiple_of(base + step * TILE, TILE), TILE)
 
 
-def lead_body(rows, weight, onehot, table, query, mixed, rel):
+def fetch(pairs, sems):
+    copies = [pltpu.make_async_copy(source, target, sems.at[i]) for i, (source, target) in enumerate(pairs)]
+    for copy in copies:
+        copy.start()
+    return copies
+
+
+def wait(copies):
+    for copy in copies:
+        copy.wait()
+
+
+def call(body, outs, args, scratch, grant, flops, moved):
+    return pl.pallas_call(
+        body,
+        out_shape=outs,
+        in_specs=[
+            pl.BlockSpec(memory_space=pltpu.SMEM if arg.ndim == 1 else pl.ANY) for arg in args
+        ],
+        out_specs=(pl.BlockSpec(memory_space=pl.ANY),) * len(outs),
+        scratch_shapes=scratch,
+        compiler_params=pltpu.CompilerParams(vmem_limit_bytes=grant * 1024 * 1024),
+        cost_estimate=pl.CostEstimate(flops=flops, bytes_accessed=moved, transcendentals=0),
+    )(*args)
+
+
+def room(*arrays):
+    return [pltpu.VMEM(array.shape, array.dtype) for array in arrays]
+
+
+def lead_body(
+    rows_at, weight_at, onehot_at, table_at, query_at, mixed_at, rel_at,
+    rows, weight, onehot, table, query, mixed, rel, small, large, stored,
+):
     half = weight.shape[0] // 2
     steps = half // TILE
+    early = fetch([(onehot_at, onehot), (rows_at, rows), (table_at, table)], small)
+    pieces = [at(step, base) for step in range(steps) for base in (0, half)]
+    loads = fetch([(weight_at.at[piece], weight.at[piece]) for piece in pieces], large)
+    wait(early)
     for step in range(steps):
         span = pl.ds(step * TILE, TILE)
         r_re = dot(onehot[...], table[:, at(step)], 1, 0)
         r_im = dot(onehot[...], table[:, at(step, half)], 1, 0)
+        rel[0, :, span], rel[1, :, span] = r_re.astype(BF16), r_im.astype(BF16)
+        wait(loads[2 * step:2 * step + 2])
         q_re = dot(rows[...], weight[at(step)], 1, 1).astype(BF16)
         q_im = dot(rows[...], weight[at(step, half)], 1, 1).astype(BF16)
         query[0, :, span], query[1, :, span] = q_re, q_im
-        rel[0, :, span], rel[1, :, span] = r_re.astype(BF16), r_im.astype(BF16)
         z_re, z_im = mix(q_re.astype(F32), q_im.astype(F32), r_re, r_im)
         if mixed.shape[2] == TILE:
             mixed[step], mixed[steps + step] = z_re, z_im
         else:
             mixed[0, :, span], mixed[1, :, span] = z_re, z_im
+    wait(fetch([(query, query_at), (mixed, mixed_at), (rel, rel_at)], stored))
 
 
 def lead(rows, weight, onehot, table, chips):
@@ -52,29 +90,33 @@
     half = width // 2
     cols = width // chips
     count_rel = table.shape[0]
-    vmem = pl.BlockSpec(memory_space=pltpu.VMEM)
     pair = jax.ShapeDtypeStruct((2, rows_dev, half), BF16)
     apart = jax.ShapeDtypeStruct((chips, rows_dev, cols), BF16) if cols == TILE else pair
-    query, mixed, rel = pl.pallas_call(
-        lead_body,
-        out_shape=(pair, apart, pair),
-        in_specs=[vmem] * 4,
-        out_specs=(vmem,) * 3,
-        compiler_params=pltpu.CompilerParams(vmem_limit_bytes=GRANT),
-        cost_estimate=pl.CostEstimate(
-            flops=2 * rows_dev * width * (hidden + count_rel), bytes_accessed=2 * width * hidden, transcendentals=0
-        ),
-    )(rows, weight, onehot, table)
+    outs = (pair, apart, pair)
+    args = (rows, weight, onehot, table)
+    dma = pltpu.SemaphoreType.DMA
+    query, mixed, rel = call(
+        lead_body, outs, args,
+        room(*args, *outs) + [dma((3,)), dma((width // TILE,)), dma((3,))],
+        56, 2 * rows_dev * width * (hidden + count_rel), 2 * width * hidden,
+    )
     if cols != TILE:
         mixed = mixed.reshape(2, rows_dev, chips // 2, cols).transpose(0, 2, 1, 3).reshape(chips, rows_dev, cols)
     return query, mixed, rel
 
 
-def trail_body(first, query, rows, weight, rel, onehot, right, query_grad, give, keep, mixed, hidden):
+def trail_body(
+    first, query_at, rows_at, weight_at, rel_at, onehot_at, right_at, grad_at, give_at, keep_at,
+    query, rows, weight, rel, onehot, right, query_grad, give, keep, mixed, hidden, small, large, stored, last,
+):
     width = weight.shape[0]
     half = width // 2
     is_first = first[0] == 1
     owned = give.shape[0]
+    early = fetch([(query_at, query), (rel_at, rel), (rows_at, rows), (onehot_at, onehot)], small)
+    pieces = [at(step) for step in range(weight.shape[1] // TILE)]
+    loads = fetch([(weight_at.at[:, piece], weight.at[:, piece]) for piece in pieces], large)
+    wait(early)
 
     def make_mixed(step, carry):
         mixed[:, at(step)], mixed[:, at(step, half)] = mix(
@@ -85,16 +127,15 @@
 
     lax.fori_loop(0, half // TILE, make_mixed, 0)
 
-    def make_hidden(step, carry):
+    for step, load in enumerate(loads):
+        load.wait()
         pre = dot(mixed[...], weight[:, at(step)], 1, 0)
         sig = jax.nn.sigmoid(pre)
         cot = rows[:, at(step)]
         grad = (cot.astype(F32) * (sig * (1.0 + pre * (1.0 - sig)))).astype(BF16)
         hidden[:, at(step)] = grad
         right[:, at(step)] = jnp.where(is_first, cot, grad)
-        return carry
-
-    lax.fori_loop(0, weight.shape[1] // TILE, make_hidden, 0)
+    send = fetch([(right, right_at)], stored)
 
     def make_query(step, carry):
         gz_re = dot(hidden[...], weight[at(step), :], 1, 1)
@@ -112,30 +153,72 @@
         return carry
 
     lax.fori_loop(0, half // TILE, make_query, 0)
+    wait(fetch([(query_grad, grad_at), (give, give_at), (keep, keep_at)], last) + send)
 
 
 def trail(first, query, rows, weight, rel, onehot):
     rows_dev, hidden = rows.shape
     width = weight.shape[0]
     count_rel = onehot.shape[0]
-    vmem = pl.BlockSpec(memory_space=pltpu.VMEM)
-    flops = 4 * rows_dev * width * hidden + 4 * rows_dev * count_rel * width
-    return pl.pallas_call(
-        trail_body,
-        out_shape=(
-            jax.ShapeDtypeStruct((rows_dev, hidden), BF16),
-            jax.ShapeDtypeStruct((rows_dev, width), BF16),
-            jax.ShapeDtypeStruct((count_rel // 2, width), F32),
-            jax.ShapeDtypeStruct((count_rel // 2, width), F32),
-        ),
-        in_specs=[pl.BlockSpec(memory_space=pltpu.SMEM)] + [vmem] * 5,
-        out_specs=(vmem,) * 4,
-        scratch_shapes=[pltpu.VMEM((rows_dev, width), BF16), pltpu.VMEM((rows_dev, hidden), BF16)],
-        compiler_params=pltpu.CompilerParams(vmem_limit_bytes=GRANT),
-        cost_estimate=pl.CostEstimate(
-            flops=flops, bytes_accessed=4 * width * hidden, transcendentals=rows_dev * hidden
-        ),
-    )(first, query, rows, weight, rel, onehot)
+    partial = jax.ShapeDtypeStruct((count_rel // 2, width), F32)
+    outs = (
+        jax.ShapeDtypeStruct((rows_dev, hidden), BF16), jax.ShapeDtypeStruct((rows_dev, width), BF16),
+        partial, partial,
+    )
+    args = (query, rows, weight, rel, onehot)
+    dma = pltpu.SemaphoreType.DMA
+    scratch = room(*args, *outs) + [pltpu.VMEM((rows_dev, width), BF16), pltpu.VMEM((rows_dev, hidden), BF16)]
+    return call(
+        trail_body, outs, (first,) + args,
+        scratch + [dma((4,)), dma((hidden // TILE,)), dma((1,)), dma((3,))],
+        56, 4 * rows_dev * width * (hidden + count_rel), 4 * width * hidden,
+    )
+
+
+def product_body(parts, before, order, left_at, *refs):
+    count = sum(len(part) for part in parts)
+    inputs = refs[:count + before]
+    outs = refs[count + before:count + before + 2]
+    left, blocks = refs[count + before + 2], refs[count + before + 3:-4]
+    sums = refs[-4:-2]
+    sems, stored = refs[-2:]
+    pairs = [(left_at, left)] + list(zip(inputs[:count], blocks))
+    pairs += list(zip(inputs[count:], sums)) if before else []
+    wait(fetch(pairs, sems))
+    owned = sums[0].shape[0]
+
+    def column(step, carry):
+        acc = jnp.zeros((left.shape[2], TILE), F32)
+        taken = 0
+        for number, part in enumerate(parts):
+            block = jnp.concatenate([blocks[taken + i][:, at(step)] for i in range(len(part))], axis=0)
+            taken += len(part)
+            acc = acc + dot(left[order[number]], block, 0, 0)
+        for i in range(2):
+            half = acc[i * owned:(i + 1) * owned]
+            sums[i][:, at(step)] = sums[i][:, at(step)] + half if before else half
+        return carry
+
+    lax.fori_loop(0, sums[0].shape[1] // TILE, column, 0)
+    wait(fetch(list(zip(sums, outs)), stored))
+
+
+def product(order, left, parts, before):
+    chips, rows_dev, cols = left.shape
+    width = parts[0][0].shape[1]
+    blocks = [block for part in parts for block in part]
+    partial = jax.ShapeDtypeStruct((cols // 2, width), F32)
+    dma = pltpu.SemaphoreType.DMA
+
+    def body(*refs):
+        product_body(parts, len(before), *refs)
+
+    return call(
+        body, (partial, partial), (order, left, *blocks, *before),
+        room(left, *blocks, partial, partial)
+        + [dma((1 + len(blocks) + len(before),)), dma((2,))],
+        48, 2 * cols * width * rows_dev * len(parts), 2 * width * rows_dev * len(parts),
+    )
 
 
 def local(section_rows, weights, relation_table, relation_ids):
@@ -185,23 +268,22 @@
     place = jnp.where(lax.rem(chip, 2) == 0, chip // 2, chips - 1 - chip // 2)
     up = [(ring[i], ring[(i + 1) % chips]) for i in range(chips)]
     down = [(b, a) for a, b in up]
-    blocks = [(right, 0, 0)]
     mid = rows_dev // 2
-    fwd = bwd = [right[:mid], right[mid:]]
+    fwd = bwd = (right[:mid], right[mid:])
+    parts = [((right,), 0)]
     for s in range(1, (chips + 1) // 2):
-        fwd = [lax.ppermute(part, "chip", up) for part in fwd]
-        bwd = [lax.ppermute(part, "chip", down) for part in bwd]
-        for base, ahead, behind in zip((0, mid), fwd, bwd):
-            blocks += [(ahead, chips - s, base), (behind, s, base)]
+        fwd = tuple(lax.ppermute(part, "chip", up) for part in fwd)
+        bwd = tuple(lax.ppermute(part, "chip", down) for part in bwd)
+        parts += [(fwd, chips - s), (bwd, s)]
     if chips % 2 == 0:
-        blocks.append((lax.ppermute(fwd[0], "chip", up), chips // 2, 0))
-        blocks.append((lax.ppermute(bwd[1], "chip", down), chips // 2, mid))
+        far = (lax.ppermute(fwd[0], "chip", up), lax.ppermute(bwd[1], "chip", down))
+        parts.append((far, chips // 2))
 
     rel_sent = (rel_keep + rel_got).astype(BF16).reshape(chips, 2 * owned, chips, cols)
     rel_sent = rel_sent.transpose(0, 2, 1, 3).reshape(chips, 2 * owned * chips, cols)
     if rel_sent.shape[1] == rows_dev:
         shared = jnp.where(first, columns(query_back), rel_sent)
-        shared, _ = lax.optimization_barrier((shared, tuple(block for block, _, _ in blocks[1:5])))
+        shared, _ = lax.optimization_barrier((shared, (parts[3][0][0], parts[4][0][0], z_cols)))
         query_cols = rel_rows = lax.all_to_all(shared, "chip", 0, 0, tiled=True)
     else:
         query_cols = lax.all_to_all(columns(query_back), "chip", 0, 0, tiled=True)
@@ -211,15 +293,17 @@
     relation_grad = jnp.where(first, lax.ppermute(rel_sum[0], "hop", [(1, 0)]), rel_sum[1])
 
     left_cols = jnp.where(first, query_cols, z_cols)
-    partial = jnp.zeros((cols, width), F32)
-    for block, step, base in blocks:
-        left = lax.dynamic_index_in_dim(left_cols, chip_at(place + step), 0, keepdims=False)
-        if step == chips // 2:
-            left, relation_grad = lax.optimization_barrier((left, relation_grad))
-        partial = partial + dot(left[base:base + block.shape[0]], block, 0, 0)
-    partial = partial.reshape(2, cols // 2, width)
-    keep = lax.dynamic_index_in_dim(partial, core, 0, keepdims=False)
-    give = lax.dynamic_index_in_dim(partial, 1 - core, 0, keepdims=False)
+    lower, upper = left_cols[..., :cols // 2], left_cols[..., cols // 2:]
+    left_cols = jnp.concatenate(
+        [jnp.where(core == 0, upper, lower), jnp.where(core == 0, lower, upper)], axis=2
+    )
+    sums = ()
+    split = len(parts) - 3
+    for group in (parts[:split], parts[split:]):
+        order = jnp.stack([chip_at(place + step) for _, step in group])
+        sums = product(order, left_cols, [part for part, _ in group], sums)
+        left_cols, relation_grad = lax.optimization_barrier((left_cols, relation_grad))
+    give, keep = sums
     weight_grad = (keep + swap_core(give)) * (1.0 / jnp.sqrt(F32(total_rows)))
     return weight_grad[None], relation_grad, query_grad
 

time: 122 us -> 128 us (1.049)
  Pallas kernels: 12.6 us -> 31.2 us
  matrix products: 15.8 us -> 0 us
  local copies, waits for them, and re-layouts: 10.4 us -> 6.96 us
  starting transfers between devices: 35.1 us -> 38.2 us
  other arithmetic: 7.02 us -> 9.84 us
  waiting for transfers between devices: 37.6 us -> 38.9 us
    pallas_call x2 -> x4, Pallas kernels: 12.6 us -> 31.2 us  [call(): pl.pallas_call(body, out_shape=outs, in_specs=[pl.BlockSpec(memory_space=...]
    dot_general x15 -> x0, matrix products: 15.8 us -> none  [dot(): lax.dot_general(a, b, (((ca,), (cb,)), ((), ())), preferred_element_type=...]
    ppermute x14, waiting for transfers between devices: 21.3 us -> 26.3 us  [the longest x6 20.6 us: local(): bwd = tuple((lax.ppermute(part, 'chip', down) for part in bwd))]
    unnamed x17 -> x25, local copies, waits for them, and re-layouts: 9.16 us -> 4.48 us
    ppermute x1, waiting for transfers between devices: 9.86 us -> 6.87 us  [local(): query_back = lax.ppermute(grad_query, 'hop', [(1, 0)])]
    ppermute x2, starting transfers between devices: 5.58 us -> 8.23 us  [swap_core(): return lax.ppermute(block, 'core', [(0, 1), (1, 0)])]
    ppermute x1, starting transfers between devices: 2.02 us -> 4.05 us  [local(): z_cols = lax.ppermute(z_cols, 'hop', [(0, 1)])]
    slice x1, local copies, waits for them, and re-layouts: 0.04 us -> 1.8 us  [local(): fwd = bwd = (right[:mid], right[mid:])]
  transfers between devices with their start and end apart: 22 -> 22, of which waited for: 6 -> 8; matrix products, arithmetic and copies ran while one was open for 16% -> 8% of each run, Pallas kernels for 7% -> 14%
where the time goes in v3:
time: 128 us; the launch traced here: 126 us
  waiting for transfers between devices  38.9 us (30%)
  starting transfers between devices  38.2 us (30%)
  Pallas kernels  31.2 us (24%)
  other arithmetic  9.84 us (8%)
  local copies, waits for them, and re-layouts  6.96 us (5%)
    pallas_call x4, Pallas kernels, call(): pl.pallas_call(body, out_shape=outs, in_specs=[pl.BlockSpec(memory_space=...  31.2 us
    ppermute x6, waiting for transfers between devices, local(): bwd = tuple((lax.ppermute(part, 'chip', down) for part in bwd))  20.6 us
    ppermute x2, starting transfers between devices, swap_core(): return lax.ppermute(block, 'core', [(0, 1), (1, 0)])  8.23 us
    ppermute x1, waiting for transfers between devices, local(): query_back = lax.ppermute(grad_query, 'hop', [(1, 0)])  6.87 us
    ppermute x6, starting transfers between devices, local(): fwd = tuple((lax.ppermute(part, 'chip', up) for part in fwd))  6.11 us
    all_to_all x1, starting transfers between devices, local(): z_cols = lax.all_to_all(own_mixed, 'chip', 0, 0, tiled=True)  5.73 us
    ppermute x6, waiting for transfers between devices, local(): fwd = tuple((lax.ppermute(part, 'chip', up) for part in fwd))  5.66 us
    all_to_all x1, starting transfers between devices, local(): query_cols = rel_rows = lax.all_to_all(shared, 'chip', 0, 0, tiled=True)  4.73 us
  transfers between devices with their start and end apart: 22, of which 8 were waited for; matrix products, arithmetic and copies ran while one was open for 8% of the time, Pallas kernels for 14%

profile of v3, /device:TPU:9, one launch (start us, length us, event | category | flops | bytes accessed | tf_op | source)
XLA Modules:
  0.0 126.1 jit_solution(6444754857062620678)
XLA Ops:
  0.6 1.4 %fusion.onehot_at = bf16[128,256]{1,0:T(8,128)(2,1)} fusion(s32[128]{0:T(128)} %param.7), kind=kLoop, calls=%fused_computation.10 | loop fusion | flops 65536 | bytes 66048 | tf_op jit(solution)/shard_map/convert_element_type | solution.py:241
  2.1 8.5 %shard_map.67 = (bf16[2,128,1024]{2,1,0:T(8,128)(2,1)}, bf16[8,128,256]{2,1,0:T(8,128)(2,1)}, bf16[2,128,1024]{2,1,0:T(8,128)(2,1)}) custom-call(bf16[128,2048]{1,0:T(8,128)(2,1)} %bitcast.30, bf16[2048,2048]{1,0:T(8,128)(2,1)} %bitcast.28, bf16[128,256]{1,0:T(8,128)(2,1)} %fusion.onehot_at, bf16[256,2048]{1,0:T(8,128)(2,1)} %table_at.1), custom_call_target="tpu_custom_call" | custom-call | flops 1207959552 | bytes 8388608 | tf_op jit(solution)/shard_map/pallas_call | solution.py:43
  10.5 3.1 %collective-permute-start = (bf16[2,128,1024]{2,1,0:T(8,128)(2,1)}, bf16[2,128,1024]{2,1,0:T(8,128)(2,1)S(1)}, u32[]{:S(2)}, u32[]{:S(2)}) collective-permute-start(bf16[2,128,1024]{2,1,0:T(8,128)(2,1)} %get-tuple-element.20), channel_id=1, source_target_pairs={{0,16},{1,17},{2,18},{3,19},{4,20},{5,21},{6,22},{7,23},{8,24},{9,... | collective-permute-start | bytes 1572872 | tf_op jit(solution)/shard_map/ppermute | solution.py:251
  13.7 5.7 %all-to-all-start = ((bf16[8,128,256]{2,1,0:T(8,128)(2,1)}), bf16[8,128,256]{2,1,0:T(8,128)(2,1)}, u32[]{:S(2)}, u32[]{:S(2)}) async-start(bf16[8,128,256]{2,1,0:T(8,128)(2,1)} %get-tuple-element.25), calls=%async_computation | async-start | bytes 1048576 | tf_op jit(solution)/shard_map/all_to_all | solution.py:252
  19.4 0.7 compare_convert_fusion.onehot_at
  20.2 4.4 %collective-permute-done.query_at = bf16[2,128,1024]{2,1,0:T(8,128)(2,1)S(1)} collective-permute-done((bf16[2,128,1024]{2,1,0:T(8,128)(2,1)}, bf16[2,128,1024]{2,1,0:T(8,128)(2,1)S(1)}, u32[]{:S(2)}, u32[]{:S(2)}) %collective-permute-start) | collective-permute-done | bytes 524320 | tf_op jit(solution)/shard_map/ppermute | solution.py:251
  24.6 0.8 copy-done.8
  25.3 13.4 %shard_map.68 = (bf16[128,2048]{1,0:T(8,128)(2,1)}, bf16[128,2048]{1,0:T(8,128)(2,1)}, f32[128,2048]{1,0:T(8,128)}, f32[128,2048]{1,0:T(8,128)}) custom-call(s32[1]{0:T(128)} %bitcast.3.first, bf16[2,128,1024]{2,1,0:T(8,128)(2,1)} %copy-done.8, bf16[128,2048]{1,0:T(8,128)(2,1)} %bitcast.31, bf16[2048,2048]{1,0:T(8,128)(2,1)} %bitcast.29, ...), custom_call_target="tpu_custom_call" | custom-call | flops 2415919104 | bytes 16777216 | tf_op jit(solution)/shard_map/pallas_call | solution.py:43
  38.7 1.6 %collective-permute-start.2 = (f32[128,2048]{1,0:T(8,128)}, f32[128,2048]{1,0:T(8,128)}, u32[]{:S(2)}, u32[]{:S(2)}) collective-permute-start(f32[128,2048]{1,0:T(8,128)} %get-tuple-element.24), channel_id=1, source_target_pairs={{0,1},{1,0},{2,3},{3,2},{4,5},{5,4},{6,7},{7,6},{8,9},{9,8},{10,11... | collective-permute-start | bytes 3145736 | tf_op jit(solution)/shard_map/ppermute | solution.py:19
  40.4 1.3 %collective-permute-start.1 = (bf16[128,2048]{1,0:T(8,128)(2,1)}, bf16[128,2048]{1,0:T(8,128)(2,1)S(1)}, u32[]{:S(2)}, u32[]{:S(2)}) collective-permute-start(bf16[128,2048]{1,0:T(8,128)(2,1)} %get-tuple-element.22), channel_id=1, source_target_pairs={{16,0},{17,1},{18,2},{19,3},{20,4},{21,5},{22,6},{23,7},{24,8},{25... | collective-permute-start | bytes 1572872 | tf_op jit(solution)/shard_map/ppermute | solution.py:257
  41.7 1.8 %fusion.5 = (bf16[64,2048]{1,0:T(8,128)(2,1)}, bf16[64,2048]{1,0:T(8,128)(2,1)S(1)}) fusion(bf16[128,2048]{1,0:T(8,128)(2,1)} %get-tuple-element.27.refs_2_), kind=kLoop, calls=%fused_computation.36 | loop fusion | bytes 1048576 | tf_op jit(solution)/shard_map/slice | solution.py:272
  43.5 1.3 %collective-permute-start.3 = (bf16[64,2048]{1,0:T(8,128)(2,1)S(1)}, bf16[64,2048]{1,0:T(8,128)(2,1)S(1)}, u32[]{:S(2)}, u32[]{:S(2)}) collective-permute-start(bf16[64,2048]{1,0:T(8,128)(2,1)S(1)} %get-tuple-element.37), channel_id=1, source_target_pairs={{0,4},{4,8},{8,12},{12,14},{14,10},{10,6},{6,2},{2,0},{1,5},{5,9},... | collective-permute-start | bytes 786440 | tf_op jit(solution)/shard_map/ppermute | solution.py:275
  44.7 0.2 collective-permute-start.5
  44.9 4.0 %collective-permute-start.7 = (bf16[8,128,256]{2,1,0:T(8,128)(2,1)}, bf16[8,128,256]{2,1,0:T(8,128)(2,1)S(1)}, u32[]{:S(2)}, u32[]{:S(2)}) collective-permute-start(bf16[8,128,256]{2,1,0:T(8,128)(2,1)} %all-to-all-done), channel_id=1, source_target_pairs={{0,16},{1,17},{2,18},{3,19},{4,20},{5,21},{6,22},{7,23},{8,24},{9,... | collective-permute-start | bytes 1572872 | tf_op jit(solution)/shard_map/ppermute | solution.py:260
  49.0 6.9 %collective-permute-done.1 = bf16[128,2048]{1,0:T(8,128)(2,1)S(1)} collective-permute-done((bf16[128,2048]{1,0:T(8,128)(2,1)}, bf16[128,2048]{1,0:T(8,128)(2,1)S(1)}, u32[]{:S(2)}, u32[]{:S(2)}) %collective-permute-start.1) | collective-permute-done | bytes 524320 | tf_op jit(solution)/shard_map/ppermute | solution.py:257
  55.8 0.3 copy.8
  56.1 0.2 copy.9
  56.4 1.4 %collective-permute-start.4 = (bf16[64,2048]{1,0:T(8,128)(2,1)S(1)}, bf16[64,2048]{1,0:T(8,128)(2,1)S(1)}, u32[]{:S(2)}, u32[]{:S(2)}) collective-permute-start(bf16[64,2048]{1,0:T(8,128)(2,1)S(1)} %collective-permute-done.3.refs_3_), channel_id=1, source_target_pairs={{0,4},{4,8},{8,12},{12,14},{14,10},{10,6},{6,2},{2,0},{1,5},{5,9},... | collective-permute-start | bytes 786440 | tf_op jit(solution)/shard_map/ppermute | solution.py:275
  57.7 0.2 collective-permute-start.6
  57.9 1.7 %add_convert_fusion = bf16[128,2048]{1,0:T(8,128)(2,1)S(1)} fusion(f32[128,2048]{1,0:T(8,128)} %get-tuple-element.23, f32[128,2048]{1,0:T(8,128)} %collective-permute-done.2), kind=kLoop, calls=%fused_computation.2 | loop fusion | flops 524288 | bytes 2621440 | tf_op jit(solution)/shard_map/convert_element_type | solution.py:282
  59.8 0.9 bitcast_select_fusion
  60.7 2.6 %collective-permute-done.4.refs_7_ = bf16[64,2048]{1,0:T(8,128)(2,1)S(1)} collective-permute-done((bf16[64,2048]{1,0:T(8,128)(2,1)S(1)}, bf16[64,2048]{1,0:T(8,128)(2,1)S(1)}, u32[]{:S(2)}, u32[]{:S(2)}) %collective-permute-start.4) | collective-permute-done | bytes 262176 | tf_op jit(solution)/shard_map/ppermute | solution.py:275
  63.3 1.0 collective-permute-done.6.refs_9_
  64.3 4.7 %all-to-all-start.1 = ((bf16[8,128,256]{2,1,0:T(8,128)(2,1)}), bf16[8,128,256]{2,1,0:T(8,128)(2,1)}, u32[]{:S(2)}, u32[]{:S(2)}) async-start(bf16[8,128,256]{2,1,0:T(8,128)(2,1)} %bitcast_select_fusion), calls=%async_computation.1 | async-start | bytes 1048576 | tf_op jit(solution)/shard_map/all_to_all | solution.py:287
  69.0 1.4 %collective-permute-start.10 = (bf16[64,2048]{1,0:T(8,128)(2,1)}, bf16[64,2048]{1,0:T(8,128)(2,1)S(1)}, u32[]{:S(2)}, u32[]{:S(2)}) collective-permute-start(bf16[64,2048]{1,0:T(8,128)(2,1)} %get-tuple-element.36), channel_id=1, source_target_pairs={{0,4},{4,8},{8,12},{12,14},{14,10},{10,6},{6,2},{2,0},{1,5},{5,9},... | collective-permute-start | bytes 786440 | tf_op jit(solution)/shard_map/ppermute | solution.py:275
  70.5 15.9 %collective-permute-done.14.refs_6_ = bf16[64,2048]{1,0:T(8,128)(2,1)S(1)} collective-permute-done((bf16[64,2048]{1,0:T(8,128)(2,1)}, bf16[64,2048]{1,0:T(8,128)(2,1)S(1)}, u32[]{:S(2)}, u32[]{:S(2)}) %collective-permute-start.14) | collective-permute-done | bytes 262176 | tf_op jit(solution)/shard_map/ppermute | solution.py:276
  86.4 1.5 %collective-permute-start.11 = (bf16[64,2048]{1,0:T(8,128)(2,1)S(1)}, bf16[64,2048]{1,0:T(8,128)(2,1)}, u32[]{:S(2)}, u32[]{:S(2)}) collective-permute-start(bf16[64,2048]{1,0:T(8,128)(2,1)S(1)} %collective-permute-done.10.refs_4_), channel_id=1, source_target_pairs={{0,4},{4,8},{8,12},{12,14},{14,10},{10,6},{6,2},{2,0},{1,5},{5,9},... | collective-permute-start | bytes 786440 | tf_op jit(solution)/shard_map/ppermute | solution.py:275
  87.9 3.7 %collective-permute-done.15.refs_10_ = bf16[64,2048]{1,0:T(8,128)(2,1)S(1)} collective-permute-done((bf16[64,2048]{1,0:T(8,128)(2,1)S(1)}, bf16[64,2048]{1,0:T(8,128)(2,1)S(1)}, u32[]{:S(2)}, u32[]{:S(2)}) %collective-permute-start.15) | collective-permute-done | bytes 262176 | tf_op jit(solution)/shard_map/ppermute | solution.py:276
  91.6 0.4 collective-permute-start.16
  92.0 0.7 copy-done.4
  92.8 1.0 collective-permute-start.13
  93.8 0.5 collective-permute-start.12
  94.3 3.0 %collective-permute-done.9.refs_2_ = bf16[64,2048]{1,0:T(8,128)(2,1)S(1)} collective-permute-done((bf16[64,2048]{1,0:T(8,128)(2,1)S(1)}, bf16[64,2048]{1,0:T(8,128)(2,1)S(1)}, u32[]{:S(2)}, u32[]{:S(2)}) %collective-permute-start.9) | collective-permute-done | bytes 262176 | tf_op jit(solution)/shard_map/ppermute | solution.py:275
  97.4 1.1 collective-permute-start.17
  98.5 0.8 collective-permute-start.18
  99.3 1.2 convert_reduce_fusion
  100.6 1.3 %collective-permute-start.8 = (f32[8,2048]{1,0:T(8,128)S(1)}, f32[8,2048]{1,0:T(8,128)S(1)}, u32[]{:S(2)}, u32[]{:S(2)}) collective-permute-start(f32[8,2048]{1,0:T(8,128)S(1)} %bitcast.37), channel_id=1, source_target_pairs={{16,0},{17,1},{18,2},{19,3},{20,4},{21,5},{22,6},{23,7},{24,8},{25... | collective-permute-start | bytes 196616 | tf_op jit(solution)/shard_map/ppermute | solution.py:293
  101.9 1.1 broadcast_select_fusion.1
  103.1 0.9 copy-done.3
  104.1 0.9 copy-done.5
  105.0 4.8 %shard_map.69 = (f32[128,2048]{1,0:T(8,128)S(1)}, f32[128,2048]{1,0:T(8,128)S(1)}) custom-call(s32[5]{0:T(128)S(1)} %stack.39.refs_0_, bf16[8,128,256]{2,1,0:T(8,128)(2,1)S(1)} %pad_maximum_fusion.refs_1_, bf16[128,2048]{1,0:T(8,128)(2,1)S(1)} %copy-done, bf16[64,2048]{1,0:T(8,128)(2,1)S(1)} %collective-permute-done.3.refs_3_, ...), custom_call_target="tpu_custom_call" | custom-call | flops 671088640 | bytes 2621440 | tf_op jit(solution)/shard_map/pallas_call | solution.py:43
  109.9 1.0 copy-done.1
  110.8 0.6 broadcast_select_fusion.4
  111.5 4.6 %shard_map.70 = (f32[128,2048]{1,0:T(8,128)S(1)}, f32[128,2048]{1,0:T(8,128)S(1)}) custom-call(s32[3]{0:T(128)S(1)} %pad_add_fusion.refs_0_, bf16[8,128,256]{2,1,0:T(8,128)(2,1)S(1)} %pad_maximum_fusion.refs_1_, bf16[64,2048]{1,0:T(8,128)(2,1)S(1)} %collective-permute-done.9.refs_2_, bf16[64,2048]{1,0:T(8,128)(2,1)S(1)} %collective-permute-done.12.refs_3_, ...), custom_call_target="tpu_custom_call" | custom-call | flops 402653184 | bytes 1572864 | tf_op jit(solution)/shard_map/pallas_call | solution.py:43
  116.1 6.6 %collective-permute-start.19 = (f32[128,2048]{1,0:T(8,128)S(1)}, f32[128,2048]{1,0:T(8,128)S(1)}, u32[]{:S(2)}, u32[]{:S(2)}) collective-permute-start(f32[128,2048]{1,0:T(8,128)S(1)} %get-tuple-element.34), channel_id=1, source_target_pairs={{0,1},{1,0},{2,3},{3,2},{4,5},{5,4},{6,7},{7,6},{8,9},{9,8},{10,11... | collective-permute-start | bytes 3145736 | tf_op jit(solution)/shard_map/ppermute | solution.py:19
  122.7 0.8 broadcast_select_fusion
  123.6 1.4 %collective-permute-done.19 = f32[128,2048]{1,0:T(8,128)S(1)} collective-permute-done((f32[128,2048]{1,0:T(8,128)S(1)}, f32[128,2048]{1,0:T(8,128)S(1)}, u32[]{:S(2)}, u32[]{:S(2)}) %collective-permute-start.19) | collective-permute-done | bytes 1048608 | tf_op jit(solution)/shard_map/ppermute | solution.py:19
  125.0 1.1 multiply_bitcast_fusion
  (45 shorter events, 0.7 us)
Async XLA Ops:
  0.6 18.8 %copy-start.11 = (s32[128]{0:T(128)S(1)}, s32[128]{0:T(128)}, u32[]{:S(2)}) copy-start(s32[128]{0:T(128)} %param.7) | copy-start | bytes 1540
  10.5 14.0 %collective-permute-start = (bf16[2,128,1024]{2,1,0:T(8,128)(2,1)}, bf16[2,128,1024]{2,1,0:T(8,128)(2,1)S(1)}, u32[]{:S(2)}, u32[]{:S(2)}) collective-permute-start(bf16[2,128,1024]{2,1,0:T(8,128)(2,1)} %get-tuple-element.20), channel_id=1, source_target_pairs={{0,16},{1,17},{2,18},{3,19},{4,20},{5,21},{6,22},{7,23},{8,24},{9,... | collective-permute-start | bytes 1572872 | tf_op jit(solution)/shard_map/ppermute | solution.py:251
  13.7 27.9 %all-to-all-start = ((bf16[8,128,256]{2,1,0:T(8,128)(2,1)}), bf16[8,128,256]{2,1,0:T(8,128)(2,1)}, u32[]{:S(2)}, u32[]{:S(2)}) async-start(bf16[8,128,256]{2,1,0:T(8,128)(2,1)} %get-tuple-element.25), calls=%async_computation | async-start | bytes 1048576 | tf_op jit(solution)/shard_map/all_to_all | solution.py:252
  24.6 0.8 copy-start.8
  38.7 64.4 %copy-start = (bf16[128,2048]{1,0:T(8,128)(2,1)S(1)}, bf16[128,2048]{1,0:T(8,128)(2,1)}, u32[]{:S(2)}) copy-start(bf16[128,2048]{1,0:T(8,128)(2,1)} %get-tuple-element.27.refs_2_) | copy-start | bytes 1572868
  38.7 19.1 %collective-permute-start.2 = (f32[128,2048]{1,0:T(8,128)}, f32[128,2048]{1,0:T(8,128)}, u32[]{:S(2)}, u32[]{:S(2)}) collective-permute-start(f32[128,2048]{1,0:T(8,128)} %get-tuple-element.24), channel_id=1, source_target_pairs={{0,1},{1,0},{2,3},{3,2},{4,5},{5,4},{6,7},{7,6},{8,9},{9,8},{10,11... | collective-permute-start | bytes 3145736 | tf_op jit(solution)/shard_map/ppermute | solution.py:19
  40.4 15.5 %collective-permute-start.1 = (bf16[128,2048]{1,0:T(8,128)(2,1)}, bf16[128,2048]{1,0:T(8,128)(2,1)S(1)}, u32[]{:S(2)}, u32[]{:S(2)}) collective-permute-start(bf16[128,2048]{1,0:T(8,128)(2,1)} %get-tuple-element.22), channel_id=1, source_target_pairs={{16,0},{17,1},{18,2},{19,3},{20,4},{21,5},{22,6},{23,7},{24,8},{25... | collective-permute-start | bytes 1572872 | tf_op jit(solution)/shard_map/ppermute | solution.py:257
  43.5 12.9 %collective-permute-start.3 = (bf16[64,2048]{1,0:T(8,128)(2,1)S(1)}, bf16[64,2048]{1,0:T(8,128)(2,1)S(1)}, u32[]{:S(2)}, u32[]{:S(2)}) collective-permute-start(bf16[64,2048]{1,0:T(8,128)(2,1)S(1)} %get-tuple-element.37), channel_id=1, source_target_pairs={{0,4},{4,8},{8,12},{12,14},{14,10},{10,6},{6,2},{2,0},{1,5},{5,9},... | collective-permute-start | bytes 786440 | tf_op jit(solution)/shard_map/ppermute | solution.py:275
  44.7 13.0 %collective-permute-start.5 = (bf16[64,2048]{1,0:T(8,128)(2,1)S(1)}, bf16[64,2048]{1,0:T(8,128)(2,1)S(1)}, u32[]{:S(2)}, u32[]{:S(2)}) collective-permute-start(bf16[64,2048]{1,0:T(8,128)(2,1)S(1)} %get-tuple-element.37), channel_id=1, source_target_pairs={{4,0},{8,4},{12,8},{14,12},{10,14},{6,10},{2,6},{0,2},{5,1},{9,5},... | collective-permute-start | bytes 786440 | tf_op jit(solution)/shard_map/ppermute | solution.py:276
  44.9 19.4 %collective-permute-start.7 = (bf16[8,128,256]{2,1,0:T(8,128)(2,1)}, bf16[8,128,256]{2,1,0:T(8,128)(2,1)S(1)}, u32[]{:S(2)}, u32[]{:S(2)}) collective-permute-start(bf16[8,128,256]{2,1,0:T(8,128)(2,1)} %all-to-all-done), channel_id=1, source_target_pairs={{0,16},{1,17},{2,18},{3,19},{4,20},{5,21},{6,22},{7,23},{8,24},{9,... | collective-permute-start | bytes 1572872 | tf_op jit(solution)/shard_map/ppermute | solution.py:260
  55.8 2.0 %copy-start.6 = (bf16[128,2048]{1,0:T(8,128)(2,1)}, bf16[128,2048]{1,0:T(8,128)(2,1)S(1)}, u32[]{:S(2)}) copy-start(bf16[128,2048]{1,0:T(8,128)(2,1)S(1)} %collective-permute-done.1) | copy-start | bytes 1572868
  56.4 6.9 %collective-permute-start.4 = (bf16[64,2048]{1,0:T(8,128)(2,1)S(1)}, bf16[64,2048]{1,0:T(8,128)(2,1)S(1)}, u32[]{:S(2)}, u32[]{:S(2)}) collective-permute-start(bf16[64,2048]{1,0:T(8,128)(2,1)S(1)} %collective-permute-done.3.refs_3_), channel_id=1, source_target_pairs={{0,4},{4,8},{8,12},{12,14},{14,10},{10,6},{6,2},{2,0},{1,5},{5,9},... | collective-permute-start | bytes 786440 | tf_op jit(solution)/shard_map/ppermute | solution.py:275
  57.7 6.6 %collective-permute-start.6 = (bf16[64,2048]{1,0:T(8,128)(2,1)S(1)}, bf16[64,2048]{1,0:T(8,128)(2,1)S(1)}, u32[]{:S(2)}, u32[]{:S(2)}) collective-permute-start(bf16[64,2048]{1,0:T(8,128)(2,1)S(1)} %collective-permute-done.5.refs_5_), channel_id=1, source_target_pairs={{4,0},{8,4},{12,8},{14,12},{10,14},{6,10},{2,6},{0,2},{5,1},{9,5},... | collective-permute-start | bytes 786440 | tf_op jit(solution)/shard_map/ppermute | solution.py:276
  64.3 28.5 %copy-start.10 = (bf16[8,128,256]{2,1,0:T(8,128)(2,1)}, bf16[8,128,256]{2,1,0:T(8,128)(2,1)S(1)}, u32[]{:S(2)}) copy-start(bf16[8,128,256]{2,1,0:T(8,128)(2,1)S(1)} %collective-permute-done.7) | copy-start | bytes 1572868
  64.3 35.0 %all-to-all-start.1 = ((bf16[8,128,256]{2,1,0:T(8,128)(2,1)}), bf16[8,128,256]{2,1,0:T(8,128)(2,1)}, u32[]{:S(2)}, u32[]{:S(2)}) async-start(bf16[8,128,256]{2,1,0:T(8,128)(2,1)} %bitcast_select_fusion), calls=%async_computation.1 | async-start | bytes 1048576 | tf_op jit(solution)/shard_map/all_to_all | solution.py:287
  69.0 17.3 %collective-permute-start.14 = (bf16[64,2048]{1,0:T(8,128)(2,1)}, bf16[64,2048]{1,0:T(8,128)(2,1)S(1)}, u32[]{:S(2)}, u32[]{:S(2)}) collective-permute-start(bf16[64,2048]{1,0:T(8,128)(2,1)} %get-tuple-element.36), channel_id=1, source_target_pairs={{4,0},{8,4},{12,8},{14,12},{10,14},{6,10},{2,6},{0,2},{5,1},{9,5},... | collective-permute-start | bytes 786440 | tf_op jit(solution)/shard_map/ppermute | solution.py:276
  69.0 17.3 %collective-permute-start.10 = (bf16[64,2048]{1,0:T(8,128)(2,1)}, bf16[64,2048]{1,0:T(8,128)(2,1)S(1)}, u32[]{:S(2)}, u32[]{:S(2)}) collective-permute-start(bf16[64,2048]{1,0:T(8,128)(2,1)} %get-tuple-element.36), channel_id=1, source_target_pairs={{0,4},{4,8},{8,12},{12,14},{14,10},{10,6},{6,2},{2,0},{1,5},{5,9},... | collective-permute-start | bytes 786440 | tf_op jit(solution)/shard_map/ppermute | solution.py:275
  86.4 5.2 %collective-permute-start.15 = (bf16[64,2048]{1,0:T(8,128)(2,1)S(1)}, bf16[64,2048]{1,0:T(8,128)(2,1)S(1)}, u32[]{:S(2)}, u32[]{:S(2)}) collective-permute-start(bf16[64,2048]{1,0:T(8,128)(2,1)S(1)} %collective-permute-done.14.refs_6_), channel_id=1, source_target_pairs={{4,0},{8,4},{12,8},{14,12},{10,14},{6,10},{2,6},{0,2},{5,1},{9,5},... | collective-permute-start | bytes 786440 | tf_op jit(solution)/shard_map/ppermute | solution.py:276
  86.4 7.4 %copy-start.2 = (bf16[64,2048]{1,0:T(8,128)(2,1)}, bf16[64,2048]{1,0:T(8,128)(2,1)S(1)}, u32[]{:S(2)}) copy-start(bf16[64,2048]{1,0:T(8,128)(2,1)S(1)} %collective-permute-done.10.refs_4_) | copy-start | bytes 786436
  86.4 7.4 %collective-permute-start.11 = (bf16[64,2048]{1,0:T(8,128)(2,1)S(1)}, bf16[64,2048]{1,0:T(8,128)(2,1)}, u32[]{:S(2)}, u32[]{:S(2)}) collective-permute-start(bf16[64,2048]{1,0:T(8,128)(2,1)S(1)} %collective-permute-done.10.refs_4_), channel_id=1, source_target_pairs={{0,4},{4,8},{8,12},{12,14},{14,10},{10,6},{6,2},{2,0},{1,5},{5,9},... | collective-permute-start | bytes 786440 | tf_op jit(solution)/shard_map/ppermute | solution.py:275
  87.8 9.5 %collective-permute-start.9 = (bf16[64,2048]{1,0:T(8,128)(2,1)S(1)}, bf16[64,2048]{1,0:T(8,128)(2,1)S(1)}, u32[]{:S(2)}, u32[]{:S(2)}) collective-permute-start(bf16[64,2048]{1,0:T(8,128)(2,1)S(1)} %collective-permute-done.4.refs_7_), channel_id=1, source_target_pairs={{0,4},{4,8},{8,12},{12,14},{14,10},{10,6},{6,2},{2,0},{1,5},{5,9},... | collective-permute-start | bytes 786440 | tf_op jit(solution)/shard_map/ppermute | solution.py:275
  91.6 6.9 %collective-permute-start.16 = (bf16[64,2048]{1,0:T(8,128)(2,1)S(1)}, bf16[64,2048]{1,0:T(8,128)(2,1)S(1)}, u32[]{:S(2)}, u32[]{:S(2)}) collective-permute-start(bf16[64,2048]{1,0:T(8,128)(2,1)S(1)} %collective-permute-done.15.refs_10_), channel_id=1, source_target_pairs={{4,0},{8,4},{12,8},{14,12},{10,14},{6,10},{2,6},{0,2},{5,1},{9,5},... | collective-permute-start | bytes 786440 | tf_op jit(solution)/shard_map/ppermute | solution.py:276
  92.0 0.7 copy-start.4
  92.8 18.6 %collective-permute-start.13 = (bf16[64,2048]{1,0:T(8,128)(2,1)S(1)}, bf16[64,2048]{1,0:T(8,128)(2,1)S(1)}, u32[]{:S(2)}, u32[]{:S(2)}) collective-permute-start(bf16[64,2048]{1,0:T(8,128)(2,1)S(1)} %collective-permute-done.6.refs_9_), channel_id=1, source_target_pairs={{4,0},{8,4},{12,8},{14,12},{10,14},{6,10},{2,6},{0,2},{5,1},{9,5},... | collective-permute-start | bytes 786440 | tf_op jit(solution)/shard_map/ppermute | solution.py:276
  93.8 17.7 %collective-permute-start.12 = (bf16[64,2048]{1,0:T(8,128)(2,1)}, bf16[64,2048]{1,0:T(8,128)(2,1)S(1)}, u32[]{:S(2)}, u32[]{:S(2)}) collective-permute-start(bf16[64,2048]{1,0:T(8,128)(2,1)} %collective-permute-done.11.refs_8_), channel_id=1, source_target_pairs={{0,4},{4,8},{8,12},{12,14},{14,10},{10,6},{6,2},{2,0},{1,5},{5,9},... | collective-permute-start | bytes 786440 | tf_op jit(solution)/shard_map/ppermute | solution.py:275
  97.4 14.1 %collective-permute-start.17 = (bf16[64,2048]{1,0:T(8,128)(2,1)S(1)}, bf16[64,2048]{1,0:T(8,128)(2,1)S(1)}, u32[]{:S(2)}, u32[]{:S(2)}) collective-permute-start(bf16[64,2048]{1,0:T(8,128)(2,1)S(1)} %collective-permute-done.9.refs_2_), channel_id=1, source_target_pairs={{0,4},{4,8},{8,12},{12,14},{14,10},{10,6},{6,2},{2,0},{1,5},{5,9},... | collective-permute-start | bytes 786440 | tf_op jit(solution)/shard_map/ppermute | solution.py:279
  98.5 13.0 %collective-permute-start.18 = (bf16[64,2048]{1,0:T(8,128)(2,1)S(1)}, bf16[64,2048]{1,0:T(8,128)(2,1)S(1)}, u32[]{:S(2)}, u32[]{:S(2)}) collective-permute-start(bf16[64,2048]{1,0:T(8,128)(2,1)S(1)} %collective-permute-done.16.refs_5_), channel_id=1, source_target_pairs={{4,0},{8,4},{12,8},{14,12},{10,14},{6,10},{2,6},{0,2},{5,1},{9,5},... | collective-permute-start | bytes 786440 | tf_op jit(solution)/shard_map/ppermute | solution.py:279
  99.3 23.4 %copy-start.7 = (bf16[128,2048]{1,0:T(8,128)(2,1)S(1)}, bf16[128,2048]{1,0:T(8,128)(2,1)}, u32[]{:S(2)}) copy-start(bf16[128,2048]{1,0:T(8,128)(2,1)} %copy-done.6) | copy-start | bytes 1572868
  99.3 23.4 %copy-start.9 = (bf16[128,2048]{1,0:T(8,128)(2,1)S(1)}, bf16[128,2048]{1,0:T(8,128)(2,1)}, u32[]{:S(2)}) copy-start(bf16[128,2048]{1,0:T(8,128)(2,1)} %get-tuple-element.22) | copy-start | bytes 1572868
  100.6 10.3 %collective-permute-start.8 = (f32[8,2048]{1,0:T(8,128)S(1)}, f32[8,2048]{1,0:T(8,128)S(1)}, u32[]{:S(2)}, u32[]{:S(2)}) collective-permute-start(f32[8,2048]{1,0:T(8,128)S(1)} %bitcast.37), channel_id=1, source_target_pairs={{16,0},{17,1},{18,2},{19,3},{20,4},{21,5},{22,6},{23,7},{24,8},{25... | collective-permute-start | bytes 196616 | tf_op jit(solution)/shard_map/ppermute | solution.py:293
  103.1 1.0 copy-start.3
  104.1 0.9 copy-start.5
  109.9 1.0 copy-start.1
  116.1 8.9 %collective-permute-start.19 = (f32[128,2048]{1,0:T(8,128)S(1)}, f32[128,2048]{1,0:T(8,128)S(1)}, u32[]{:S(2)}, u32[]{:S(2)}) collective-permute-start(f32[128,2048]{1,0:T(8,128)S(1)} %get-tuple-element.34), channel_id=1, source_target_pairs={{0,1},{1,0},{2,3},{3,2},{4,5},{5,4},{6,7},{7,6},{8,9},{9,8},{10,11... | collective-permute-start | bytes 3145736 | tf_op jit(solution)/shard_map/ppermute | solution.py:19

commit v4 on v1

--- a/solution.py
+++ b/solution.py
@@ -83,17 +83,15 @@
     return query, mixed, rel
 
 
-def trail_body(first, query, rows, weight, rel, onehot, right, query_grad, give, keep, mixed, hidden, held, sems):
-    width = weight.shape[0]
+def hidden_body(first, query, rows, weight_at, rel, right, mixed, weight, sems):
+    width, hidden = weight.shape
     half = width // 2
     is_first = first[0] == 1
-    owned = give.shape[0]
-    tiles = weight.shape[1] // TILE
 
     def load(step):
-        return pltpu.make_async_copy(weight.at[:, at(step)], held.at[:, at(step)], sems.at[step])
-
-    for step in range(tiles):
+        return pltpu.make_async_copy(weight_at.at[:, at(step)], weight.at[:, at(step)], sems.at[step])
+
+    for step in range(hidden // TILE):
         load(step).start()
 
     def make_mixed(step, carry):
@@ -107,19 +105,33 @@
 
     def make_hidden(step, carry):
         load(step).wait()
-        pre = dot(mixed[...], held[:, at(step)], 1, 0)
+        pre = dot(mixed[...], weight[:, at(step)], 1, 0)
         sig = jax.nn.sigmoid(pre)
         cot = rows[:, at(step)]
         grad = (cot.astype(F32) * (sig * (1.0 + pre * (1.0 - sig)))).astype(BF16)
-        hidden[:, at(step)] = grad
         right[:, at(step)] = jnp.where(is_first, cot, grad)
         return carry
 
-    lax.fori_loop(0, tiles, make_hidden, 0)
+    lax.fori_loop(0, hidden // TILE, make_hidden, 0)
+
+
+def query_body(hidden, query, weight_at, rel, onehot, query_grad, give, keep, weight, sems):
+    half = weight.shape[0] // 2
+    owned = give.shape[0]
+
+    def load(step, side):
+        piece = at(step, side * half)
+        return pltpu.make_async_copy(weight_at.at[piece], weight.at[piece], sems.at[2 * step + side])
+
+    for step in range(half // TILE):
+        for side in range(2):
+            load(step, side).start()
 
     def make_query(step, carry):
-        gz_re = dot(hidden[...], held[at(step), :], 1, 1)
-        gz_im = dot(hidden[...], held[at(step, half), :], 1, 1)
+        load(step, 0).wait()
+        gz_re = dot(hidden[...], weight[at(step), :], 1, 1)
+        load(step, 1).wait()
+        gz_im = dot(hidden[...], weight[at(step, half), :], 1, 1)
         r_re, r_im = rel[0, :, at(step)].astype(F32), rel[1, :, at(step)].astype(F32)
         query_grad[:, at(step)] = (gz_re * r_re + gz_im * r_im).astype(BF16)
         query_grad[:, at(step, half)] = (gz_im * r_re - gz_re * r_im).astype(BF16)
@@ -135,33 +147,47 @@
     lax.fori_loop(0, half // TILE, make_query, 0)
 
 
-def trail(first, query, rows, weight, rel, onehot):
+VMEM = pl.BlockSpec(memory_space=pltpu.VMEM)
+LARGE = pl.BlockSpec(memory_space=pltpu.HBM)
+
+
+def hidden_grad(first, query, rows, weight, rel):
     rows_dev, hidden = rows.shape
     width = weight.shape[0]
-    count_rel = onehot.shape[0]
-    vmem = pl.BlockSpec(memory_space=pltpu.VMEM)
-    flops = 4 * rows_dev * width * hidden + 4 * rows_dev * count_rel * width
     return pl.pallas_call(
-        trail_body,
-        out_shape=(
-            jax.ShapeDtypeStruct((rows_dev, hidden), BF16),
-            jax.ShapeDtypeStruct((rows_dev, width), BF16),
-            jax.ShapeDtypeStruct((count_rel // 2, width), F32),
-            jax.ShapeDtypeStruct((count_rel // 2, width), F32),
-        ),
-        in_specs=[pl.BlockSpec(memory_space=pltpu.SMEM), vmem, vmem, pl.BlockSpec(memory_space=pltpu.HBM), vmem, vmem],
-        out_specs=(vmem,) * 4,
+        hidden_body,
+        out_shape=jax.ShapeDtypeStruct((rows_dev, hidden), BF16),
+        in_specs=[pl.BlockSpec(memory_space=pltpu.SMEM), VMEM, VMEM, LARGE, VMEM],
+        out_specs=VMEM,
         scratch_shapes=[
             pltpu.VMEM((rows_dev, width), BF16),
-            pltpu.VMEM((rows_dev, hidden), BF16),
             pltpu.VMEM((width, hidden), BF16),
             pltpu.SemaphoreType.DMA((hidden // TILE,)),
         ],
         compiler_params=pltpu.CompilerParams(vmem_limit_bytes=56 * 1024 * 1024),
         cost_estimate=pl.CostEstimate(
-            flops=flops, bytes_accessed=2 * width * hidden, transcendentals=rows_dev * hidden
+            flops=2 * rows_dev * width * hidden, bytes_accessed=2 * width * hidden, transcendentals=rows_dev * hidden
         ),
-    )(first, query, rows, weight, rel, onehot)
+    )(first, query, rows, weight, rel)
+
+
+def query_and_relation_grad(hidden, query, weight, rel, onehot):
+    rows_dev = hidden.shape[0]
+    width = weight.shape[0]
+    count_rel = onehot.shape[0]
+    partial = jax.ShapeDtypeStruct((count_rel // 2, width), F32)
+    return pl.pallas_call(
+        query_body,
+        out_shape=(jax.ShapeDtypeStruct((rows_dev, width), BF16), partial, partial),
+        in_specs=[VMEM, VMEM, LARGE, VMEM, VMEM],
+        out_specs=(VMEM,) * 3,
+        scratch_shapes=[pltpu.VMEM(weight.shape, BF16), pltpu.SemaphoreType.DMA((width // TILE,))],
+        compiler_params=pltpu.CompilerParams(vmem_limit_bytes=56 * 1024 * 1024),
+        cost_estimate=pl.CostEstimate(
+            flops=2 * rows_dev * width * (weight.shape[1] + 2 * count_rel),
+            bytes_accessed=2 * width * weight.shape[1], transcendentals=0,
+        ),
+    )(hidden, query, weight, rel, onehot)
 
 
 def local(section_rows, weights, relation_table, relation_ids):
@@ -193,11 +219,10 @@
     own_query, own_mixed, rel = lead(rows, weight, onehot, relation_table, chips)
     query = lax.ppermute(own_query, "hop", [(0, 1)])
     z_cols = lax.all_to_all(own_mixed, "chip", 0, 0, tiled=True)
-    query, z_cols = lax.optimization_barrier((query, z_cols))
-
-    right, grad_query, rel_give, rel_keep = trail(
-        first.astype(jnp.int32).reshape(1), query, rows, weight, rel, onehot_t
-    )
+
+    right = hidden_grad(first.astype(jnp.int32).reshape(1), query, rows, weight, rel)
+    hidden, z_cols = lax.optimization_barrier((right, z_cols))
+    grad_query, rel_give, rel_keep = query_and_relation_grad(hidden, query, weight, rel, onehot_t)
     query_back = lax.ppermute(grad_query, "hop", [(1, 0)])
     query_grad = jnp.where(first, query_back, grad_query)
     z_cols, _ = lax.optimization_barrier((z_cols, grad_query))

time: 118 us -> 125 us (1.059)
  Pallas kernels: 21.3 us -> 27 us
    pallas_call x1 -> x2, Pallas kernels: 11.6 us -> 17.3 us  [the longest x1 11 us: query_and_relation_grad(): pl.pallas_call(query_body, out_shape=(jax.ShapeDtypeStruct((rows_dev, wid...]
  transfers between devices with their start and end apart: 16 -> 16, of which waited for: 5 -> 5; matrix products, arithmetic and copies ran while one was open for 11% -> 11% of each run, Pallas kernels for 0% -> 5%
where the time goes in v4:
time: 125 us; the launch traced here: 124 us
  waiting for transfers between devices  48.6 us (39%)
  starting transfers between devices  27.4 us (22%)
  Pallas kernels  27 us (22%)
  other arithmetic  9.34 us (7%)
  matrix products  7.4 us (6%)
  local copies, waits for them, and re-layouts  3.58 us (3%)
    ppermute x3, waiting for transfers between devices, local(): fwd = lax.ppermute(fwd, 'chip', up)  23.8 us
    ppermute x1, waiting for transfers between devices, local(): query = lax.ppermute(own_query, 'hop', [(0, 1)])  12.2 us
    pallas_call x1, Pallas kernels, query_and_relation_grad(): pl.pallas_call(query_body, out_shape=(jax.ShapeDtypeStruct((rows_dev, wid...  11 us
    ppermute x3, waiting for transfers between devices, local(): bwd = lax.ppermute(bwd, 'chip', down)  10.8 us
    pallas_call x1, Pallas kernels, lead(): pl.pallas_call(lead_body, out_shape=(pair, apart, pair), in_specs=[vmem,...  9.69 us
    dot_general x9, matrix products, dot(): lax.dot_general(a, b, (((ca,), (cb,)), ((), ())), preferred_element_type=...  7.4 us
    pallas_call x1, Pallas kernels, hidden_grad(): pl.pallas_call(hidden_body, out_shape=jax.ShapeDtypeStruct((rows_dev, hid...  6.31 us
    all_to_all x1, starting transfers between devices, local(): z_cols = lax.all_to_all(own_mixed, 'chip', 0, 0, tiled=True)  5.67 us
  transfers between devices with their start and end apart: 16, of which 5 were waited for; matrix products, arithmetic and copies ran while one was open for 11% of the time, Pallas kernels for 5%

profile of v4, /device:TPU:15, one launch (start us, length us, event | category | flops | bytes accessed | tf_op | source)
XLA Modules:
  0.0 124.1 jit_solution(2509210910899366773)
XLA Ops:
  0.6 1.4 %fusion.8.onehot = bf16[128,256]{1,0:T(8,128)(2,1)} fusion(s32[128]{0:T(128)} %param.7), kind=kLoop, calls=%fused_computation.20 | loop fusion | flops 65536 | bytes 66048 | tf_op jit(solution)/shard_map/convert_element_type | solution.py:210
  2.0 9.7 %shard_map.67 = (bf16[2,128,1024]{2,1,0:T(8,128)(2,1)}, bf16[8,128,256]{2,1,0:T(8,128)(2,1)}, bf16[2,128,1024]{2,1,0:T(8,128)(2,1)}) custom-call(bf16[128,2048]{1,0:T(8,128)(2,1)} %bitcast.77, bf16[2048,2048]{1,0:T(8,128)(2,1)} %bitcast.69, bf16[128,256]{1,0:T(8,128)(2,1)} %fusion.8.onehot, bf16[256,2048]{1,0:T(8,128)(2,1)} %table.1), custom_call_target="tpu_custom_call" | custom-call | flops 1207959552 | bytes 8388608 | tf_op jit(solution)/shard_map/pallas_call | solution.py:67
  11.7 5.7 %all-to-all-start = ((bf16[8,128,256]{2,1,0:T(8,128)(2,1)}), bf16[8,128,256]{2,1,0:T(8,128)(2,1)}, u32[]{:S(2)}, u32[]{:S(2)}) async-start(bf16[8,128,256]{2,1,0:T(8,128)(2,1)} %get-tuple-element.19), calls=%async_computation | async-start | bytes 1048576 | tf_op jit(solution)/shard_map/all_to_all | solution.py:221
  17.4 1.3 %collective-permute-start = (bf16[2,128,1024]{2,1,0:T(8,128)(2,1)}, bf16[2,128,1024]{2,1,0:T(8,128)(2,1)S(1)}, u32[]{:S(2)}, u32[]{:S(2)}) collective-permute-start(bf16[2,128,1024]{2,1,0:T(8,128)(2,1)} %get-tuple-element.17), channel_id=1, source_target_pairs={{0,16},{1,17},{2,18},{3,19},{4,20},{5,21},{6,22},{7,23},{8,24},{9,... | collective-permute-start | bytes 1572872 | tf_op jit(solution)/shard_map/ppermute | solution.py:220
  18.7 0.7 compare_convert_fusion.onehot
  19.4 12.2 %collective-permute-done.query = bf16[2,128,1024]{2,1,0:T(8,128)(2,1)S(1)} collective-permute-done((bf16[2,128,1024]{2,1,0:T(8,128)(2,1)}, bf16[2,128,1024]{2,1,0:T(8,128)(2,1)S(1)}, u32[]{:S(2)}, u32[]{:S(2)}) %collective-permute-start) | collective-permute-done | bytes 524320 | tf_op jit(solution)/shard_map/ppermute | solution.py:220
  31.6 0.8 copy-done.1
  32.4 6.3 %shard_map.68.hidden = bf16[128,2048]{1,0:T(8,128)(2,1)} custom-call(s32[1]{0:T(128)} %bitcast.first, bf16[2,128,1024]{2,1,0:T(8,128)(2,1)} %copy-done.1, bf16[128,2048]{1,0:T(8,128)(2,1)} %bitcast.78, bf16[2048,2048]{1,0:T(8,128)(2,1)} %bitcast.70, bf16[2,128,1024]{2,1,0:T(8,128)(2,1)} %get-tuple-element.18.rel), custom_call_target="tpu_custom_call" | custom-call | flops 1073741824 | bytes 8388608 | tf_op jit(solution)/shard_map/pallas_call | solution.py:157
  38.8 11.0 %shard_map.69 = (bf16[128,2048]{1,0:T(8,128)(2,1)}, f32[128,2048]{1,0:T(8,128)}, f32[128,2048]{1,0:T(8,128)}) custom-call(bf16[128,2048]{1,0:T(8,128)(2,1)} %shard_map.68.hidden, bf16[2,128,1024]{2,1,0:T(8,128)(2,1)} %copy-done.1, bf16[2048,2048]{1,0:T(8,128)(2,1)} %bitcast.71, bf16[2,128,1024]{2,1,0:T(8,128)(2,1)} %get-tuple-element.18.rel, ...), custom_call_target="tpu_custom_call" | custom-call | flops 1342177280 | bytes 8388608 | tf_op jit(solution)/shard_map/pallas_call | solution.py:179
  49.8 2.2 %collective-permute-start.2 = (f32[128,2048]{1,0:T(8,128)}, f32[128,2048]{1,0:T(8,128)S(1)}, u32[]{:S(2)}, u32[]{:S(2)}) collective-permute-start(f32[128,2048]{1,0:T(8,128)} %get-tuple-element.23), channel_id=1, source_target_pairs={{0,1},{1,0},{2,3},{3,2},{4,5},{5,4},{6,7},{7,6},{8,9},{9,8},{10,11... | collective-permute-start | bytes 3145736 | tf_op jit(solution)/shard_map/ppermute | solution.py:19
  52.0 1.2 collective-permute-start.4
  53.2 0.3 collective-permute-start.3
  53.5 1.3 %collective-permute-start.1 = (bf16[128,2048]{1,0:T(8,128)(2,1)}, bf16[128,2048]{1,0:T(8,128)(2,1)S(1)}, u32[]{:S(2)}, u32[]{:S(2)}) collective-permute-start(bf16[128,2048]{1,0:T(8,128)(2,1)} %get-tuple-element.21), channel_id=1, source_target_pairs={{16,0},{17,1},{18,2},{19,3},{20,4},{21,5},{22,6},{23,7},{24,8},{25... | collective-permute-start | bytes 1572872 | tf_op jit(solution)/shard_map/ppermute | solution.py:226
  54.8 10.8 %collective-permute-done.4 = bf16[128,2048]{1,0:T(8,128)(2,1)} collective-permute-done((bf16[128,2048]{1,0:T(8,128)(2,1)S(1)}, bf16[128,2048]{1,0:T(8,128)(2,1)}, u32[]{:S(2)}, u32[]{:S(2)}) %collective-permute-start.4) | collective-permute-done | bytes 524320 | tf_op jit(solution)/shard_map/ppermute | solution.py:244
  65.6 1.2 collective-permute-start.7
  66.8 0.0 collective-permute-done.3
  66.8 0.3 collective-permute-start.6
  67.1 1.3 %add_convert_fusion = bf16[128,2048]{1,0:T(8,128)(2,1)S(1)} fusion(f32[128,2048]{1,0:T(8,128)} %get-tuple-element.22, f32[128,2048]{1,0:T(8,128)S(1)} %collective-permute-done.2), kind=kLoop, calls=%fused_computation.13 | loop fusion | flops 524288 | bytes 2621440 | tf_op jit(solution)/shard_map/convert_element_type | solution.py:251
  68.4 0.1 copy.10
  68.6 0.1 copy.8
  68.7 0.9 fusion.7
  69.6 5.4 %all-to-all-start.1 = ((bf16[8,128,256]{2,1,0:T(8,128)(2,1)}), bf16[8,128,256]{2,1,0:T(8,128)(2,1)S(1)}, u32[]{:S(2)}, u32[]{:S(2)}) async-start(bf16[8,128,256]{2,1,0:T(8,128)(2,1)} %fusion.7), calls=%async_computation.1 | async-start | bytes 1048576 | tf_op jit(solution)/shard_map/all_to_all | solution.py:256
  75.0 4.1 %collective-permute-done.6 = bf16[128,2048]{1,0:T(8,128)(2,1)} collective-permute-done((bf16[128,2048]{1,0:T(8,128)(2,1)S(1)}, bf16[128,2048]{1,0:T(8,128)(2,1)}, u32[]{:S(2)}, u32[]{:S(2)}) %collective-permute-start.6) | collective-permute-done | bytes 524320 | tf_op jit(solution)/shard_map/ppermute | solution.py:243
  79.1 0.3 collective-permute-start.8
  79.4 1.2 collective-permute-start.9
  80.6 1.3 %collective-permute-start.5 = (bf16[8,128,256]{2,1,0:T(8,128)(2,1)}, bf16[8,128,256]{2,1,0:T(8,128)(2,1)}, u32[]{:S(2)}, u32[]{:S(2)}) collective-permute-start(bf16[8,128,256]{2,1,0:T(8,128)(2,1)} %all-to-all-done), channel_id=1, source_target_pairs={{0,16},{1,17},{2,18},{3,19},{4,20},{5,21},{6,22},{7,23},{8,24},{9,... | collective-permute-start | bytes 1572872 | tf_op jit(solution)/shard_map/ppermute | solution.py:229
  81.9 19.6 %collective-permute-done.8 = bf16[128,2048]{1,0:T(8,128)(2,1)S(1)} collective-permute-done((bf16[128,2048]{1,0:T(8,128)(2,1)}, bf16[128,2048]{1,0:T(8,128)(2,1)S(1)}, u32[]{:S(2)}, u32[]{:S(2)}) %collective-permute-start.8) | collective-permute-done | bytes 524320 | tf_op jit(solution)/shard_map/ppermute | solution.py:243
  101.5 0.7 slice.28
  102.3 0.7 slice.29
  103.0 1.5 %collective-permute-start.12 = (bf16[64,2048]{1,0:T(8,128)(2,1)}, bf16[64,2048]{1,0:T(8,128)(2,1)S(1)}, u32[]{:S(2)}, u32[]{:S(2)}) collective-permute-start(bf16[64,2048]{1,0:T(8,128)(2,1)} %slice.29), channel_id=1, source_target_pairs={{4,0},{8,4},{12,8},{14,12},{10,14},{6,10},{2,6},{0,2},{5,1},{9,5},... | collective-permute-start | bytes 786440 | tf_op jit(solution)/shard_map/ppermute | solution.py:249
  104.4 0.1 convert_reduce_fusion
  104.6 1.4 %collective-permute-start.10 = (f32[8,2048]{1,0:T(8,128)S(1)}, f32[8,2048]{1,0:T(8,128)S(1)}, u32[]{:S(2)}, u32[]{:S(2)}) collective-permute-start(f32[8,2048]{1,0:T(8,128)S(1)} %bitcast.81), channel_id=1, source_target_pairs={{16,0},{17,1},{18,2},{19,3},{20,4},{21,5},{22,6},{23,7},{24,8},{25... | collective-permute-start | bytes 196616 | tf_op jit(solution)/shard_map/ppermute | solution.py:262
  106.0 1.1 broadcast_select_fusion.1
  107.1 0.5 fusion.17
  107.6 1.5 %fusion.15 = f32[256,2048]{1,0:T(8,128)S(1)} fusion(bf16[128,2048]{1,0:T(8,128)(2,1)} %collective-permute-done.4, bf16[8,128,256]{2,1,0:T(8,128)(2,1)S(1)} %broadcast_select_fusion.1, s32[]{:T(128)S(6)} %select_n.169), kind=kOutput, calls=%fused_computation.28 | convolution fusion | flops 134217728 | bytes 2686980 | tf_op jit(solution)/shard_map/dot_general | solution.py:15
  109.1 0.5 fusion.4
  109.6 1.5 %fusion.12 = f32[256,2048]{1,0:T(8,128)S(1)} fusion(bf16[128,2048]{1,0:T(8,128)(2,1)} %collective-permute-done.7, bf16[8,128,256]{2,1,0:T(8,128)(2,1)S(1)} %broadcast_select_fusion.1, s32[]{:T(128)S(6)} %select_n.173), kind=kOutput, calls=%fused_computation.25 | convolution fusion | flops 134217728 | bytes 2686980 | tf_op jit(solution)/shard_map/dot_general | solution.py:15
  111.1 0.5 fusion.9
  111.5 1.5 %fusion.3 = f32[256,2048]{1,0:T(8,128)S(1)} fusion(f32[256,2048]{1,0:T(8,128)S(1)} %fusion.12, f32[256,2048]{1,0:T(8,128)S(1)} %fusion.4, bf16[128,2048]{1,0:T(8,128)(2,1)} %collective-permute-done.6, bf16[8,128,256]{2,1,0:T(8,128)(2,1)S(1)} %broadcast_select_fusion.1, s32[]{:T(128)S(6)} %select_n.171), kind=kOutput, calls=%fused_computation.5 | convolution fusion | flops 135266304 | bytes 6881284 | tf_op jit(solution)/shard_map/dot_general | solution.py:15
  113.1 0.6 broadcast_select_fusion.2
  113.7 0.5 fusion.29
  114.2 0.4 fusion.27
  114.6 0.6 fusion.2
  115.2 1.1 dynamic-slice_bitcast_fusion
  116.3 2.9 %collective-permute-start.13 = (f32[128,2048]{1,0:T(8,128)}, f32[128,2048]{1,0:T(8,128)}, u32[]{:S(2)}, u32[]{:S(2)}) collective-permute-start(f32[128,2048]{1,0:T(8,128)} %dynamic-slice_bitcast_fusion), channel_id=1, source_target_pairs={{0,1},{1,0},{2,3},{3,2},{4,5},{5,4},{6,7},{7,6},{8,9},{9,8},{10,11... | collective-permute-start | bytes 3145736 | tf_op jit(solution)/shard_map/ppermute | solution.py:19
  119.2 0.8 broadcast_select_fusion
  120.0 1.8 %collective-permute-done.13 = f32[128,2048]{1,0:T(8,128)} collective-permute-done((f32[128,2048]{1,0:T(8,128)}, f32[128,2048]{1,0:T(8,128)}, u32[]{:S(2)}, u32[]{:S(2)}) %collective-permute-start.13) | collective-permute-done | bytes 1048608 | tf_op jit(solution)/shard_map/ppermute | solution.py:19
  121.8 2.3 %fusion.6 = f32[1,128,2048]{2,1,0:T(8,128)} fusion(f32[128,2048]{1,0:T(8,128)} %collective-permute-done.13, f32[2,128,2048]{2,1,0:T(8,128)S(1)} %bitcast.73, s32[]{:T(128)S(6)} %select_n.182), kind=kLoop, calls=%fused_computation.10 | loop fusion | flops 524288 | bytes 3145732 | tf_op jit(solution)/shard_map/broadcast_in_dim | solution.py:275
  (27 shorter events, 0.1 us)
Async XLA Ops:
  2.0 16.7 %copy-start.5 = (s32[128]{0:T(128)S(1)}, s32[128]{0:T(128)}, u32[]{:S(2)}) copy-start(s32[128]{0:T(128)} %param.7) | copy-start | bytes 1540
  11.7 27.1 %all-to-all-start = ((bf16[8,128,256]{2,1,0:T(8,128)(2,1)}), bf16[8,128,256]{2,1,0:T(8,128)(2,1)}, u32[]{:S(2)}, u32[]{:S(2)}) async-start(bf16[8,128,256]{2,1,0:T(8,128)(2,1)} %get-tuple-element.19), calls=%async_computation | async-start | bytes 1048576 | tf_op jit(solution)/shard_map/all_to_all | solution.py:221
  17.4 14.3 %collective-permute-start = (bf16[2,128,1024]{2,1,0:T(8,128)(2,1)}, bf16[2,128,1024]{2,1,0:T(8,128)(2,1)S(1)}, u32[]{:S(2)}, u32[]{:S(2)}) collective-permute-start(bf16[2,128,1024]{2,1,0:T(8,128)(2,1)} %get-tuple-element.17), channel_id=1, source_target_pairs={{0,16},{1,17},{2,18},{3,19},{4,20},{5,21},{6,22},{7,23},{8,24},{9,... | collective-permute-start | bytes 1572872 | tf_op jit(solution)/shard_map/ppermute | solution.py:220
  31.6 0.8 copy-start.1
  38.8 13.2 %copy-start = (bf16[128,2048]{1,0:T(8,128)(2,1)S(1)}, bf16[128,2048]{1,0:T(8,128)(2,1)}, u32[]{:S(2)}) copy-start(bf16[128,2048]{1,0:T(8,128)(2,1)} %shard_map.68.hidden) | copy-start | bytes 1572868
  49.8 17.3 %collective-permute-start.2 = (f32[128,2048]{1,0:T(8,128)}, f32[128,2048]{1,0:T(8,128)S(1)}, u32[]{:S(2)}, u32[]{:S(2)}) collective-permute-start(f32[128,2048]{1,0:T(8,128)} %get-tuple-element.23), channel_id=1, source_target_pairs={{0,1},{1,0},{2,3},{3,2},{4,5},{5,4},{6,7},{7,6},{8,9},{9,8},{10,11... | collective-permute-start | bytes 3145736 | tf_op jit(solution)/shard_map/ppermute | solution.py:19
  52.0 13.6 %collective-permute-start.4 = (bf16[128,2048]{1,0:T(8,128)(2,1)S(1)}, bf16[128,2048]{1,0:T(8,128)(2,1)}, u32[]{:S(2)}, u32[]{:S(2)}) collective-permute-start(bf16[128,2048]{1,0:T(8,128)(2,1)S(1)} %copy-done), channel_id=1, source_target_pairs={{4,0},{8,4},{12,8},{14,12},{10,14},{6,10},{2,6},{0,2},{5,1},{9,5},... | collective-permute-start | bytes 1572872 | tf_op jit(solution)/shard_map/ppermute | solution.py:244
  53.2 13.6 %collective-permute-start.3 = (bf16[128,2048]{1,0:T(8,128)(2,1)S(1)}, bf16[128,2048]{1,0:T(8,128)(2,1)S(1)}, u32[]{:S(2)}, u32[]{:S(2)}) collective-permute-start(bf16[128,2048]{1,0:T(8,128)(2,1)S(1)} %copy-done), channel_id=1, source_target_pairs={{0,4},{4,8},{8,12},{12,14},{14,10},{10,6},{6,2},{2,0},{1,5},{5,9},... | collective-permute-start | bytes 1572872 | tf_op jit(solution)/shard_map/ppermute | solution.py:243
  53.5 15.2 %collective-permute-start.1 = (bf16[128,2048]{1,0:T(8,128)(2,1)}, bf16[128,2048]{1,0:T(8,128)(2,1)S(1)}, u32[]{:S(2)}, u32[]{:S(2)}) collective-permute-start(bf16[128,2048]{1,0:T(8,128)(2,1)} %get-tuple-element.21), channel_id=1, source_target_pairs={{16,0},{17,1},{18,2},{19,3},{20,4},{21,5},{22,6},{23,7},{24,8},{25... | collective-permute-start | bytes 1572872 | tf_op jit(solution)/shard_map/ppermute | solution.py:226
  65.6 13.9 %collective-permute-start.7 = (bf16[128,2048]{1,0:T(8,128)(2,1)}, bf16[128,2048]{1,0:T(8,128)(2,1)}, u32[]{:S(2)}, u32[]{:S(2)}) collective-permute-start(bf16[128,2048]{1,0:T(8,128)(2,1)} %collective-permute-done.4), channel_id=1, source_target_pairs={{4,0},{8,4},{12,8},{14,12},{10,14},{6,10},{2,6},{0,2},{5,1},{9,5},... | collective-permute-start | bytes 1572872 | tf_op jit(solution)/shard_map/ppermute | solution.py:244
  66.8 8.2 %copy-start.3 = (bf16[128,2048]{1,0:T(8,128)(2,1)}, bf16[128,2048]{1,0:T(8,128)(2,1)S(1)}, u32[]{:S(2)}) copy-start(bf16[128,2048]{1,0:T(8,128)(2,1)S(1)} %collective-permute-done.3) | copy-start | bytes 1572868
  66.8 12.4 %collective-permute-start.6 = (bf16[128,2048]{1,0:T(8,128)(2,1)S(1)}, bf16[128,2048]{1,0:T(8,128)(2,1)}, u32[]{:S(2)}, u32[]{:S(2)}) collective-permute-start(bf16[128,2048]{1,0:T(8,128)(2,1)S(1)} %collective-permute-done.3), channel_id=1, source_target_pairs={{0,4},{4,8},{8,12},{12,14},{14,10},{10,6},{6,2},{2,0},{1,5},{5,9},... | collective-permute-start | bytes 1572872 | tf_op jit(solution)/shard_map/ppermute | solution.py:243
  69.6 34.9 %all-to-all-start.1 = ((bf16[8,128,256]{2,1,0:T(8,128)(2,1)}), bf16[8,128,256]{2,1,0:T(8,128)(2,1)S(1)}, u32[]{:S(2)}, u32[]{:S(2)}) async-start(bf16[8,128,256]{2,1,0:T(8,128)(2,1)} %fusion.7), calls=%async_computation.1 | async-start | bytes 1048576 | tf_op jit(solution)/shard_map/all_to_all | solution.py:256
  79.1 22.4 %collective-permute-start.8 = (bf16[128,2048]{1,0:T(8,128)(2,1)}, bf16[128,2048]{1,0:T(8,128)(2,1)S(1)}, u32[]{:S(2)}, u32[]{:S(2)}) collective-permute-start(bf16[128,2048]{1,0:T(8,128)(2,1)} %collective-permute-done.6), channel_id=1, source_target_pairs={{0,4},{4,8},{8,12},{12,14},{14,10},{10,6},{6,2},{2,0},{1,5},{5,9},... | collective-permute-start | bytes 1572872 | tf_op jit(solution)/shard_map/ppermute | solution.py:243
  79.4 22.8 %collective-permute-start.9 = (bf16[128,2048]{1,0:T(8,128)(2,1)}, bf16[128,2048]{1,0:T(8,128)(2,1)S(1)}, u32[]{:S(2)}, u32[]{:S(2)}) collective-permute-start(bf16[128,2048]{1,0:T(8,128)(2,1)} %collective-permute-done.7), channel_id=1, source_target_pairs={{4,0},{8,4},{12,8},{14,12},{10,14},{6,10},{2,6},{0,2},{5,1},{9,5},... | collective-permute-start | bytes 1572872 | tf_op jit(solution)/shard_map/ppermute | solution.py:244
  80.6 25.4 %collective-permute-start.5 = (bf16[8,128,256]{2,1,0:T(8,128)(2,1)}, bf16[8,128,256]{2,1,0:T(8,128)(2,1)}, u32[]{:S(2)}, u32[]{:S(2)}) collective-permute-start(bf16[8,128,256]{2,1,0:T(8,128)(2,1)} %all-to-all-done), channel_id=1, source_target_pairs={{0,16},{1,17},{2,18},{3,19},{4,20},{5,21},{6,22},{7,23},{8,24},{9,... | collective-permute-start | bytes 1572872 | tf_op jit(solution)/shard_map/ppermute | solution.py:229
  102.2 11.5 %collective-permute-start.11 = (bf16[64,2048]{1,0:T(8,128)(2,1)}, bf16[64,2048]{1,0:T(8,128)(2,1)S(1)}, u32[]{:S(2)}, u32[]{:S(2)}) collective-permute-start(bf16[64,2048]{1,0:T(8,128)(2,1)} %slice.28), channel_id=1, source_target_pairs={{0,4},{4,8},{8,12},{12,14},{14,10},{10,6},{6,2},{2,0},{1,5},{5,9},... | collective-permute-start | bytes 786440 | tf_op jit(solution)/shard_map/ppermute | solution.py:248
  103.0 11.2 %collective-permute-start.12 = (bf16[64,2048]{1,0:T(8,128)(2,1)}, bf16[64,2048]{1,0:T(8,128)(2,1)S(1)}, u32[]{:S(2)}, u32[]{:S(2)}) collective-permute-start(bf16[64,2048]{1,0:T(8,128)(2,1)} %slice.29), channel_id=1, source_target_pairs={{4,0},{8,4},{12,8},{14,12},{10,14},{6,10},{2,6},{0,2},{5,1},{9,5},... | collective-permute-start | bytes 786440 | tf_op jit(solution)/shard_map/ppermute | solution.py:249
  104.4 2.7 %copy-start.4 = (bf16[128,2048]{1,0:T(8,128)(2,1)S(1)}, bf16[128,2048]{1,0:T(8,128)(2,1)}, u32[]{:S(2)}) copy-start(bf16[128,2048]{1,0:T(8,128)(2,1)} %copy-done.3) | copy-start | bytes 1572868
  104.6 8.5 %collective-permute-start.10 = (f32[8,2048]{1,0:T(8,128)S(1)}, f32[8,2048]{1,0:T(8,128)S(1)}, u32[]{:S(2)}, u32[]{:S(2)}) collective-permute-start(f32[8,2048]{1,0:T(8,128)S(1)} %bitcast.81), channel_id=1, source_target_pairs={{16,0},{17,1},{18,2},{19,3},{20,4},{21,5},{22,6},{23,7},{24,8},{25... | collective-permute-start | bytes 196616 | tf_op jit(solution)/shard_map/ppermute | solution.py:262
  115.2 3.9 %copy-start.2 = (bf16[128,2048]{1,0:T(8,128)(2,1)S(1)}, bf16[128,2048]{1,0:T(8,128)(2,1)}, u32[]{:S(2)}) copy-start(bf16[128,2048]{1,0:T(8,128)(2,1)} %get-tuple-element.21) | copy-start | bytes 1572868
  116.3 5.5 %collective-permute-start.13 = (f32[128,2048]{1,0:T(8,128)}, f32[128,2048]{1,0:T(8,128)}, u32[]{:S(2)}, u32[]{:S(2)}) collective-permute-start(f32[128,2048]{1,0:T(8,128)} %dynamic-slice_bitcast_fusion), channel_id=1, source_target_pairs={{0,1},{1,0},{2,3},{3,2},{4,5},{5,4},{6,7},{7,6},{8,9},{9,8},{10,11... | collective-permute-start | bytes 3145736 | tf_op jit(solution)/shard_map/ppermute | solution.py:19

commit v5 on v2

--- a/solution.py
+++ b/solution.py
@@ -185,23 +185,21 @@
     place = jnp.where(lax.rem(chip, 2) == 0, chip // 2, chips - 1 - chip // 2)
     up = [(ring[i], ring[(i + 1) % chips]) for i in range(chips)]
     down = [(b, a) for a, b in up]
-    blocks = [(right, 0, 0)]
     mid = rows_dev // 2
-    fwd = bwd = [right[:mid], right[mid:]]
+    fwd = bwd = (right[:mid], right[mid:])
+    parts = [((right,), 0)]
     for s in range(1, (chips + 1) // 2):
-        fwd = [lax.ppermute(part, "chip", up) for part in fwd]
-        bwd = [lax.ppermute(part, "chip", down) for part in bwd]
-        for base, ahead, behind in zip((0, mid), fwd, bwd):
-            blocks += [(ahead, chips - s, base), (behind, s, base)]
+        fwd = tuple(lax.ppermute(part, "chip", up) for part in fwd)
+        bwd = tuple(lax.ppermute(part, "chip", down) for part in bwd)
+        parts += [(fwd, chips - s), (bwd, s)]
     if chips % 2 == 0:
-        blocks.append((lax.ppermute(fwd[0], "chip", up), chips // 2, 0))
-        blocks.append((lax.ppermute(bwd[1], "chip", down), chips // 2, mid))
+        parts.append(((lax.ppermute(fwd[0], "chip", up), lax.ppermute(bwd[1], "chip", down)), chips // 2))
 
     rel_sent = (rel_keep + rel_got).astype(BF16).reshape(chips, 2 * owned, chips, cols)
     rel_sent = rel_sent.transpose(0, 2, 1, 3).reshape(chips, 2 * owned * chips, cols)
     if rel_sent.shape[1] == rows_dev:
         shared = jnp.where(first, columns(query_back), rel_sent)
-        shared, _ = lax.optimization_barrier((shared, tuple(block for block, _, _ in blocks[1:5])))
+        shared, _ = lax.optimization_barrier((shared, (parts[1][0], parts[2][0], parts[3][0][0], parts[4][0][0], z_cols)))
         query_cols = rel_rows = lax.all_to_all(shared, "chip", 0, 0, tiled=True)
     else:
         query_cols = lax.all_to_all(columns(query_back), "chip", 0, 0, tiled=True)
@@ -212,11 +210,11 @@
 
     left_cols = jnp.where(first, query_cols, z_cols)
     partial = jnp.zeros((cols, width), F32)
-    for block, step, base in blocks:
+    for part, step in parts:
         left = lax.dynamic_index_in_dim(left_cols, chip_at(place + step), 0, keepdims=False)
         if step == chips // 2:
             left, relation_grad = lax.optimization_barrier((left, relation_grad))
-        partial = partial + dot(left[base:base + block.shape[0]], block, 0, 0)
+        partial = partial + dot(left, jnp.concatenate(part, axis=0), 0, 0)
     partial = partial.reshape(2, cols // 2, width)
     keep = lax.dynamic_index_in_dim(partial, core, 0, keepdims=False)
     give = lax.dynamic_index_in_dim(partial, 1 - core, 0, keepdims=False)

time: 122 us -> 123 us (level)
  matrix products: 15.8 us -> 9.58 us
  starting transfers between devices: 35.1 us -> 39 us
  waiting for transfers between devices: 37.6 us -> 40.3 us
    ppermute x14, waiting for transfers between devices: 21.3 us -> 28 us  [the longest x6 25.4 us: local(): bwd = tuple((lax.ppermute(part, 'chip', down) for part in bwd))]
    dot_general x15 -> x8, matrix products: 15.8 us -> 9.58 us  [dot(): lax.dot_general(a, b, (((ca,), (cb,)), ((), ())), preferred_element_type=...]
    ppermute x1, waiting for transfers between devices: 9.86 us -> 5.87 us  [local(): query_back = lax.ppermute(grad_query, 'hop', [(1, 0)])]
    ppermute x1, starting transfers between devices: 2.02 us -> 4.16 us  [local(): z_cols = lax.ppermute(z_cols, 'hop', [(0, 1)])]
    unnamed x17 -> x21, local copies, waits for them, and re-layouts: 9.16 us -> 9.61 us
  transfers between devices with their start and end apart: 22 -> 22, of which waited for: 6 -> 7; matrix products, arithmetic and copies ran while one was open for 16% -> 10% of each run, Pallas kernels for 7% -> 7%
where the time goes in v5:
time: 123 us; the launch traced here: 120 us
  waiting for transfers between devices  40.3 us (33%)
  starting transfers between devices  39 us (32%)
  Pallas kernels  12.6 us (10%)
  local copies, waits for them, and re-layouts  10.9 us (9%)
  matrix products  9.58 us (8%)
  other arithmetic  7.02 us (6%)
    ppermute x6, waiting for transfers between devices, local(): bwd = tuple((lax.ppermute(part, 'chip', down) for part in bwd))  25.4 us
    unnamed x21, local copies, waits for them, and re-layouts  9.61 us
    dot_general x8, matrix products, dot(): lax.dot_general(a, b, (((ca,), (cb,)), ((), ())), preferred_element_type=...  9.58 us
    pallas_call x1, Pallas kernels, trail(): pl.pallas_call(trail_body, out_shape=(jax.ShapeDtypeStruct((rows_dev, hid...  8.75 us
    ppermute x6, starting transfers between devices, local(): fwd = tuple((lax.ppermute(part, 'chip', up) for part in fwd))  8.05 us
    ppermute x2, starting transfers between devices, swap_core(): return lax.ppermute(block, 'core', [(0, 1), (1, 0)])  6.65 us
    ppermute x1, waiting for transfers between devices, local(): query_back = lax.ppermute(grad_query, 'hop', [(1, 0)])  5.87 us
    all_to_all x1, starting transfers between devices, local(): z_cols = lax.all_to_all(own_mixed, 'chip', 0, 0, tiled=True)  5.73 us
  transfers between devices with their start and end apart: 22, of which 7 were waited for; matrix products, arithmetic and copies ran while one was open for 10% of the time, Pallas kernels for 7%

profile of v5, /device:TPU:9, one launch (start us, length us, event | category | flops | bytes accessed | tf_op | source)
XLA Modules:
  0.0 120.4 jit_solution(8658936820225264174)
XLA Ops:
  0.6 0.7 fusion.31.onehot
  1.4 3.4 %copy-done = bf16[1,2048,2048]{2,1,0:T(8,128)(2,1)S(1)} copy-done((bf16[1,2048,2048]{2,1,0:T(8,128)(2,1)S(1)}, bf16[1,2048,2048]{2,1,0:T(8,128)(2,1)}, u32[]{:S(2)}) %copy-start) | copy-done | bytes 8388632
  4.8 1.0 copy-done.2
  5.8 1.2 %copy-done.4 = bf16[256,2048]{1,0:T(8,128)(2,1)S(1)} copy-done((bf16[256,2048]{1,0:T(8,128)(2,1)S(1)}, bf16[256,2048]{1,0:T(8,128)(2,1)}, u32[]{:S(2)}) %copy-start.4) | copy-done | bytes 1048600
  7.0 3.9 %shard_map.67 = (bf16[2,128,1024]{2,1,0:T(8,128)(2,1)S(1)}, bf16[8,128,256]{2,1,0:T(8,128)(2,1)}, bf16[2,128,1024]{2,1,0:T(8,128)(2,1)S(1)}) custom-call(bf16[128,2048]{1,0:T(8,128)(2,1)S(1)} %bitcast.64, bf16[2048,2048]{1,0:T(8,128)(2,1)S(1)} %bitcast.62, bf16[128,256]{1,0:T(8,128)(2,1)S(1)} %fusion.31.onehot, bf16[256,2048]{1,0:T(8,128)(2,1)S(1)} %copy-done.4), custom_call_target="tpu_custom_call" | custom-call | flops 1207959552 | bytes 8388608 | tf_op jit(solution)/shard_map/pallas_call | solution.py:58
  10.9 3.1 %collective-permute-start = (bf16[2,128,1024]{2,1,0:T(8,128)(2,1)S(1)}, bf16[2,128,1024]{2,1,0:T(8,128)(2,1)S(1)}, u32[]{:S(2)}, u32[]{:S(2)}) collective-permute-start(bf16[2,128,1024]{2,1,0:T(8,128)(2,1)S(1)} %get-tuple-element.15), channel_id=1, source_target_pairs={{0,16},{1,17},{2,18},{3,19},{4,20},{5,21},{6,22},{7,23},{8,24},{9,... | collective-permute-start | bytes 1572872 | tf_op jit(solution)/shard_map/ppermute | solution.py:168
  14.1 5.7 %all-to-all-start = ((bf16[8,128,256]{2,1,0:T(8,128)(2,1)}), bf16[8,128,256]{2,1,0:T(8,128)(2,1)}, u32[]{:S(2)}, u32[]{:S(2)}) async-start(bf16[8,128,256]{2,1,0:T(8,128)(2,1)} %get-tuple-element.20), calls=%async_computation | async-start | bytes 1048576 | tf_op jit(solution)/shard_map/all_to_all | solution.py:169
  19.9 4.7 %collective-permute-done.query = bf16[2,128,1024]{2,1,0:T(8,128)(2,1)S(1)} collective-permute-done((bf16[2,128,1024]{2,1,0:T(8,128)(2,1)S(1)}, bf16[2,128,1024]{2,1,0:T(8,128)(2,1)S(1)}, u32[]{:S(2)}, u32[]{:S(2)}) %collective-permute-start) | collective-permute-done | bytes 524320 | tf_op jit(solution)/shard_map/ppermute | solution.py:168
  24.6 3.4 %copy-done.1 = bf16[1,2048,2048]{2,1,0:T(8,128)(2,1)S(1)} copy-done((bf16[1,2048,2048]{2,1,0:T(8,128)(2,1)S(1)}, bf16[1,2048,2048]{2,1,0:T(8,128)(2,1)}, u32[]{:S(2)}) %copy-start.1) | copy-done | bytes 8388632
  28.0 8.8 %shard_map.68 = (bf16[128,2048]{1,0:T(8,128)(2,1)S(1)}, bf16[128,2048]{1,0:T(8,128)(2,1)}, f32[128,2048]{1,0:T(8,128)}, f32[128,2048]{1,0:T(8,128)S(1)}) custom-call(s32[1]{0:T(128)} %bitcast.first, bf16[2,128,1024]{2,1,0:T(8,128)(2,1)S(1)} %collective-permute-done.query, bf16[128,2048]{1,0:T(8,128)(2,1)S(1)} %bitcast.65, bf16[2048,2048]{1,0:T(8,128)(2,1)S(1)} %bitcast.63, ...), custom_call_target="tpu_custom_call" | custom-call | flops 2415919104 | bytes 16777216 | tf_op jit(solution)/shard_map/pallas_call | solution.py:123
  36.7 1.5 %collective-permute-start.2 = (f32[128,2048]{1,0:T(8,128)}, f32[128,2048]{1,0:T(8,128)}, u32[]{:S(2)}, u32[]{:S(2)}) collective-permute-start(f32[128,2048]{1,0:T(8,128)} %get-tuple-element.19), channel_id=1, source_target_pairs={{0,1},{1,0},{2,3},{3,2},{4,5},{5,4},{6,7},{7,6},{8,9},{9,8},{10,11... | collective-permute-start | bytes 3145736 | tf_op jit(solution)/shard_map/ppermute | solution.py:20
  38.3 1.3 %collective-permute-start.1 = (bf16[128,2048]{1,0:T(8,128)(2,1)}, bf16[128,2048]{1,0:T(8,128)(2,1)S(1)}, u32[]{:S(2)}, u32[]{:S(2)}) collective-permute-start(bf16[128,2048]{1,0:T(8,128)(2,1)} %get-tuple-element.17), channel_id=1, source_target_pairs={{16,0},{17,1},{18,2},{19,3},{20,4},{21,5},{22,6},{23,7},{24,8},{25... | collective-permute-start | bytes 1572872 | tf_op jit(solution)/shard_map/ppermute | solution.py:174
  39.6 1.4 %collective-permute-start.3 = (bf16[64,2048]{1,0:T(8,128)(2,1)S(1)}, bf16[64,2048]{1,0:T(8,128)(2,1)S(1)}, u32[]{:S(2)}, u32[]{:S(2)}) collective-permute-start(bf16[64,2048]{1,0:T(8,128)(2,1)S(1)} %get-tuple-element.27), channel_id=1, source_target_pairs={{0,4},{4,8},{8,12},{12,14},{14,10},{10,6},{6,2},{2,0},{1,5},{5,9},... | collective-permute-start | bytes 786440 | tf_op jit(solution)/shard_map/ppermute | solution.py:192
  41.0 0.2 collective-permute-start.5
  41.2 1.3 %collective-permute-start.4 = (bf16[64,2048]{1,0:T(8,128)(2,1)S(1)}, bf16[64,2048]{1,0:T(8,128)(2,1)}, u32[]{:S(2)}, u32[]{:S(2)}) collective-permute-start(bf16[64,2048]{1,0:T(8,128)(2,1)S(1)} %get-tuple-element.28), channel_id=1, source_target_pairs={{0,4},{4,8},{8,12},{12,14},{14,10},{10,6},{6,2},{2,0},{1,5},{5,9},... | collective-permute-start | bytes 786440 | tf_op jit(solution)/shard_map/ppermute | solution.py:192
  42.5 4.2 %collective-permute-start.9 = (bf16[8,128,256]{2,1,0:T(8,128)(2,1)}, bf16[8,128,256]{2,1,0:T(8,128)(2,1)S(1)}, u32[]{:S(2)}, u32[]{:S(2)}) collective-permute-start(bf16[8,128,256]{2,1,0:T(8,128)(2,1)} %all-to-all-done), channel_id=1, source_target_pairs={{0,16},{1,17},{2,18},{3,19},{4,20},{5,21},{6,22},{7,23},{8,24},{9,... | collective-permute-start | bytes 1572872 | tf_op jit(solution)/shard_map/ppermute | solution.py:177
  46.6 1.3 %add_convert_fusion = bf16[128,2048]{1,0:T(8,128)(2,1)S(1)} fusion(f32[128,2048]{1,0:T(8,128)S(1)} %get-tuple-element.18, f32[128,2048]{1,0:T(8,128)} %collective-permute-done.2), kind=kLoop, calls=%fused_computation.12 | loop fusion | flops 524288 | bytes 2621440 | tf_op jit(solution)/shard_map/convert_element_type | solution.py:198
  48.0 0.1 copy.10
  48.2 5.9 %collective-permute-done.1 = bf16[128,2048]{1,0:T(8,128)(2,1)S(1)} collective-permute-done((bf16[128,2048]{1,0:T(8,128)(2,1)}, bf16[128,2048]{1,0:T(8,128)(2,1)S(1)}, u32[]{:S(2)}, u32[]{:S(2)}) %collective-permute-start.1) | collective-permute-done | bytes 524320 | tf_op jit(solution)/shard_map/ppermute | solution.py:174
  54.1 0.2 collective-permute-start.6
  54.3 1.3 %collective-permute-start.7 = (bf16[64,2048]{1,0:T(8,128)(2,1)S(1)}, bf16[64,2048]{1,0:T(8,128)(2,1)S(1)}, u32[]{:S(2)}, u32[]{:S(2)}) collective-permute-start(bf16[64,2048]{1,0:T(8,128)(2,1)S(1)} %collective-permute-done.3), channel_id=1, source_target_pairs={{0,4},{4,8},{8,12},{12,14},{14,10},{10,6},{6,2},{2,0},{1,5},{5,9},... | collective-permute-start | bytes 786440 | tf_op jit(solution)/shard_map/ppermute | solution.py:192
  55.6 0.2 collective-permute-start.8
  55.7 0.9 fusion.5
  56.6 4.6 %collective-permute-done.6 = bf16[64,2048]{1,0:T(8,128)(2,1)S(1)} collective-permute-done((bf16[64,2048]{1,0:T(8,128)(2,1)S(1)}, bf16[64,2048]{1,0:T(8,128)(2,1)S(1)}, u32[]{:S(2)}, u32[]{:S(2)}) %collective-permute-start.6) | collective-permute-done | bytes 262176 | tf_op jit(solution)/shard_map/ppermute | solution.py:193
  61.2 5.7 %collective-permute-done.8 = bf16[64,2048]{1,0:T(8,128)(2,1)} collective-permute-done((bf16[64,2048]{1,0:T(8,128)(2,1)S(1)}, bf16[64,2048]{1,0:T(8,128)(2,1)}, u32[]{:S(2)}, u32[]{:S(2)}) %collective-permute-start.8) | collective-permute-done | bytes 262176 | tf_op jit(solution)/shard_map/ppermute | solution.py:193
  66.9 5.7 %all-to-all-start.1 = ((bf16[8,128,256]{2,1,0:T(8,128)(2,1)}), bf16[8,128,256]{2,1,0:T(8,128)(2,1)S(1)}, u32[]{:S(2)}, u32[]{:S(2)}) async-start(bf16[8,128,256]{2,1,0:T(8,128)(2,1)} %fusion.5), calls=%async_computation.1 | async-start | bytes 1048576 | tf_op jit(solution)/shard_map/all_to_all | solution.py:203
  72.7 1.4 %collective-permute-start.10 = (bf16[64,2048]{1,0:T(8,128)(2,1)}, bf16[64,2048]{1,0:T(8,128)(2,1)}, u32[]{:S(2)}, u32[]{:S(2)}) collective-permute-start(bf16[64,2048]{1,0:T(8,128)(2,1)} %collective-permute-done.4), channel_id=1, source_target_pairs={{0,4},{4,8},{8,12},{12,14},{14,10},{10,6},{6,2},{2,0},{1,5},{5,9},... | collective-permute-start | bytes 786440 | tf_op jit(solution)/shard_map/ppermute | solution.py:192
  74.1 1.2 collective-permute-start.12
  75.3 15.1 %collective-permute-done.11 = bf16[64,2048]{1,0:T(8,128)(2,1)S(1)} collective-permute-done((bf16[64,2048]{1,0:T(8,128)(2,1)S(1)}, bf16[64,2048]{1,0:T(8,128)(2,1)S(1)}, u32[]{:S(2)}, u32[]{:S(2)}) %collective-permute-start.11) | collective-permute-done | bytes 262176 | tf_op jit(solution)/shard_map/ppermute | solution.py:193
  90.4 1.5 %collective-permute-start.13 = (bf16[64,2048]{1,0:T(8,128)(2,1)}, bf16[64,2048]{1,0:T(8,128)(2,1)}, u32[]{:S(2)}, u32[]{:S(2)}) collective-permute-start(bf16[64,2048]{1,0:T(8,128)(2,1)} %collective-permute-done.10), channel_id=1, source_target_pairs={{0,4},{4,8},{8,12},{12,14},{14,10},{10,6},{6,2},{2,0},{1,5},{5,9},... | collective-permute-start | bytes 786440 | tf_op jit(solution)/shard_map/ppermute | solution.py:192
  91.9 2.6 %collective-permute-done.12 = bf16[64,2048]{1,0:T(8,128)(2,1)S(1)} collective-permute-done((bf16[64,2048]{1,0:T(8,128)(2,1)S(1)}, bf16[64,2048]{1,0:T(8,128)(2,1)S(1)}, u32[]{:S(2)}, u32[]{:S(2)}) %collective-permute-start.12) | collective-permute-done | bytes 262176 | tf_op jit(solution)/shard_map/ppermute | solution.py:192
  94.5 2.3 %collective-permute-start.17 = (bf16[64,2048]{1,0:T(8,128)(2,1)S(1)}, bf16[64,2048]{1,0:T(8,128)(2,1)}, u32[]{:S(2)}, u32[]{:S(2)}) collective-permute-start(bf16[64,2048]{1,0:T(8,128)(2,1)S(1)} %collective-permute-done.12), channel_id=1, source_target_pairs={{0,4},{4,8},{8,12},{12,14},{14,10},{10,6},{6,2},{2,0},{1,5},{5,9},... | collective-permute-start | bytes 786440 | tf_op jit(solution)/shard_map/ppermute | solution.py:196
  97.0 1.4 %collective-permute-start.16 = (f32[8,2048]{1,0:T(8,128)S(1)}, f32[8,2048]{1,0:T(8,128)S(1)}, u32[]{:S(2)}, u32[]{:S(2)}) collective-permute-start(f32[8,2048]{1,0:T(8,128)S(1)} %bitcast.73), channel_id=1, source_target_pairs={{16,0},{17,1},{18,2},{19,3},{20,4},{21,5},{22,6},{23,7},{24,8},{25... | collective-permute-start | bytes 196616 | tf_op jit(solution)/shard_map/ppermute | solution.py:209
  98.5 1.4 %fusion.6 = f32[256,2048]{1,0:T(8,128)S(1)} fusion(bf16[64,2048]{1,0:T(8,128)(2,1)} %collective-permute-done.4, bf16[64,2048]{1,0:T(8,128)(2,1)S(1)} %collective-permute-done.3, bf16[8,128,256]{2,1,0:T(8,128)(2,1)S(1)} %broadcast_select_fusion.1, s32[]{:T(128)S(6)} %select_n.165), kind=kOutput, calls=%fused_computation.16 | convolution fusion | flops 135266304 | bytes 2686980 | tf_op jit(solution)/shard_map/dot_general | solution.py:16
  99.9 0.5 fusion.10
  100.3 0.5 fusion.2
  100.8 0.5 copy-done.8
  101.3 1.4 %fusion.17 = f32[256,2048]{1,0:T(8,128)S(1)} fusion(bf16[64,2048]{1,0:T(8,128)(2,1)S(1)} %copy-done.8, bf16[64,2048]{1,0:T(8,128)(2,1)} %collective-permute-done.8, bf16[8,128,256]{2,1,0:T(8,128)(2,1)S(1)} %broadcast_select_fusion.1, s32[]{:T(128)S(6)} %select_n.171), kind=kOutput, calls=%fused_computation.27 | convolution fusion | flops 135266304 | bytes 2686980 | tf_op jit(solution)/shard_map/dot_general | solution.py:16
  102.7 1.4 %fusion.1 = f32[256,2048]{1,0:T(8,128)S(1)} fusion(f32[256,2048]{1,0:T(8,128)S(1)} %fusion.17, f32[256,2048]{1,0:T(8,128)S(1)} %fusion.2, bf16[64,2048]{1,0:T(8,128)(2,1)} %collective-permute-done.10, bf16[64,2048]{1,0:T(8,128)(2,1)S(1)} %collective-permute-done.7, bf16[8,128,256]{2,1,0:T(8,128)(2,1)S(1)} %broadcast_select_fusion.1, s32[]{:T(128)S(6)} %select_n.169), kind=kOutput, calls=%fused_computation.4 | convolution fusion | flops 136314880 | bytes 6881284 | tf_op jit(solution)/shard_map/dot_general | solution.py:16
  104.1 1.5 %fusion.24 = f32[256,2048]{1,0:T(8,128)S(1)} fusion(bf16[64,2048]{1,0:T(8,128)(2,1)} %collective-permute-done.15, bf16[64,2048]{1,0:T(8,128)(2,1)} %collective-permute-done.14, bf16[8,128,256]{2,1,0:T(8,128)(2,1)S(1)} %broadcast_select_fusion.1, s32[]{:T(128)S(6)} %select_n.175), kind=kOutput, calls=%fused_computation.34 | convolution fusion | flops 135266304 | bytes 2686980 | tf_op jit(solution)/shard_map/dot_general | solution.py:16
  105.6 1.4 %fusion = f32[256,2048]{1,0:T(8,128)S(1)} fusion(f32[256,2048]{1,0:T(8,128)S(1)} %fusion.24, f32[256,2048]{1,0:T(8,128)S(1)} %fusion.1, bf16[64,2048]{1,0:T(8,128)(2,1)} %collective-permute-done.13, bf16[64,2048]{1,0:T(8,128)(2,1)S(1)} %collective-permute-done.12, bf16[8,128,256]{2,1,0:T(8,128)(2,1)S(1)} %broadcast_select_fusion.1, s32[]{:T(128)S(6)} %select_n.173), kind=kOutput, calls=%fused_computation.2 | convolution fusion | flops 136314880 | bytes 6881284 | tf_op jit(solution)/shard_map/dot_general | solution.py:16
  107.1 0.6 broadcast_select_fusion.2
  107.8 1.5 %convolution_add_fusion = f32[256,2048]{1,0:T(8,128)S(1)} fusion(f32[256,2048]{1,0:T(8,128)S(1)} %fusion, bf16[128,256]{1,0:T(8,128)(2,1)S(1)} %dynamic-slice_bitcast_fusion.1, bf16[64,2048]{1,0:T(8,128)(2,1)} %collective-permute-done.18, bf16[64,2048]{1,0:T(8,128)(2,1)} %collective-permute-done.17), kind=kOutput, calls=%fused_computation | convolution fusion | flops 135790592 | bytes 4784128 | tf_op jit(solution)/shard_map/dot_general | solution.py:16
  109.2 1.1 dynamic-slice_bitcast_fusion
  110.3 5.1 %collective-permute-start.19 = (f32[128,2048]{1,0:T(8,128)}, f32[128,2048]{1,0:T(8,128)}, u32[]{:S(2)}, u32[]{:S(2)}) collective-permute-start(f32[128,2048]{1,0:T(8,128)} %dynamic-slice_bitcast_fusion), channel_id=1, source_target_pairs={{0,1},{1,0},{2,3},{3,2},{4,5},{5,4},{6,7},{7,6},{8,9},{9,8},{10,11... | collective-permute-start | bytes 3145736 | tf_op jit(solution)/shard_map/ppermute | solution.py:20
  115.4 0.9 broadcast_select_fusion
  116.3 1.8 %collective-permute-done.19 = f32[128,2048]{1,0:T(8,128)} collective-permute-done((f32[128,2048]{1,0:T(8,128)}, f32[128,2048]{1,0:T(8,128)}, u32[]{:S(2)}, u32[]{:S(2)}) %collective-permute-start.19) | collective-permute-done | bytes 1048608 | tf_op jit(solution)/shard_map/ppermute | solution.py:20
  118.0 2.3 %fusion.4 = f32[1,128,2048]{2,1,0:T(8,128)} fusion(f32[128,2048]{1,0:T(8,128)} %collective-permute-done.19, f32[2,128,2048]{2,1,0:T(8,128)S(1)} %bitcast.67, s32[]{:T(128)S(6)} %select_n.180), kind=kLoop, calls=%fused_computation.9 | loop fusion | flops 524288 | bytes 3145732 | tf_op jit(solution)/shard_map/broadcast_in_dim | solution.py:222
  (44 shorter events, 0.6 us)
Async XLA Ops:
  1.4 3.4 %copy-start = (bf16[1,2048,2048]{2,1,0:T(8,128)(2,1)S(1)}, bf16[1,2048,2048]{2,1,0:T(8,128)(2,1)}, u32[]{:S(2)}) copy-start(bf16[1,2048,2048]{2,1,0:T(8,128)(2,1)} %param.5) | copy-start | bytes 25165828
  4.8 1.0 copy-start.2
  5.8 1.2 %copy-start.4 = (bf16[256,2048]{1,0:T(8,128)(2,1)S(1)}, bf16[256,2048]{1,0:T(8,128)(2,1)}, u32[]{:S(2)}) copy-start(bf16[256,2048]{1,0:T(8,128)(2,1)} %table.1) | copy-start | bytes 3145732
  7.0 12.8 %copy-start.9 = (s32[128]{0:T(128)S(1)}, s32[128]{0:T(128)}, u32[]{:S(2)}) copy-start(s32[128]{0:T(128)} %param.7) | copy-start | bytes 1540
  7.0 17.6 %copy-start.3 = (bf16[1,128,2048]{2,1,0:T(8,128)(2,1)S(1)}, bf16[1,128,2048]{2,1,0:T(8,128)(2,1)}, u32[]{:S(2)}) copy-start(bf16[1,128,2048]{2,1,0:T(8,128)(2,1)} %param.4) | copy-start | bytes 1572868
  10.9 13.7 %collective-permute-start = (bf16[2,128,1024]{2,1,0:T(8,128)(2,1)S(1)}, bf16[2,128,1024]{2,1,0:T(8,128)(2,1)S(1)}, u32[]{:S(2)}, u32[]{:S(2)}) collective-permute-start(bf16[2,128,1024]{2,1,0:T(8,128)(2,1)S(1)} %get-tuple-element.15), channel_id=1, source_target_pairs={{0,16},{1,17},{2,18},{3,19},{4,20},{5,21},{6,22},{7,23},{8,24},{9,... | collective-permute-start | bytes 1572872 | tf_op jit(solution)/shard_map/ppermute | solution.py:168
  14.1 25.5 %all-to-all-start = ((bf16[8,128,256]{2,1,0:T(8,128)(2,1)}), bf16[8,128,256]{2,1,0:T(8,128)(2,1)}, u32[]{:S(2)}, u32[]{:S(2)}) async-start(bf16[8,128,256]{2,1,0:T(8,128)(2,1)} %get-tuple-element.20), calls=%async_computation | async-start | bytes 1048576 | tf_op jit(solution)/shard_map/all_to_all | solution.py:169
  24.6 3.4 %copy-start.1 = (bf16[1,2048,2048]{2,1,0:T(8,128)(2,1)S(1)}, bf16[1,2048,2048]{2,1,0:T(8,128)(2,1)}, u32[]{:S(2)}) copy-start(bf16[1,2048,2048]{2,1,0:T(8,128)(2,1)} %param.5) | copy-start | bytes 25165828
  36.7 5.7 %collective-permute-start.2 = (f32[128,2048]{1,0:T(8,128)}, f32[128,2048]{1,0:T(8,128)}, u32[]{:S(2)}, u32[]{:S(2)}) collective-permute-start(f32[128,2048]{1,0:T(8,128)} %get-tuple-element.19), channel_id=1, source_target_pairs={{0,1},{1,0},{2,3},{3,2},{4,5},{5,4},{6,7},{7,6},{8,9},{9,8},{10,11... | collective-permute-start | bytes 3145736 | tf_op jit(solution)/shard_map/ppermute | solution.py:20
  38.3 15.8 %collective-permute-start.1 = (bf16[128,2048]{1,0:T(8,128)(2,1)}, bf16[128,2048]{1,0:T(8,128)(2,1)S(1)}, u32[]{:S(2)}, u32[]{:S(2)}) collective-permute-start(bf16[128,2048]{1,0:T(8,128)(2,1)} %get-tuple-element.17), channel_id=1, source_target_pairs={{16,0},{17,1},{18,2},{19,3},{20,4},{21,5},{22,6},{23,7},{24,8},{25... | collective-permute-start | bytes 1572872 | tf_op jit(solution)/shard_map/ppermute | solution.py:174
  39.6 14.6 %collective-permute-start.3 = (bf16[64,2048]{1,0:T(8,128)(2,1)S(1)}, bf16[64,2048]{1,0:T(8,128)(2,1)S(1)}, u32[]{:S(2)}, u32[]{:S(2)}) collective-permute-start(bf16[64,2048]{1,0:T(8,128)(2,1)S(1)} %get-tuple-element.27), channel_id=1, source_target_pairs={{0,4},{4,8},{8,12},{12,14},{14,10},{10,6},{6,2},{2,0},{1,5},{5,9},... | collective-permute-start | bytes 786440 | tf_op jit(solution)/shard_map/ppermute | solution.py:192
  41.0 14.6 %collective-permute-start.5 = (bf16[64,2048]{1,0:T(8,128)(2,1)S(1)}, bf16[64,2048]{1,0:T(8,128)(2,1)S(1)}, u32[]{:S(2)}, u32[]{:S(2)}) collective-permute-start(bf16[64,2048]{1,0:T(8,128)(2,1)S(1)} %get-tuple-element.27), channel_id=1, source_target_pairs={{4,0},{8,4},{12,8},{14,12},{10,14},{6,10},{2,6},{0,2},{5,1},{9,5},... | collective-permute-start | bytes 786440 | tf_op jit(solution)/shard_map/ppermute | solution.py:193
  41.2 15.5 %collective-permute-start.4 = (bf16[64,2048]{1,0:T(8,128)(2,1)S(1)}, bf16[64,2048]{1,0:T(8,128)(2,1)}, u32[]{:S(2)}, u32[]{:S(2)}) collective-permute-start(bf16[64,2048]{1,0:T(8,128)(2,1)S(1)} %get-tuple-element.28), channel_id=1, source_target_pairs={{0,4},{4,8},{8,12},{12,14},{14,10},{10,6},{6,2},{2,0},{1,5},{5,9},... | collective-permute-start | bytes 786440 | tf_op jit(solution)/shard_map/ppermute | solution.py:192
  42.5 24.5 %collective-permute-start.9 = (bf16[8,128,256]{2,1,0:T(8,128)(2,1)}, bf16[8,128,256]{2,1,0:T(8,128)(2,1)S(1)}, u32[]{:S(2)}, u32[]{:S(2)}) collective-permute-start(bf16[8,128,256]{2,1,0:T(8,128)(2,1)} %all-to-all-done), channel_id=1, source_target_pairs={{0,16},{1,17},{2,18},{3,19},{4,20},{5,21},{6,22},{7,23},{8,24},{9,... | collective-permute-start | bytes 1572872 | tf_op jit(solution)/shard_map/ppermute | solution.py:177
  54.1 7.1 %collective-permute-start.6 = (bf16[64,2048]{1,0:T(8,128)(2,1)S(1)}, bf16[64,2048]{1,0:T(8,128)(2,1)S(1)}, u32[]{:S(2)}, u32[]{:S(2)}) collective-permute-start(bf16[64,2048]{1,0:T(8,128)(2,1)S(1)} %get-tuple-element.28), channel_id=1, source_target_pairs={{4,0},{8,4},{12,8},{14,12},{10,14},{6,10},{2,6},{0,2},{5,1},{9,5},... | collective-permute-start | bytes 786440 | tf_op jit(solution)/shard_map/ppermute | solution.py:193
  54.3 6.9 %collective-permute-start.7 = (bf16[64,2048]{1,0:T(8,128)(2,1)S(1)}, bf16[64,2048]{1,0:T(8,128)(2,1)S(1)}, u32[]{:S(2)}, u32[]{:S(2)}) collective-permute-start(bf16[64,2048]{1,0:T(8,128)(2,1)S(1)} %collective-permute-done.3), channel_id=1, source_target_pairs={{0,4},{4,8},{8,12},{12,14},{14,10},{10,6},{6,2},{2,0},{1,5},{5,9},... | collective-permute-start | bytes 786440 | tf_op jit(solution)/shard_map/ppermute | solution.py:192
  55.6 5.6 %copy-start.5 = (bf16[64,2048]{1,0:T(8,128)(2,1)}, bf16[64,2048]{1,0:T(8,128)(2,1)S(1)}, u32[]{:S(2)}) copy-start(bf16[64,2048]{1,0:T(8,128)(2,1)S(1)} %collective-permute-done.5) | copy-start | bytes 786436
  55.6 11.3 %collective-permute-start.8 = (bf16[64,2048]{1,0:T(8,128)(2,1)S(1)}, bf16[64,2048]{1,0:T(8,128)(2,1)}, u32[]{:S(2)}, u32[]{:S(2)}) collective-permute-start(bf16[64,2048]{1,0:T(8,128)(2,1)S(1)} %collective-permute-done.5), channel_id=1, source_target_pairs={{4,0},{8,4},{12,8},{14,12},{10,14},{6,10},{2,6},{0,2},{5,1},{9,5},... | collective-permute-start | bytes 786440 | tf_op jit(solution)/shard_map/ppermute | solution.py:193
  66.9 29.9 %all-to-all-start.1 = ((bf16[8,128,256]{2,1,0:T(8,128)(2,1)}), bf16[8,128,256]{2,1,0:T(8,128)(2,1)S(1)}, u32[]{:S(2)}, u32[]{:S(2)}) async-start(bf16[8,128,256]{2,1,0:T(8,128)(2,1)} %fusion.5), calls=%async_computation.1 | async-start | bytes 1048576 | tf_op jit(solution)/shard_map/all_to_all | solution.py:203
  72.6 17.8 %collective-permute-start.11 = (bf16[64,2048]{1,0:T(8,128)(2,1)S(1)}, bf16[64,2048]{1,0:T(8,128)(2,1)S(1)}, u32[]{:S(2)}, u32[]{:S(2)}) collective-permute-start(bf16[64,2048]{1,0:T(8,128)(2,1)S(1)} %collective-permute-done.6), channel_id=1, source_target_pairs={{4,0},{8,4},{12,8},{14,12},{10,14},{6,10},{2,6},{0,2},{5,1},{9,5},... | collective-permute-start | bytes 786440 | tf_op jit(solution)/shard_map/ppermute | solution.py:193
  72.7 17.7 %collective-permute-start.10 = (bf16[64,2048]{1,0:T(8,128)(2,1)}, bf16[64,2048]{1,0:T(8,128)(2,1)}, u32[]{:S(2)}, u32[]{:S(2)}) collective-permute-start(bf16[64,2048]{1,0:T(8,128)(2,1)} %collective-permute-done.4), channel_id=1, source_target_pairs={{0,4},{4,8},{8,12},{12,14},{14,10},{10,6},{6,2},{2,0},{1,5},{5,9},... | collective-permute-start | bytes 786440 | tf_op jit(solution)/shard_map/ppermute | solution.py:192
  74.1 20.4 %collective-permute-start.12 = (bf16[64,2048]{1,0:T(8,128)(2,1)S(1)}, bf16[64,2048]{1,0:T(8,128)(2,1)S(1)}, u32[]{:S(2)}, u32[]{:S(2)}) collective-permute-start(bf16[64,2048]{1,0:T(8,128)(2,1)S(1)} %collective-permute-done.7), channel_id=1, source_target_pairs={{0,4},{4,8},{8,12},{12,14},{14,10},{10,6},{6,2},{2,0},{1,5},{5,9},... | collective-permute-start | bytes 786440 | tf_op jit(solution)/shard_map/ppermute | solution.py:192
  90.4 6.4 %copy-start.7 = (bf16[64,2048]{1,0:T(8,128)(2,1)}, bf16[64,2048]{1,0:T(8,128)(2,1)S(1)}, u32[]{:S(2)}) copy-start(bf16[64,2048]{1,0:T(8,128)(2,1)S(1)} %collective-permute-done.11) | copy-start | bytes 786436
  90.4 6.4 %collective-permute-start.15 = (bf16[64,2048]{1,0:T(8,128)(2,1)S(1)}, bf16[64,2048]{1,0:T(8,128)(2,1)}, u32[]{:S(2)}, u32[]{:S(2)}) collective-permute-start(bf16[64,2048]{1,0:T(8,128)(2,1)S(1)} %collective-permute-done.11), channel_id=1, source_target_pairs={{4,0},{8,4},{12,8},{14,12},{10,14},{6,10},{2,6},{0,2},{5,1},{9,5},... | collective-permute-start | bytes 786440 | tf_op jit(solution)/shard_map/ppermute | solution.py:193
  90.4 13.7 %collective-permute-start.14 = (bf16[64,2048]{1,0:T(8,128)(2,1)}, bf16[64,2048]{1,0:T(8,128)(2,1)}, u32[]{:S(2)}, u32[]{:S(2)}) collective-permute-start(bf16[64,2048]{1,0:T(8,128)(2,1)} %collective-permute-done.8), channel_id=1, source_target_pairs={{4,0},{8,4},{12,8},{14,12},{10,14},{6,10},{2,6},{0,2},{5,1},{9,5},... | collective-permute-start | bytes 786440 | tf_op jit(solution)/shard_map/ppermute | solution.py:193
  90.4 15.2 %collective-permute-start.13 = (bf16[64,2048]{1,0:T(8,128)(2,1)}, bf16[64,2048]{1,0:T(8,128)(2,1)}, u32[]{:S(2)}, u32[]{:S(2)}) collective-permute-start(bf16[64,2048]{1,0:T(8,128)(2,1)} %collective-permute-done.10), channel_id=1, source_target_pairs={{0,4},{4,8},{8,12},{12,14},{14,10},{10,6},{6,2},{2,0},{1,5},{5,9},... | collective-permute-start | bytes 786440 | tf_op jit(solution)/shard_map/ppermute | solution.py:192
  94.5 13.3 %collective-permute-start.17 = (bf16[64,2048]{1,0:T(8,128)(2,1)S(1)}, bf16[64,2048]{1,0:T(8,128)(2,1)}, u32[]{:S(2)}, u32[]{:S(2)}) collective-permute-start(bf16[64,2048]{1,0:T(8,128)(2,1)S(1)} %collective-permute-done.12), channel_id=1, source_target_pairs={{0,4},{4,8},{8,12},{12,14},{14,10},{10,6},{6,2},{2,0},{1,5},{5,9},... | collective-permute-start | bytes 786440 | tf_op jit(solution)/shard_map/ppermute | solution.py:196
  96.8 10.9 %collective-permute-start.18 = (bf16[64,2048]{1,0:T(8,128)(2,1)}, bf16[64,2048]{1,0:T(8,128)(2,1)}, u32[]{:S(2)}, u32[]{:S(2)}) collective-permute-start(bf16[64,2048]{1,0:T(8,128)(2,1)} %collective-permute-done.15), channel_id=1, source_target_pairs={{4,0},{8,4},{12,8},{14,12},{10,14},{6,10},{2,6},{0,2},{5,1},{9,5},... | collective-permute-start | bytes 786440 | tf_op jit(solution)/shard_map/ppermute | solution.py:196
  96.9 2.9 %copy-start.6 = (bf16[64,2048]{1,0:T(8,128)(2,1)S(1)}, bf16[64,2048]{1,0:T(8,128)(2,1)}, u32[]{:S(2)}) copy-start(bf16[64,2048]{1,0:T(8,128)(2,1)} %copy-done.5) | copy-start | bytes 786436
  97.0 10.1 %collective-permute-start.16 = (f32[8,2048]{1,0:T(8,128)S(1)}, f32[8,2048]{1,0:T(8,128)S(1)}, u32[]{:S(2)}, u32[]{:S(2)}) collective-permute-start(f32[8,2048]{1,0:T(8,128)S(1)} %bitcast.73), channel_id=1, source_target_pairs={{16,0},{17,1},{18,2},{19,3},{20,4},{21,5},{22,6},{23,7},{24,8},{25... | collective-permute-start | bytes 196616 | tf_op jit(solution)/shard_map/ppermute | solution.py:209
  100.3 1.0 copy-start.8
  110.3 7.7 %collective-permute-start.19 = (f32[128,2048]{1,0:T(8,128)}, f32[128,2048]{1,0:T(8,128)}, u32[]{:S(2)}, u32[]{:S(2)}) collective-permute-start(f32[128,2048]{1,0:T(8,128)} %dynamic-slice_bitcast_fusion), channel_id=1, source_target_pairs={{0,1},{1,0},{2,3},{3,2},{4,5},{5,4},{6,7},{7,6},{8,9},{9,8},{10,11... | collective-permute-start | bytes 3145736 | tf_op jit(solution)/shard_map/ppermute | solution.py:20

commit v6 on v2

--- a/solution.py
+++ b/solution.py
@@ -186,22 +186,22 @@
     up = [(ring[i], ring[(i + 1) % chips]) for i in range(chips)]
     down = [(b, a) for a, b in up]
     blocks = [(right, 0, 0)]
-    mid = rows_dev // 2
-    fwd = bwd = [right[:mid], right[mid:]]
+    fwd = bwd = right
     for s in range(1, (chips + 1) // 2):
-        fwd = [lax.ppermute(part, "chip", up) for part in fwd]
-        bwd = [lax.ppermute(part, "chip", down) for part in bwd]
-        for base, ahead, behind in zip((0, mid), fwd, bwd):
-            blocks += [(ahead, chips - s, base), (behind, s, base)]
+        fwd = lax.ppermute(fwd, "chip", up)
+        bwd = lax.ppermute(bwd, "chip", down)
+        blocks += [(fwd, chips - s, 0), (bwd, s, 0)]
     if chips % 2 == 0:
-        blocks.append((lax.ppermute(fwd[0], "chip", up), chips // 2, 0))
-        blocks.append((lax.ppermute(bwd[1], "chip", down), chips // 2, mid))
-
+        mid = rows_dev // 2
+        blocks.append((lax.ppermute(fwd[:mid], "chip", up), chips // 2, 0))
+        blocks.append((lax.ppermute(bwd[mid:], "chip", down), chips // 2, mid))
+
+    rel_got, _ = lax.optimization_barrier((rel_got, query_back))
     rel_sent = (rel_keep + rel_got).astype(BF16).reshape(chips, 2 * owned, chips, cols)
     rel_sent = rel_sent.transpose(0, 2, 1, 3).reshape(chips, 2 * owned * chips, cols)
     if rel_sent.shape[1] == rows_dev:
         shared = jnp.where(first, columns(query_back), rel_sent)
-        shared, _ = lax.optimization_barrier((shared, tuple(block for block, _, _ in blocks[1:5])))
+        shared, _ = lax.optimization_barrier((shared, (blocks[1][0], blocks[2][0], z_cols)))
         query_cols = rel_rows = lax.all_to_all(shared, "chip", 0, 0, tiled=True)
     else:
         query_cols = lax.all_to_all(columns(query_back), "chip", 0, 0, tiled=True)

time: 122 us -> 135 us (1.11)
  waiting for transfers between devices: 37.6 us -> 56.6 us
  matrix products: 15.8 us -> 8.47 us
  local copies, waits for them, and re-layouts: 10.4 us -> 12.6 us
  starting transfers between devices: 35.1 us -> 37.2 us
    ppermute x14 -> x8, waiting for transfers between devices: 21.3 us -> 33.2 us  [the longest x3 23.7 us: local(): bwd = lax.ppermute(bwd, 'chip', down)]
    all_to_all x1, waiting for transfers between devices: 0.01 us -> 10.4 us  [local(): z_cols = lax.all_to_all(own_mixed, 'chip', 0, 0, tiled=True)]
    ppermute x1, waiting for transfers between devices: 9.86 us -> 0.01 us  [local(): query_back = lax.ppermute(grad_query, 'hop', [(1, 0)])]
    dot_general x15 -> x9, matrix products: 15.8 us -> 8.47 us  [dot(): lax.dot_general(a, b, (((ca,), (cb,)), ((), ())), preferred_element_type=...]
    ppermute x1, waiting for transfers between devices: 4.67 us -> 10.4 us  [local(): query = lax.ppermute(own_query, 'hop', [(0, 1)])]
    ppermute x14 -> x8, starting transfers between devices: 10.3 us -> 7.12 us  [the longest x3 4.86 us: local(): fwd = lax.ppermute(fwd, 'chip', up)]
    ppermute x1, starting transfers between devices: 2.02 us -> 4.9 us  [local(): z_cols = lax.ppermute(z_cols, 'hop', [(0, 1)])]
    unnamed x17 -> x23, local copies, waits for them, and re-layouts: 9.16 us -> 11.3 us
  transfers between devices with their start and end apart: 22 -> 16, of which waited for: 6 -> 10; matrix products, arithmetic and copies ran while one was open for 16% -> 8% of each run, Pallas kernels for 7% -> 0%
where the time goes in v6:
time: 135 us; the launch traced here: 133 us
  waiting for transfers between devices  56.6 us (42%)
  starting transfers between devices  37.2 us (28%)
  local copies, waits for them, and re-layouts  12.6 us (9%)
  Pallas kernels  11.9 us (9%)
  matrix products  8.47 us (6%)
  other arithmetic  5.81 us (4%)
    ppermute x3, waiting for transfers between devices, local(): bwd = lax.ppermute(bwd, 'chip', down)  23.7 us
    unnamed x23, local copies, waits for them, and re-layouts  11.3 us
    all_to_all x1, waiting for transfers between devices, local(): z_cols = lax.all_to_all(own_mixed, 'chip', 0, 0, tiled=True)  10.4 us
    ppermute x1, waiting for transfers between devices, local(): query = lax.ppermute(own_query, 'hop', [(0, 1)])  10.4 us
    pallas_call x1, Pallas kernels, trail(): pl.pallas_call(trail_body, out_shape=(jax.ShapeDtypeStruct((rows_dev, hid...  8.76 us
    dot_general x9, matrix products, dot(): lax.dot_general(a, b, (((ca,), (cb,)), ((), ())), preferred_element_type=...  8.47 us
    all_to_all x1, starting transfers between devices, local(): query_cols = rel_rows = lax.all_to_all(shared, 'chip', 0, 0, tiled=True)  7.16 us
    ppermute x2, starting transfers between devices, swap_core(): return lax.ppermute(block, 'core', [(0, 1), (1, 0)])  6.63 us
  transfers between devices with their start and end apart: 16, of which 10 were waited for; matrix products, arithmetic and copies ran while one was open for 8% of the time, Pallas kernels for 0%

profile of v6, /device:TPU:9, one launch (start us, length us, event | category | flops | bytes accessed | tf_op | source)
XLA Modules:
  0.0 133.4 jit_solution(5961690868870726287)
XLA Ops:
  0.6 0.7 fusion.8.onehot
  1.4 3.4 %copy-done = bf16[1,2048,2048]{2,1,0:T(8,128)(2,1)S(1)} copy-done((bf16[1,2048,2048]{2,1,0:T(8,128)(2,1)S(1)}, bf16[1,2048,2048]{2,1,0:T(8,128)(2,1)}, u32[]{:S(2)}) %copy-start) | copy-done | bytes 8388632
  4.8 1.0 copy-done.2
  5.8 1.2 copy-done.4
  7.0 3.1 %shard_map.67 = (bf16[2,128,1024]{2,1,0:T(8,128)(2,1)S(1)}, bf16[8,128,256]{2,1,0:T(8,128)(2,1)S(1)}, bf16[2,128,1024]{2,1,0:T(8,128)(2,1)S(1)}) custom-call(bf16[128,2048]{1,0:T(8,128)(2,1)S(1)} %bitcast.71, bf16[2048,2048]{1,0:T(8,128)(2,1)S(1)} %bitcast.69, bf16[128,256]{1,0:T(8,128)(2,1)S(1)} %fusion.8.onehot, bf16[256,2048]{1,0:T(8,128)(2,1)S(1)} %copy-done.4), custom_call_target="tpu_custom_call" | custom-call | flops 1207959552 | bytes 8388608 | tf_op jit(solution)/shard_map/pallas_call | solution.py:58
  10.2 0.8 copy-done.5
  11.0 3.1 %collective-permute-start = (bf16[2,128,1024]{2,1,0:T(8,128)(2,1)S(1)}, bf16[2,128,1024]{2,1,0:T(8,128)(2,1)S(1)}, u32[]{:S(2)}, u32[]{:S(2)}) collective-permute-start(bf16[2,128,1024]{2,1,0:T(8,128)(2,1)S(1)} %get-tuple-element.18), channel_id=1, source_target_pairs={{0,16},{1,17},{2,18},{3,19},{4,20},{5,21},{6,22},{7,23},{8,24},{9,... | collective-permute-start | bytes 1572872 | tf_op jit(solution)/shard_map/ppermute | solution.py:168
  14.3 10.4 %collective-permute-done.query = bf16[2,128,1024]{2,1,0:T(8,128)(2,1)S(1)} collective-permute-done((bf16[2,128,1024]{2,1,0:T(8,128)(2,1)S(1)}, bf16[2,128,1024]{2,1,0:T(8,128)(2,1)S(1)}, u32[]{:S(2)}, u32[]{:S(2)}) %collective-permute-start) | collective-permute-done | bytes 524320 | tf_op jit(solution)/shard_map/ppermute | solution.py:168
  24.6 3.4 %copy-done.1 = bf16[1,2048,2048]{2,1,0:T(8,128)(2,1)S(1)} copy-done((bf16[1,2048,2048]{2,1,0:T(8,128)(2,1)S(1)}, bf16[1,2048,2048]{2,1,0:T(8,128)(2,1)}, u32[]{:S(2)}) %copy-start.1) | copy-done | bytes 8388632
  28.0 8.8 %shard_map.68 = (bf16[128,2048]{1,0:T(8,128)(2,1)S(1)}, bf16[128,2048]{1,0:T(8,128)(2,1)S(1)}, f32[128,2048]{1,0:T(8,128)}, f32[128,2048]{1,0:T(8,128)S(1)}) custom-call(s32[1]{0:T(128)} %bitcast.first, bf16[2,128,1024]{2,1,0:T(8,128)(2,1)S(1)} %collective-permute-done.query, bf16[128,2048]{1,0:T(8,128)(2,1)S(1)} %bitcast.72, ...), custom_call_target="tpu_custom_call" | custom-call | flops 2415919104 | bytes 16777216 | tf_op jit(solution)/shard_map/pallas_call | solution.py:123
  36.8 0.8 copy-done.6
  37.6 1.5 %collective-permute-start.2 = (f32[128,2048]{1,0:T(8,128)}, f32[128,2048]{1,0:T(8,128)S(1)}, u32[]{:S(2)}, u32[]{:S(2)}) collective-permute-start(f32[128,2048]{1,0:T(8,128)} %get-tuple-element.22), channel_id=1, source_target_pairs={{0,1},{1,0},{2,3},{3,2},{4,5},{5,4},{6,7},{7,6},{8,9},{9,8},{10,11... | collective-permute-start | bytes 3145736 | tf_op jit(solution)/shard_map/ppermute | solution.py:20
  39.1 5.7 %all-to-all-start = ((bf16[8,128,256]{2,1,0:T(8,128)(2,1)}), bf16[8,128,256]{2,1,0:T(8,128)(2,1)}, u32[]{:S(2)}, u32[]{:S(2)}) async-start(bf16[8,128,256]{2,1,0:T(8,128)(2,1)} %copy-done.5), calls=%async_computation | async-start | bytes 1048576 | tf_op jit(solution)/shard_map/all_to_all | solution.py:169
  44.8 1.3 collective-permute-start.1
  46.1 10.4 %all-to-all-done = bf16[8,128,256]{2,1,0:T(8,128)(2,1)} async-done(((bf16[8,128,256]{2,1,0:T(8,128)(2,1)}), bf16[8,128,256]{2,1,0:T(8,128)(2,1)}, u32[]{:S(2)}, u32[]{:S(2)}) %all-to-all-start) | async-done | bytes 524320 | tf_op jit(solution)/shard_map/all_to_all | solution.py:169
  56.6 2.0 %collective-permute-start.3 = (bf16[128,2048]{1,0:T(8,128)(2,1)}, bf16[128,2048]{1,0:T(8,128)(2,1)}, u32[]{:S(2)}, u32[]{:S(2)}) collective-permute-start(bf16[128,2048]{1,0:T(8,128)(2,1)} %copy-done.6), channel_id=1, source_target_pairs={{0,4},{4,8},{8,12},{12,14},{14,10},{10,6},{6,2},{2,0},{1,5},{5,9},... | collective-permute-start | bytes 1572872 | tf_op jit(solution)/shard_map/ppermute | solution.py:191
  58.5 0.5 collective-permute-start.4
  59.0 4.9 %collective-permute-start.5 = (bf16[8,128,256]{2,1,0:T(8,128)(2,1)}, bf16[8,128,256]{2,1,0:T(8,128)(2,1)}, u32[]{:S(2)}, u32[]{:S(2)}) collective-permute-start(bf16[8,128,256]{2,1,0:T(8,128)(2,1)} %all-to-all-done), channel_id=1, source_target_pairs={{0,16},{1,17},{2,18},{3,19},{4,20},{5,21},{6,22},{7,23},{8,24},{9,... | collective-permute-start | bytes 1572872 | tf_op jit(solution)/shard_map/ppermute | solution.py:177
  64.3 0.9 fusion.7
  65.2 4.3 %collective-permute-done.3 = bf16[128,2048]{1,0:T(8,128)(2,1)} collective-permute-done((bf16[128,2048]{1,0:T(8,128)(2,1)}, bf16[128,2048]{1,0:T(8,128)(2,1)}, u32[]{:S(2)}, u32[]{:S(2)}) %collective-permute-start.3) | collective-permute-done | bytes 524320 | tf_op jit(solution)/shard_map/ppermute | solution.py:191
  69.5 1.9 %collective-permute-done.4 = bf16[128,2048]{1,0:T(8,128)(2,1)} collective-permute-done((bf16[128,2048]{1,0:T(8,128)(2,1)}, bf16[128,2048]{1,0:T(8,128)(2,1)}, u32[]{:S(2)}, u32[]{:S(2)}) %collective-permute-start.4) | collective-permute-done | bytes 524320 | tf_op jit(solution)/shard_map/ppermute | solution.py:192
  71.5 0.7 collective-permute-done.5
  72.2 7.2 %all-to-all-start.1 = ((bf16[8,128,256]{2,1,0:T(8,128)(2,1)}), bf16[8,128,256]{2,1,0:T(8,128)(2,1)S(1)}, u32[]{:S(2)}, u32[]{:S(2)}) async-start(bf16[8,128,256]{2,1,0:T(8,128)(2,1)} %fusion.7), calls=%async_computation.1 | async-start | bytes 1048576 | tf_op jit(solution)/shard_map/all_to_all | solution.py:205
  79.4 1.4 %collective-permute-start.6 = (bf16[128,2048]{1,0:T(8,128)(2,1)}, bf16[128,2048]{1,0:T(8,128)(2,1)}, u32[]{:S(2)}, u32[]{:S(2)}) collective-permute-start(bf16[128,2048]{1,0:T(8,128)(2,1)} %collective-permute-done.3), channel_id=1, source_target_pairs={{0,4},{4,8},{8,12},{12,14},{14,10},{10,6},{6,2},{2,0},{1,5},{5,9},... | collective-permute-start | bytes 1572872 | tf_op jit(solution)/shard_map/ppermute | solution.py:191
  80.8 21.8 %collective-permute-done.7 = bf16[128,2048]{1,0:T(8,128)(2,1)} collective-permute-done((bf16[128,2048]{1,0:T(8,128)(2,1)}, bf16[128,2048]{1,0:T(8,128)(2,1)}, u32[]{:S(2)}, u32[]{:S(2)}) %collective-permute-start.7) | collective-permute-done | bytes 524320 | tf_op jit(solution)/shard_map/ppermute | solution.py:192
  102.6 1.5 %collective-permute-start.8 = (bf16[128,2048]{1,0:T(8,128)(2,1)}, bf16[128,2048]{1,0:T(8,128)(2,1)S(1)}, u32[]{:S(2)}, u32[]{:S(2)}) collective-permute-start(bf16[128,2048]{1,0:T(8,128)(2,1)} %collective-permute-done.6), channel_id=1, source_target_pairs={{0,4},{4,8},{8,12},{12,14},{14,10},{10,6},{6,2},{2,0},{1,5},{5,9},... | collective-permute-start | bytes 1572872 | tf_op jit(solution)/shard_map/ppermute | solution.py:191
  104.2 1.3 collective-permute-start.10
  105.6 1.6 %fusion.17 = f32[256,2048]{1,0:T(8,128)S(1)} fusion(bf16[128,2048]{1,0:T(8,128)(2,1)} %collective-permute-done.3, bf16[8,128,256]{2,1,0:T(8,128)(2,1)S(1)} %broadcast_select_fusion.1, s32[]{:T(128)S(6)} %select_n.167), kind=kOutput, calls=%fused_computation.30 | convolution fusion | flops 134217728 | bytes 2686980 | tf_op jit(solution)/shard_map/dot_general | solution.py:16
  107.1 1.5 %fusion.15 = f32[256,2048]{1,0:T(8,128)S(1)} fusion(bf16[128,2048]{1,0:T(8,128)(2,1)} %collective-permute-done.4, bf16[8,128,256]{2,1,0:T(8,128)(2,1)S(1)} %broadcast_select_fusion.1, s32[]{:T(128)S(6)} %select_n.169), kind=kOutput, calls=%fused_computation.28 | convolution fusion | flops 134217728 | bytes 2686980 | tf_op jit(solution)/shard_map/dot_general | solution.py:16
  108.6 0.5 fusion.4
  109.1 1.5 %fusion.12 = f32[256,2048]{1,0:T(8,128)S(1)} fusion(bf16[128,2048]{1,0:T(8,128)(2,1)} %collective-permute-done.7, bf16[8,128,256]{2,1,0:T(8,128)(2,1)S(1)} %broadcast_select_fusion.1, s32[]{:T(128)S(6)} %select_n.173), kind=kOutput, calls=%fused_computation.25 | convolution fusion | flops 134217728 | bytes 2686980 | tf_op jit(solution)/shard_map/dot_general | solution.py:16
  110.6 1.5 %fusion.3 = f32[256,2048]{1,0:T(8,128)S(1)} fusion(f32[256,2048]{1,0:T(8,128)S(1)} %fusion.12, f32[256,2048]{1,0:T(8,128)S(1)} %fusion.4, bf16[128,2048]{1,0:T(8,128)(2,1)} %collective-permute-done.6, bf16[8,128,256]{2,1,0:T(8,128)(2,1)S(1)} %broadcast_select_fusion.1, s32[]{:T(128)S(6)} %select_n.171), kind=kOutput, calls=%fused_computation.5 | convolution fusion | flops 135266304 | bytes 6881284 | tf_op jit(solution)/shard_map/dot_general | solution.py:16
  112.2 1.7 %collective-permute-done.8 = bf16[128,2048]{1,0:T(8,128)(2,1)S(1)} collective-permute-done((bf16[128,2048]{1,0:T(8,128)(2,1)}, bf16[128,2048]{1,0:T(8,128)(2,1)S(1)}, u32[]{:S(2)}, u32[]{:S(2)}) %collective-permute-start.8) | collective-permute-done | bytes 524320 | tf_op jit(solution)/shard_map/ppermute | solution.py:191
  113.9 1.2 collective-permute-start.11
  115.1 0.5 collective-permute-start.12
  115.6 0.5 fusion.9
  116.1 0.6 broadcast_select_fusion.2
  116.8 2.5 %collective-permute-done.11 = bf16[64,2048]{1,0:T(8,128)(2,1)S(1)} collective-permute-done((bf16[64,2048]{1,0:T(8,128)(2,1)S(1)}, bf16[64,2048]{1,0:T(8,128)(2,1)S(1)}, u32[]{:S(2)}, u32[]{:S(2)}) %collective-permute-start.11) | collective-permute-done | bytes 262176 | tf_op jit(solution)/shard_map/ppermute | solution.py:196
  119.3 0.4 fusion.29
  119.8 0.9 collective-permute-done.12
  120.7 0.4 fusion.27
  121.1 0.6 copy-done.9
  121.7 0.6 fusion.2
  122.3 1.1 dynamic-slice_bitcast_fusion
  123.4 5.1 %collective-permute-start.13 = (f32[128,2048]{1,0:T(8,128)}, f32[128,2048]{1,0:T(8,128)}, u32[]{:S(2)}, u32[]{:S(2)}) collective-permute-start(f32[128,2048]{1,0:T(8,128)} %dynamic-slice_bitcast_fusion), channel_id=1, source_target_pairs={{0,1},{1,0},{2,3},{3,2},{4,5},{5,4},{6,7},{7,6},{8,9},{9,8},{10,11... | collective-permute-start | bytes 3145736 | tf_op jit(solution)/shard_map/ppermute | solution.py:20
  128.4 0.8 broadcast_select_fusion
  129.3 1.8 %collective-permute-done.13 = f32[128,2048]{1,0:T(8,128)} collective-permute-done((f32[128,2048]{1,0:T(8,128)}, f32[128,2048]{1,0:T(8,128)}, u32[]{:S(2)}, u32[]{:S(2)}) %collective-permute-start.13) | collective-permute-done | bytes 1048608 | tf_op jit(solution)/shard_map/ppermute | solution.py:20
  131.1 2.3 %fusion.6 = f32[1,128,2048]{2,1,0:T(8,128)} fusion(f32[128,2048]{1,0:T(8,128)} %collective-permute-done.13, f32[2,128,2048]{2,1,0:T(8,128)S(1)} %bitcast.74, s32[]{:T(128)S(6)} %select_n.182), kind=kLoop, calls=%fused_computation.10 | loop fusion | flops 524288 | bytes 3145732 | tf_op jit(solution)/shard_map/broadcast_in_dim | solution.py:224
  (36 shorter events, 0.8 us)
Async XLA Ops:
  1.4 3.4 %copy-start = (bf16[1,2048,2048]{2,1,0:T(8,128)(2,1)S(1)}, bf16[1,2048,2048]{2,1,0:T(8,128)(2,1)}, u32[]{:S(2)}) copy-start(bf16[1,2048,2048]{2,1,0:T(8,128)(2,1)} %param.5) | copy-start | bytes 25165828
  4.8 1.0 copy-start.2
  5.8 1.2 copy-start.4
  7.0 7.1 %copy-start.10 = (s32[128]{0:T(128)S(1)}, s32[128]{0:T(128)}, u32[]{:S(2)}) copy-start(s32[128]{0:T(128)} %param.7) | copy-start | bytes 1540
  7.0 17.6 %copy-start.3 = (bf16[1,128,2048]{2,1,0:T(8,128)(2,1)S(1)}, bf16[1,128,2048]{2,1,0:T(8,128)(2,1)}, u32[]{:S(2)}) copy-start(bf16[1,128,2048]{2,1,0:T(8,128)(2,1)} %param.4) | copy-start | bytes 1572868
  10.2 0.8 copy-start.5
  11.0 13.7 %collective-permute-start = (bf16[2,128,1024]{2,1,0:T(8,128)(2,1)S(1)}, bf16[2,128,1024]{2,1,0:T(8,128)(2,1)S(1)}, u32[]{:S(2)}, u32[]{:S(2)}) collective-permute-start(bf16[2,128,1024]{2,1,0:T(8,128)(2,1)S(1)} %get-tuple-element.18), channel_id=1, source_target_pairs={{0,16},{1,17},{2,18},{3,19},{4,20},{5,21},{6,22},{7,23},{8,24},{9,... | collective-permute-start | bytes 1572872 | tf_op jit(solution)/shard_map/ppermute | solution.py:168
  24.6 3.4 %copy-start.1 = (bf16[1,2048,2048]{2,1,0:T(8,128)(2,1)S(1)}, bf16[1,2048,2048]{2,1,0:T(8,128)(2,1)}, u32[]{:S(2)}) copy-start(bf16[1,2048,2048]{2,1,0:T(8,128)(2,1)} %param.5) | copy-start | bytes 25165828
  36.8 0.8 copy-start.6
  37.6 26.3 %collective-permute-start.2 = (f32[128,2048]{1,0:T(8,128)}, f32[128,2048]{1,0:T(8,128)S(1)}, u32[]{:S(2)}, u32[]{:S(2)}) collective-permute-start(f32[128,2048]{1,0:T(8,128)} %get-tuple-element.22), channel_id=1, source_target_pairs={{0,1},{1,0},{2,3},{3,2},{4,5},{5,4},{6,7},{7,6},{8,9},{9,8},{10,11... | collective-permute-start | bytes 3145736 | tf_op jit(solution)/shard_map/ppermute | solution.py:20
  39.1 17.4 %all-to-all-start = ((bf16[8,128,256]{2,1,0:T(8,128)(2,1)}), bf16[8,128,256]{2,1,0:T(8,128)(2,1)}, u32[]{:S(2)}, u32[]{:S(2)}) async-start(bf16[8,128,256]{2,1,0:T(8,128)(2,1)} %copy-done.5), calls=%async_computation | async-start | bytes 1048576 | tf_op jit(solution)/shard_map/all_to_all | solution.py:169
  44.8 19.1 %collective-permute-start.1 = (bf16[128,2048]{1,0:T(8,128)(2,1)S(1)}, bf16[128,2048]{1,0:T(8,128)(2,1)S(1)}, u32[]{:S(2)}, u32[]{:S(2)}) collective-permute-start(bf16[128,2048]{1,0:T(8,128)(2,1)S(1)} %get-tuple-element.20), channel_id=1, source_target_pairs={{16,0},{17,1},{18,2},{19,3},{20,4},{21,5},{22,6},{23,7},{24,8},{25... | collective-permute-start | bytes 1572872 | tf_op jit(solution)/shard_map/ppermute | solution.py:174
  56.6 12.9 %collective-permute-start.3 = (bf16[128,2048]{1,0:T(8,128)(2,1)}, bf16[128,2048]{1,0:T(8,128)(2,1)}, u32[]{:S(2)}, u32[]{:S(2)}) collective-permute-start(bf16[128,2048]{1,0:T(8,128)(2,1)} %copy-done.6), channel_id=1, source_target_pairs={{0,4},{4,8},{8,12},{12,14},{14,10},{10,6},{6,2},{2,0},{1,5},{5,9},... | collective-permute-start | bytes 1572872 | tf_op jit(solution)/shard_map/ppermute | solution.py:191
  58.5 12.9 %collective-permute-start.4 = (bf16[128,2048]{1,0:T(8,128)(2,1)}, bf16[128,2048]{1,0:T(8,128)(2,1)}, u32[]{:S(2)}, u32[]{:S(2)}) collective-permute-start(bf16[128,2048]{1,0:T(8,128)(2,1)} %copy-done.6), channel_id=1, source_target_pairs={{4,0},{8,4},{12,8},{14,12},{10,14},{6,10},{2,6},{0,2},{5,1},{9,5},... | collective-permute-start | bytes 1572872 | tf_op jit(solution)/shard_map/ppermute | solution.py:192
  59.0 13.2 %collective-permute-start.5 = (bf16[8,128,256]{2,1,0:T(8,128)(2,1)}, bf16[8,128,256]{2,1,0:T(8,128)(2,1)}, u32[]{:S(2)}, u32[]{:S(2)}) collective-permute-start(bf16[8,128,256]{2,1,0:T(8,128)(2,1)} %all-to-all-done), channel_id=1, source_target_pairs={{0,16},{1,17},{2,18},{3,19},{4,20},{5,21},{6,22},{7,23},{8,24},{9,... | collective-permute-start | bytes 1572872 | tf_op jit(solution)/shard_map/ppermute | solution.py:177
  72.2 31.9 %all-to-all-start.1 = ((bf16[8,128,256]{2,1,0:T(8,128)(2,1)}), bf16[8,128,256]{2,1,0:T(8,128)(2,1)S(1)}, u32[]{:S(2)}, u32[]{:S(2)}) async-start(bf16[8,128,256]{2,1,0:T(8,128)(2,1)} %fusion.7), calls=%async_computation.1 | async-start | bytes 1048576 | tf_op jit(solution)/shard_map/all_to_all | solution.py:205
  79.3 23.3 %collective-permute-start.7 = (bf16[128,2048]{1,0:T(8,128)(2,1)}, bf16[128,2048]{1,0:T(8,128)(2,1)}, u32[]{:S(2)}, u32[]{:S(2)}) collective-permute-start(bf16[128,2048]{1,0:T(8,128)(2,1)} %collective-permute-done.4), channel_id=1, source_target_pairs={{4,0},{8,4},{12,8},{14,12},{10,14},{6,10},{2,6},{0,2},{5,1},{9,5},... | collective-permute-start | bytes 1572872 | tf_op jit(solution)/shard_map/ppermute | solution.py:192
  79.4 23.2 %collective-permute-start.6 = (bf16[128,2048]{1,0:T(8,128)(2,1)}, bf16[128,2048]{1,0:T(8,128)(2,1)}, u32[]{:S(2)}, u32[]{:S(2)}) collective-permute-start(bf16[128,2048]{1,0:T(8,128)(2,1)} %collective-permute-done.3), channel_id=1, source_target_pairs={{0,4},{4,8},{8,12},{12,14},{14,10},{10,6},{6,2},{2,0},{1,5},{5,9},... | collective-permute-start | bytes 1572872 | tf_op jit(solution)/shard_map/ppermute | solution.py:191
  102.6 12.5 %collective-permute-start.9 = (bf16[128,2048]{1,0:T(8,128)(2,1)}, bf16[128,2048]{1,0:T(8,128)(2,1)S(1)}, u32[]{:S(2)}, u32[]{:S(2)}) collective-permute-start(bf16[128,2048]{1,0:T(8,128)(2,1)} %collective-permute-done.7), channel_id=1, source_target_pairs={{4,0},{8,4},{12,8},{14,12},{10,14},{6,10},{2,6},{0,2},{5,1},{9,5},... | collective-permute-start | bytes 1572872 | tf_op jit(solution)/shard_map/ppermute | solution.py:192
  102.6 11.2 %collective-permute-start.8 = (bf16[128,2048]{1,0:T(8,128)(2,1)}, bf16[128,2048]{1,0:T(8,128)(2,1)S(1)}, u32[]{:S(2)}, u32[]{:S(2)}) collective-permute-start(bf16[128,2048]{1,0:T(8,128)(2,1)} %collective-permute-done.6), channel_id=1, source_target_pairs={{0,4},{4,8},{8,12},{12,14},{14,10},{10,6},{6,2},{2,0},{1,5},{5,9},... | collective-permute-start | bytes 1572872 | tf_op jit(solution)/shard_map/ppermute | solution.py:191
  104.2 11.9 %collective-permute-start.10 = (f32[8,2048]{1,0:T(8,128)S(1)}, f32[8,2048]{1,0:T(8,128)S(1)}, u32[]{:S(2)}, u32[]{:S(2)}) collective-permute-start(f32[8,2048]{1,0:T(8,128)S(1)} %bitcast.80), channel_id=1, source_target_pairs={{16,0},{17,1},{18,2},{19,3},{20,4},{21,5},{22,6},{23,7},{24,8},{25... | collective-permute-start | bytes 196616 | tf_op jit(solution)/shard_map/ppermute | solution.py:211
  105.6 3.1 %copy-start.7 = (bf16[128,2048]{1,0:T(8,128)(2,1)S(1)}, bf16[128,2048]{1,0:T(8,128)(2,1)}, u32[]{:S(2)}) copy-start(bf16[128,2048]{1,0:T(8,128)(2,1)} %copy-done.6) | copy-start | bytes 1572868
  113.8 5.9 %copy-start.8 = (bf16[128,2048]{1,0:T(8,128)(2,1)}, bf16[128,2048]{1,0:T(8,128)(2,1)S(1)}, u32[]{:S(2)}) copy-start(bf16[128,2048]{1,0:T(8,128)(2,1)S(1)} %collective-permute-done.8) | copy-start | bytes 1572868
  113.9 5.4 %collective-permute-start.11 = (bf16[64,2048]{1,0:T(8,128)(2,1)S(1)}, bf16[64,2048]{1,0:T(8,128)(2,1)S(1)}, u32[]{:S(2)}, u32[]{:S(2)}) collective-permute-start(bf16[64,2048]{1,0:T(8,128)(2,1)S(1)} %slice.28), channel_id=1, source_target_pairs={{0,4},{4,8},{8,12},{12,14},{14,10},{10,6},{6,2},{2,0},{1,5},{5,9},... | collective-permute-start | bytes 786440 | tf_op jit(solution)/shard_map/ppermute | solution.py:196
  115.1 5.6 %collective-permute-start.12 = (bf16[64,2048]{1,0:T(8,128)(2,1)S(1)}, bf16[64,2048]{1,0:T(8,128)(2,1)S(1)}, u32[]{:S(2)}, u32[]{:S(2)}) collective-permute-start(bf16[64,2048]{1,0:T(8,128)(2,1)S(1)} %slice.29), channel_id=1, source_target_pairs={{4,0},{8,4},{12,8},{14,12},{10,14},{6,10},{2,6},{0,2},{5,1},{9,5},... | collective-permute-start | bytes 786440 | tf_op jit(solution)/shard_map/ppermute | solution.py:197
  120.7 1.0 copy-start.9
  123.4 7.7 %collective-permute-start.13 = (f32[128,2048]{1,0:T(8,128)}, f32[128,2048]{1,0:T(8,128)}, u32[]{:S(2)}, u32[]{:S(2)}) collective-permute-start(f32[128,2048]{1,0:T(8,128)} %dynamic-slice_bitcast_fusion), channel_id=1, source_target_pairs={{0,1},{1,0},{2,3},{3,2},{4,5},{5,4},{6,7},{7,6},{8,9},{9,8},{10,11... | collective-permute-start | bytes 3145736 | tf_op jit(solution)/shard_map/ppermute | solution.py:20
